TPU v7x, 1024 devices: a whole 4x8x16 slice. The times are simulated.
1024 devices in a mesh: dp: 16 (over z), sp: 32 (over y, x), tp: 2 (over core).
Axes of the slice: x: 4, y: 8, z: 16, core: 2. Of those that a mesh axis runs over, the one named last changes fastest.
Arguments:
- qkv: bfloat16 [16, 64, 128, 1920], P('dp', None, ('sp', 'tp')), may hold values from -8 to 8
- out_grad: bfloat16 [16, 64, 128, 1280], P('dp', None, ('sp', 'tp')), may hold values from -16 to 16
- block_image: int32 [16, 64], P('dp'), may hold values from 0 to 47, never falling along the last dimension, each value on 1 to 2 neighbouring positions
- proj_weight: bfloat16 [640, 1280], replicated, may hold values from -0.25 to 0.25
- proj_bias: bfloat16 [1280], replicated, may hold values from -3 to 3
Outputs:
- branch_out: bfloat16 [16, 64, 128, 1280], P('dp', None, ('sp', 'tp'))
- qkv_grad: bfloat16 [16, 64, 128, 1920], P('dp', None, ('sp', 'tp'))
- weight_grad: float32 [640, 1280], P(None, ('sp', 'tp'))
- bias_grad: float32 [1280], P(('sp', 'tp'))
Inputs may be any that keep to these rules, and one draw needn't show every extreme that they name: `block_image`: within a sample, ids never fall; every image covers 1 to 2 consecutive blocks and one covers exactly 2.
All inputs are finite; a program needn't handle non-finite values.
Results may differ from a plain program's by a relative error of at most 0.02.
Values may be sent and summed in bfloat16 or wider, within the bound.
No kernel may reach another device: no remote copies, remote signals or barrier semaphores. Data moves between devices by JAX's collectives and lax.ppermute only.
A program may use at most 128 MiB of HBM per device.

v0:
```python
import jax
import jax.numpy as jnp
from jax import lax
from jax.sharding import PartitionSpec as P

HD = 80
IMGB = 2


masked_score = -1e30


def body(qkv, out_grad, block_image, proj_weight, proj_bias):
    sp_count = lax.axis_size("sp")
    tp_count = lax.axis_size("tp")
    blocks = qkv.shape[1]
    shard_rows = qkv.shape[2]
    head_cols = proj_weight.shape[0]
    model_dim = proj_weight.shape[1]
    group_cols = head_cols // tp_count
    local_heads = group_cols // HD
    per_device = blocks // sp_count
    capacity = per_device + IMGB - 1
    block_len = shard_rows * sp_count * tp_count
    total_len = capacity * block_len
    payload = 4 * group_cols
    score_scale = HD ** (-0.5)
    images = block_image[0]
    block_index = jnp.arange(blocks, dtype=jnp.int32)
    starts = jnp.concatenate([jnp.ones((1,), jnp.bool_), images[1:] != images[:-1]])
    first_block = lax.cummax(jnp.where(starts, block_index, 0), axis=0)
    target = first_block // per_device
    earlier = (target[None, :] == target[:, None]) & (block_index[None, :] < block_index[:, None])
    slot_index = jnp.sum(earlier.astype(jnp.int32), axis=1)
    slot_range = jnp.arange(capacity, dtype=jnp.int32)
    device_range = jnp.arange(sp_count, dtype=jnp.int32)
    placement = (
        (slot_index[None, None, :] == slot_range[:, None, None])
        & (target[None, None, :] == device_range[None, :, None])
    ).astype(jnp.bfloat16)
    own_sp = lax.axis_index("sp")
    own_hits = (slot_index[None, :] == slot_range[:, None]) & (target[None, :] == own_sp)
    slot_image = jnp.sum(jnp.where(own_hits, images[None, :], 0), axis=1)
    slot_used = jnp.any(own_hits, axis=1)
    slot_ids = jnp.where(slot_used, slot_image, -1 - slot_range)
    grad_rows = out_grad[0].reshape(blocks * shard_rows, model_dim)
    out_delta = lax.dot_general(
        grad_rows, proj_weight, (((1,), (1,)), ((), ())), preferred_element_type=jnp.float32
    ).astype(jnp.bfloat16)
    pieces = jnp.concatenate(
        [
            qkv[0].reshape(blocks, shard_rows, 3, tp_count, group_cols),
            out_delta.reshape(blocks, shard_rows, 1, tp_count, group_cols),
        ],
        axis=2,
    )
    outgoing = jnp.einsum(
        "cdb,brkgf->cdgrkf", placement, pieces, preferred_element_type=jnp.float32
    ).astype(jnp.bfloat16)
    arrived = lax.all_to_all(
        outgoing.reshape(capacity, sp_count * tp_count, shard_rows, payload),
        ("sp", "tp"),
        split_axis=1,
        concat_axis=1,
        tiled=True,
    )
    arrived = arrived.reshape(capacity, block_len, 4, local_heads, HD)
    key_all = arrived[:, :, 1].reshape(total_len, local_heads, HD)
    value_all = arrived[:, :, 2].reshape(total_len, local_heads, HD)
    key_ids = jnp.repeat(slot_ids, block_len)
    row_ids = jnp.broadcast_to(slot_ids[:, None], (capacity, block_len))

    def attend_slot(running, inputs):
        key_grad, value_grad = running
        query_rows, delta_rows, query_ids = inputs
        scores = (
            jnp.einsum("ihd,jhd->hij", query_rows, key_all, preferred_element_type=jnp.float32)
            * score_scale
        )
        scores = jnp.where((query_ids[:, None] == key_ids[None, :])[None], scores, masked_score)
        exp_scores = jnp.exp(scores - jnp.max(scores, axis=-1, keepdims=True))
        probs_f = exp_scores / jnp.sum(exp_scores, axis=-1, keepdims=True)
        probs_bf = probs_f.astype(jnp.bfloat16)
        attended = jnp.einsum(
            "hij,jhd->ihd", probs_bf, value_all, preferred_element_type=jnp.float32
        ).astype(jnp.bfloat16)
        prob_grad = jnp.einsum(
            "ihd,jhd->hij", delta_rows, value_all, preferred_element_type=jnp.float32
        )
        centre = jnp.sum(probs_f * prob_grad, axis=-1, keepdims=True)
        score_grad = (probs_f * (prob_grad - centre) * score_scale).astype(jnp.bfloat16)
        query_grad = jnp.einsum(
            "hij,jhd->ihd", score_grad, key_all, preferred_element_type=jnp.float32
        ).astype(jnp.bfloat16)
        key_grad = key_grad + jnp.einsum(
            "hij,ihd->jhd", score_grad, query_rows, preferred_element_type=jnp.float32
        )
        value_grad = value_grad + jnp.einsum(
            "hij,ihd->jhd", probs_bf, delta_rows, preferred_element_type=jnp.float32
        )
        return ((key_grad, value_grad), (attended, query_grad))

    empty_grad = jnp.zeros((total_len, local_heads, HD), jnp.float32)
    (key_grad, value_grad), (attended_slots, query_slots) = lax.scan(
        attend_slot, (empty_grad, empty_grad), (arrived[:, :, 0], arrived[:, :, 3], row_ids)
    )
    returning = jnp.stack(
        [
            attended_slots,
            query_slots,
            key_grad.astype(jnp.bfloat16).reshape(capacity, block_len, local_heads, HD),
            value_grad.astype(jnp.bfloat16).reshape(capacity, block_len, local_heads, HD),
        ],
        axis=2,
    )
    returned = lax.all_to_all(
        returning.reshape(capacity, sp_count * tp_count, shard_rows, payload),
        ("sp", "tp"),
        split_axis=1,
        concat_axis=1,
        tiled=True,
    )
    returned = returned.reshape(capacity, sp_count, tp_count, shard_rows, 4, group_cols)
    collected = jnp.einsum(
        "cdb,cdgrkf->brkgf", placement, returned, preferred_element_type=jnp.float32
    ).astype(jnp.bfloat16)
    attended_rows = collected[:, :, 0].reshape(blocks * shard_rows, head_cols)
    qkv_grad = collected[:, :, 1:].reshape(1, blocks, shard_rows, 3 * head_cols)
    branch = jnp.dot(
        attended_rows, proj_weight, preferred_element_type=jnp.float32
    ) + proj_bias.astype(jnp.float32)
    branch = branch.astype(jnp.bfloat16).reshape(1, blocks, shard_rows, model_dim)
    weight_part = lax.dot_general(
        attended_rows, grad_rows, (((0,), (0,)), ((), ())), preferred_element_type=jnp.float32
    )
    bias_part = jnp.sum(grad_rows, axis=0, dtype=jnp.float32)[None, :]
    weight_share, bias_share = (
        lax.psum_scatter(weight_part, ("sp", "tp"), scatter_dimension=1, tiled=True),
        lax.psum_scatter(bias_part, ("sp", "tp"), scatter_dimension=1, tiled=True),
    )
    weight_total, bias_total = (
        lax.psum(weight_share.astype(jnp.bfloat16), "dp").astype(jnp.float32),
        lax.psum(bias_share.astype(jnp.bfloat16), "dp").astype(jnp.float32),
    )
    grad_scale = (lax.axis_size("dp") * blocks * block_len) ** (-0.5)
    return (branch, qkv_grad, weight_total * grad_scale, bias_total[0] * grad_scale)


def solution(mesh):
    in_specs = (
        P("dp", None, ("sp", "tp"), None),
        P("dp", None, ("sp", "tp"), None),
        P("dp", None),
        P(),
        P(),
    )
    out_specs = (
        P("dp", None, ("sp", "tp"), None),
        P("dp", None, ("sp", "tp"), None),
        P(None, ("sp", "tp")),
        P(("sp", "tp")),
    )
    return jax.shard_map(body, mesh=mesh, in_specs=in_specs, out_specs=out_specs, check_vma=False)
```

profile of v0, /device:TPU:32, one launch (start us, length us, event | category | flops | bytes accessed | tf_op | source)
XLA Modules:
  0.0 521.3 jit_solution(13069034671279760903)
XLA Ops:
  6.5 2.3 reshape.276
  8.8 17.1 %all-to-all-start = ((bf16[3,64,2,1280]{3,2,0,1:T(2,128)(2,1)}), bf16[3,64,2,1280]{3,2,0,1:T(2,128)(2,1)S(1)}, u32[]{:S(2)}, u32[]{:S(2)}) async-start(bf16[3,64,2,1280]{3,2,0,1:T(2,128)(2,1)} %reshape.276), calls=%async_computation | async-start | bytes 1966080 | tf_op jit(solution)/shard_map/all_to_all | solution.py:60
  26.0 23.9 %all-to-all-done = bf16[3,64,2,1280]{3,2,0,1:T(2,128)(2,1)S(1)} async-done(((bf16[3,64,2,1280]{3,2,0,1:T(2,128)(2,1)}), bf16[3,64,2,1280]{3,2,0,1:T(2,128)(2,1)S(1)}, u32[]{:S(2)}, u32[]{:S(2)}) %all-to-all-start) | async-done | bytes 983072 | tf_op jit(solution)/shard_map/all_to_all | solution.py:60
  49.9 1.6 copy.56
  51.6 5.3 %reshape.267 = bf16[3,128,4,4,80]{4,3,2,1,0:T(4,128)(2,1)S(1)} reshape(bf16[3,64,2,1280]{3,2,1,0:T(2,128)(2,1)} %copy.56) | data formatting | bytes 1966080 | tf_op jit(solution)/shard_map/reshape | solution.py:67
  59.7 1.9 copy.76
  63.2 50.5 %while.18 = (s32[]{:T(128)}, f32[384,4,80]{0,2,1:T(8,128)}, f32[384,4,80]{0,2,1:T(8,128)}, bf16[3,128,4,80]{1,3,2,0:T(8,128)(2,1)}, bf16[3,128,4,80]{1,3,2,0:T(8...) while((s32[]{:T(128)}, f32[384,4,80]{0,2,1:T(8,128)}, ...), condition=%wide.region_8.9_spmd.clone, body=%wide.region_4.8_spmd.clone.sunk | while | flops 257789824 | bytes 12177051 | solution.py:104
  63.6 2.2 fusion.133
  65.9 4.7 fusion.134
  70.6 2.4 fusion.135
  73.0 2.3 fusion.136
  75.2 4.5 fusion.137
  80.2 2.2 fusion.133
  82.5 4.9 fusion.134
  87.4 2.6 fusion.135
  89.9 2.3 fusion.136
  92.2 4.5 fusion.137
  97.2 2.2 fusion.133
  99.4 4.9 fusion.134
  104.3 2.6 fusion.135
  106.9 2.3 fusion.136
  109.2 4.5 fusion.137
  116.5 2.3 pad_maximum_fusion
  118.8 3.2 copy.63
  122.0 3.3 reshape.268
  125.3 2.9 copy.64
  128.2 9.4 %all-to-all-start.1 = ((bf16[3,64,2,1280]{3,2,0,1:T(2,128)(2,1)}), bf16[3,64,2,1280]{3,2,0,1:T(2,128)(2,1)}, u32[]{:S(2)}, u32[]{:S(2)}) async-start(bf16[3,64,2,1280]{3,2,0,1:T(2,128)(2,1)} %copy.64), calls=%async_computation.1 | async-start | bytes 1966080 | tf_op jit(solution)/shard_map/all_to_all | solution.py:116
  139.9 21.8 %all-to-all-done.1 = bf16[3,64,2,1280]{3,2,0,1:T(2,128)(2,1)} async-done(((bf16[3,64,2,1280]{3,2,0,1:T(2,128)(2,1)}), bf16[3,64,2,1280]{3,2,0,1:T(2,128)(2,1)}, u32[]{:S(2)}, u32[]{:S(2)}) %all-to-all-start.1) | async-done | bytes 983072 | tf_op jit(solution)/shard_map/all_to_all | solution.py:116
  161.7 3.8 reshape.277
  166.4 2.3 fusion.79
  172.2 285.0 %all-reduce.5 = (bf16[640,1280]{0,1:T(8,128)(2,1)}, bf16[1,1280]{1,0:T(2,128)(2,1)S(1)}) all-reduce(f32[640,1280]{0,1:T(8,128)} %fusion.79, f32[1,1280]{1,0:T(1,128)S(1)} %broadcast_in_dim.77), channel_id=2, replica_groups=mesh['dp'=16,'sp'=32,'tp'=2] {'sp','tp'}, use_global_device_ids=true, to_apply=%region_9.10.clone | all-reduce | flops 820480 | bytes 4922880
  458.0 62.1 %all-reduce.3 = (bf16[640,20]{0,1:T(8,128)(2,1)S(1)}, bf16[1,20]{1,0:T(2,128)(2,1)S(1)}) all-reduce(bf16[640,20]{0,1:T(8,128)(2,1)S(1)} %dynamic-slice_convert_fusion, bf16[1,20]{1,0:T(2,128)(2,1)S(1)} %fusion.73), channel_id=1, replica_groups=mesh['dp'=16,'sp'=32,'tp'=2] {'dp'}, use_global_device_ids=true, to_apply=%region_10.11 | all-reduce | flops 12820 | bytes 51280 | tf_op jit(solution)/shard_map/psum | solution.py:142
  (73 shorter events, 22.1 us)
Async XLA Ops:
  0.6 2.6 copy-start
  3.2 1.0 copy-start.3
  6.5 19.4 %copy-start.6 = (s32[1,64]{1,0:T(1,128)S(1)}, s32[1,64]{1,0:T(1,128)}, u32[]{:S(2)}) copy-start(s32[1,64]{1,0:T(1,128)} %param.9) | copy-start | bytes 772
  8.8 41.1 %all-to-all-start = ((bf16[3,64,2,1280]{3,2,0,1:T(2,128)(2,1)}), bf16[3,64,2,1280]{3,2,0,1:T(2,128)(2,1)S(1)}, u32[]{:S(2)}, u32[]{:S(2)}) async-start(bf16[3,64,2,1280]{3,2,0,1:T(2,128)(2,1)} %reshape.276), calls=%async_computation | async-start | bytes 1966080 | tf_op jit(solution)/shard_map/all_to_all | solution.py:60
  58.5 4.3 copy-start.1
  113.7 1.2 copy-start.4
  125.3 12.3 %copy-start.5 = (bf16[1280]{0:T(1024)(128)(2,1)S(1)}, bf16[1280]{0:T(1024)(128)(2,1)}, u32[]{:S(2)}) copy-start(bf16[1280]{0:T(1024)(128)(2,1)} %param.11) | copy-start | bytes 7684
  125.3 12.3 %copy-start.2 = (bf16[1,64,2,1280]{3,2,1,0:T(2,128)(2,1)S(1)}, bf16[1,64,2,1280]{3,2,1,0:T(2,128)(2,1)}, u32[]{:S(2)}) copy-start(bf16[1,64,2,1280]{3,2,1,0:T(2,128)(2,1)} %param.8) | copy-start | bytes 983044
  128.2 33.6 %all-to-all-start.1 = ((bf16[3,64,2,1280]{3,2,0,1:T(2,128)(2,1)}), bf16[3,64,2,1280]{3,2,0,1:T(2,128)(2,1)}, u32[]{:S(2)}, u32[]{:S(2)}) async-start(bf16[3,64,2,1280]{3,2,0,1:T(2,128)(2,1)} %copy.64), calls=%async_computation.1 | async-start | bytes 1966080 | tf_op jit(solution)/shard_map/all_to_all | solution.py:116
where the time goes:
time: 523 us; the launch traced here: 521 us
  blocking collectives  347 us (66%)
  matrix products  54.4 us (10%)
  waiting for transfers between devices  45.7 us (9%)
  local copies, waits for them, and re-layouts  39.1 us (7%)
  starting transfers between devices  26.5 us (5%)
  other arithmetic  6.75 us (1%)
    unnamed x1, blocking collectives  285 us
    psum x1, blocking collectives, body(): lax.psum(weight_share.astype(jnp.bfloat16), 'dp').astype(jnp.float32)  62.1 us
    all_to_all x1, waiting for transfers between devices, body(): lax.all_to_all(outgoing.reshape(capacity, sp_count * tp_count, shard_rows...  23.9 us
    all_to_all x1, waiting for transfers between devices, body(): lax.all_to_all(returning.reshape(capacity, sp_count * tp_count, shard_row...  21.8 us
    all_to_all x1, starting transfers between devices, body(): lax.all_to_all(outgoing.reshape(capacity, sp_count * tp_count, shard_rows...  17.1 us
    dot_general x3, matrix products, attend_slot(): jnp.einsum('hij,ihd->jhd', score_grad, query_rows, preferred_element_type...  14.5 us
    dot_general x3, matrix products, attend_slot(): jnp.einsum('hij,jhd->ihd', score_grad, key_all, preferred_element_type=jn...  13.6 us
  transfers between devices with their start and end apart: 2, of which 2 were waited for; matrix products, arithmetic and copies ran while one was open for 0% of the time, Pallas kernels for 0%

commit v1 on v0

v1 whole, which is shorter than its diff:
```python
import jax
import jax.numpy as jnp
import numpy as np
from jax import lax
from jax.experimental import pallas as pl
from jax.experimental.pallas import tpu as pltpu
from jax.sharding import PartitionSpec as P

HD = 80
BF = jnp.bfloat16
F32 = jnp.float32
masked_score = -1e30

VM = pl.BlockSpec(memory_space=pltpu.VMEM)
SM = pl.BlockSpec(memory_space=pltpu.SMEM)
PARAMS = pltpu.CompilerParams(vmem_limit_bytes=48 * 1024 * 1024)


def dot(a, b, ca=1, cb=0):
    return lax.dot_general(a, b, (((ca,), (cb,)), ((), ())), preferred_element_type=F32)


def call(kernel, outs, specs, *args):
    return pl.pallas_call(
        kernel,
        out_shape=outs,
        in_specs=specs,
        out_specs=jax.tree.map(lambda _: VM, outs),
        compiler_params=PARAMS,
    )(*args)


def arr(shape, dtype):
    return jax.ShapeDtypeStruct(shape, dtype)


def rows_at(row_of, count):
    n = row_of.shape[1]
    return jnp.where(lax.broadcasted_iota(jnp.int32, (count, n), 0) == row_of, 1.0, 0.0).astype(BF)


def slot_rows(shape, dim):
    i = lax.broadcasted_iota(jnp.int32, shape, dim)
    return ((i >> 2) & 3) * 256 + ((i >> 1) & 1) * 128 + (i >> 4) * 2 + (i & 1)


def send_kernel(qkv_ref, grad_ref, weight_ref, dst_ref, pick_ref, out_ref):
    grad = grad_ref[...]
    delta = dot(grad, weight_ref[...], 1, 1).astype(BF)
    pick = rows_at(pick_ref[...], 640)
    low = dot(grad[:, :640], pick).astype(BF)
    high = dot(grad[:, 640:], pick).astype(BF)
    blocks = []
    for t in range(2):
        picked = jnp.concatenate([low[:, t * 384:(t + 1) * 384], high[:, t * 384:(t + 1) * 384]], axis=1)
        for g in range(4):
            if g < 3:
                at = g * 640 + t * 320
                kind = qkv_ref[:, at:at + 320]
            else:
                kind = delta[:, t * 320:(t + 1) * 320]
            blocks.append(jnp.concatenate([kind, picked[:, g * 192:(g + 1) * 192]], axis=1))
    stack = jnp.concatenate(blocks, axis=0)
    out_ref[...] = dot(rows_at(dst_ref[...], 1024), stack).astype(BF)


def head_masks(rows):
    lane = lax.broadcasted_iota(jnp.int32, (rows, 320), 1)
    return [(lane >= h * HD) & (lane < (h + 1) * HD) for h in range(4)]


def by_head(x, masks):
    zero = jnp.zeros_like(x)
    return jnp.concatenate([jnp.where(m, x, zero) for m in masks], axis=0)


def own_head(x, masks):
    total = jnp.zeros((256, 320), F32)
    for h, m in enumerate(masks):
        total = jnp.where(m, x[h * 256:(h + 1) * 256], total)
    return total


def attend_kernel(double_ref, got_ref, att_ref, probs_ref, sorted_ref):
    sel = rows_at(slot_rows((1, 1024), 1), 1024)
    rows = dot(sel, got_ref[...]).astype(BF)
    sorted_ref[...] = rows
    query, key, value = rows[:256, :320], rows[256:512, :320], rows[512:768, :320]
    masks = head_masks(256)
    scores = dot(by_head(query, masks), key, 1, 1) * (HD ** -0.5)
    row = lax.broadcasted_iota(jnp.int32, (1024, 256), 0)
    col = lax.broadcasted_iota(jnp.int32, (1024, 256), 1)
    apart = (((row ^ col) >> 7) & 1) > double_ref[0]
    scores = jnp.where(apart, masked_score, scores)
    exp_scores = jnp.exp(scores - jnp.max(scores, axis=-1, keepdims=True))
    probs = exp_scores / jnp.sum(exp_scores, axis=-1, keepdims=True)
    probs_ref[...] = probs
    att_ref[...] = own_head(dot(probs.astype(BF), value), masks).astype(BF)


def back_kernel(sorted_ref, probs_ref, att_ref, out_ref):
    rows = sorted_ref[...]
    query, key = rows[:256, :320], rows[256:512, :320]
    value, delta = rows[512:768, :320], rows[768:, :320]
    masks = head_masks(256)
    query_heads, delta_heads = by_head(query, masks), by_head(delta, masks)
    probs = probs_ref[...]
    prob_grad = dot(delta_heads, value, 1, 1)
    centre = jnp.sum(probs * prob_grad, axis=-1, keepdims=True)
    score_grad = (probs * (prob_grad - centre) * (HD ** -0.5)).astype(BF)
    query_grad = own_head(dot(score_grad, key), masks).astype(BF)
    key_grad = dot(score_grad, query_heads, 0, 0).astype(BF)
    value_grad = dot(probs.astype(BF), delta_heads, 0, 0).astype(BF)
    stack = jnp.concatenate([att_ref[...], query_grad, key_grad, value_grad], axis=0)
    lane = lax.broadcasted_iota(jnp.int32, (1024, 1024), 1)
    back = jnp.where(lane == slot_rows((1024, 1), 0), 1.0, 0.0).astype(BF)
    out_ref[...] = dot(back, stack).astype(BF)


def weight_kernel(core_ref, sorted_ref, own_ref, other_ref, out_ref):
    rows = sorted_ref[...]
    grad = jnp.concatenate([rows[g * 256:(g + 1) * 256, 320:] for g in range(4)], axis=1)
    first = core_ref[0] == 0
    own, other = own_ref[...], other_ref[...]
    att = jnp.concatenate([jnp.where(first, own, other), jnp.where(first, other, own)], axis=1)
    part = dot(grad, att, 0, 0)
    sums = dot(jnp.ones((8, 256), BF), grad)[:1]
    row = lax.broadcasted_iota(jnp.int32, (768, 768), 0)
    col = lax.broadcasted_iota(jnp.int32, (768, 768), 1)
    start = row - 20
    own_sums = jnp.where((col >= start) & (col < row), sums, 0.0).astype(BF)
    in_chunk = lax.broadcasted_iota(jnp.int32, (768, 1), 0)
    in_chunk = in_chunk - (in_chunk * 2731 >> 16) * 24
    lane = lax.broadcasted_iota(jnp.int32, (768, 640), 1)
    spread = jnp.where(lane == in_chunk, 1.0, 0.0).astype(BF)
    bias = dot(own_sums, spread)
    out_ref[...] = jnp.where(in_chunk == 20, bias, part).astype(BF)


def home_kernel(got_ref, dst_ref, weight_ref, bias_ref, branch_ref, grad_ref):
    rows = dot(rows_at(dst_ref[...], 1024), got_ref[...], 0, 0).astype(BF)
    att = jnp.concatenate([rows[:128], rows[512:640]], axis=1)
    branch_ref[...] = (dot(att, weight_ref[...]) + bias_ref[...].astype(F32)).astype(BF)
    grad_ref[...] = jnp.concatenate(
        [rows[(t * 4 + g) * 128:(t * 4 + g + 1) * 128] for g in range(1, 4) for t in range(2)], axis=1
    )


def picked_columns():
    col = np.arange(768)
    t, sp, j = col // 384, (col % 384) // 24, col % 24
    return np.where(j < 20, sp * 40 + t * 20 + j, -1).astype(np.int32)[None]


def body(qkv, out_grad, block_image, proj_weight, proj_bias):
    own_sp, own_tp = lax.axis_index("sp"), lax.axis_index("tp")
    dp_count = lax.axis_size("dp")
    images = block_image[0]
    index = jnp.arange(64, dtype=jnp.int32)
    alike = (images[:, None] == images[None, :]) & (index[:, None] != index[None, :])
    twin = jnp.any(alike, axis=1)
    twin_row = jnp.any(alike, axis=0)
    before = index[None, :] < index[:, None]
    rank = jnp.sum((before & (twin_row[None, :] == twin[:, None])).astype(jnp.int32), axis=1)
    twins = jnp.sum(twin.astype(jnp.int32))
    place = jnp.where(twin, rank, twins + rank)
    is_double = (2 * own_sp < twins).astype(jnp.int32)[None]
    four = jnp.arange(4, dtype=jnp.int32)
    two = jnp.arange(2, dtype=jnp.int32)
    dst = (
        ((place >> 1) * 32 + (place & 1) * 2)[None, None, :, None]
        + two[:, None, None, None] * 16
        + four[None, :, None, None] * 4
        + two[None, None, None, :]
    ).reshape(1, 1024)
    qkv_rows = qkv.reshape(128, 1920)
    grad_rows = out_grad.reshape(128, 1280)
    outgoing = call(
        send_kernel, arr((1024, 512), BF), [VM] * 5,
        qkv_rows, grad_rows, proj_weight, dst, jnp.asarray(picked_columns()),
    )
    arrived = lax.all_to_all(
        outgoing.reshape(64, 16, 512), ("sp", "tp"), split_axis=0, concat_axis=0, tiled=True
    ).reshape(1024, 512)
    attended, probs, ordered = call(
        attend_kernel, (arr((256, 320), BF), arr((1024, 256), F32), arr((1024, 512), BF)), [SM, VM],
        is_double, arrived,
    )
    other = lax.ppermute(attended, "tp", [(0, 1), (1, 0)])
    returning = call(back_kernel, arr((1024, 320), BF), [VM] * 3, ordered, probs, attended)
    core = own_tp.astype(jnp.int32)[None]
    part = call(weight_kernel, arr((768, 640), BF), [SM, VM, VM, VM], core, ordered, attended, other)
    shares = lax.all_to_all(part.reshape(32, 24, 640), "sp", split_axis=0, concat_axis=0, tiled=True)
    share = jnp.sum(shares.astype(F32), axis=0).astype(BF)
    spread = jnp.broadcast_to(share[None], (dp_count, 24, 640))
    totals = lax.all_to_all(spread, "dp", split_axis=0, concat_axis=0, tiled=True)
    total = jnp.sum(totals.astype(F32), axis=0) * ((dp_count * 8192) ** -0.5)
    returned = lax.all_to_all(
        returning.reshape(64, 16, 320), ("sp", "tp"), split_axis=0, concat_axis=0, tiled=True
    ).reshape(1024, 320)
    branch, qkv_grad = call(
        home_kernel, (arr((128, 1280), BF), arr((128, 1920), BF)), [VM] * 4,
        returned, dst, proj_weight, proj_bias.reshape(1, 1280),
    )
    return (
        branch.reshape(1, 64, 2, 1280),
        qkv_grad.reshape(1, 64, 2, 1920),
        total[:20].T,
        total[20, :20],
    )


def solution(mesh):
    in_specs = (
        P("dp", None, ("sp", "tp"), None),
        P("dp", None, ("sp", "tp"), None),
        P("dp", None),
        P(),
        P(),
    )
    out_specs = (
        P("dp", None, ("sp", "tp"), None),
        P("dp", None, ("sp", "tp"), None),
        P(None, ("sp", "tp")),
        P(("sp", "tp")),
    )
    return jax.shard_map(body, mesh=mesh, in_specs=in_specs, out_specs=out_specs, check_vma=False)
```

time: 523 us -> 171 us (0.33)
  the two profiles are of different devices: /device:TPU:32 before, /device:TPU:8 now
where the time goes in v1:
time: 171 us; the launch traced here: 170 us
  waiting for transfers between devices  95.9 us (56%)
  starting transfers between devices  44.2 us (26%)
  Pallas kernels  12.7 us (7%)
  local copies, waits for them, and re-layouts  10.7 us (6%)
  other arithmetic  5.23 us (3%)
    all_to_all x1, waiting for transfers between devices, body(): lax.all_to_all(outgoing.reshape(64, 16, 512), ('sp', 'tp'), split_axis=0,...  27.3 us
    all_to_all x1, waiting for transfers between devices, body(): lax.all_to_all(spread, 'dp', split_axis=0, concat_axis=0, tiled=True)  25.1 us
    all_to_all x1, waiting for transfers between devices, body(): lax.all_to_all(part.reshape(32, 24, 640), 'sp', split_axis=0, concat_axis...  21.3 us
    all_to_all x1, waiting for transfers between devices, body(): lax.all_to_all(returning.reshape(64, 16, 320), ('sp', 'tp'), split_axis=0...  21 us
    all_to_all x1, starting transfers between devices, body(): lax.all_to_all(outgoing.reshape(64, 16, 512), ('sp', 'tp'), split_axis=0,...  17.2 us
    pallas_call x5, Pallas kernels, call(): pl.pallas_call(kernel, out_shape=outs, in_specs=specs, out_specs=jax.tree...  12.7 us
    all_to_all x1, starting transfers between devices, body(): lax.all_to_all(spread, 'dp', split_axis=0, concat_axis=0, tiled=True)  12.2 us
    all_to_all x1, starting transfers between devices, body(): lax.all_to_all(returning.reshape(64, 16, 320), ('sp', 'tp'), split_axis=0...  6.59 us
  transfers between devices with their start and end apart: 5, of which 5 were waited for; matrix products, arithmetic and copies ran while one was open for 2% of the time, Pallas kernels for 3%

profile of v1, /device:TPU:8, one launch (start us, length us, event | category | flops | bytes accessed | tf_op | source)
XLA Modules:
  0.0 170.3 jit_solution(5244831844341223116)
XLA Ops:
  0.7 1.0 fusion.2
  1.7 0.6 convert_reduce_fusion.2
  2.5 0.7 multiply_add_fusion
  3.5 0.2 add.88.dst_ref
  3.6 1.2 reshape.125.qkv_ref
  5.0 3.1 %shard_map.93 = bf16[1024,512]{1,0:T(8,128)(2,1)} custom-call(bf16[128,1920]{1,0:T(8,128)(2,1)S(1)} %reshape.125.qkv_ref, bf16[128,1280]{1,0:T(8,128)(2,1)S(1)} %reshape.126.grad_ref, bf16[640,1280]{1,0:T(8,128)(2,1)S(1)} %copy-done, s32[1,1024]{1,0:T(1,128)S(1)} %add.88.dst_ref, s32[1,768]{1,0:T(1,128)S(1)} %copy-done.6), custom_call_target="tpu_custom_call" | custom-call | tf_op jit(solution)/shard_map/pallas_call | solution.py:24
  8.1 17.2 %all-to-all-start = ((bf16[64,16,512]{2,1,0:T(8,128)(2,1)}), bf16[64,16,512]{2,1,0:T(8,128)(2,1)S(1)}, u32[]{:S(2)}, u32[]{:S(2)}) async-start(bf16[64,16,512]{2,1,0:T(8,128)(2,1)} %bitcast.2), calls=%async_computation | async-start | bytes 2097152 | tf_op jit(solution)/shard_map/all_to_all | solution.py:182
  26.0 27.3 %all-to-all-done = bf16[64,16,512]{2,1,0:T(8,128)(2,1)S(1)} async-done(((bf16[64,16,512]{2,1,0:T(8,128)(2,1)}), bf16[64,16,512]{2,1,0:T(8,128)(2,1)S(1)}, u32[]{:S(2)}, u32[]{:S(2)}) %all-to-all-start) | async-done | bytes 1048608 | tf_op jit(solution)/shard_map/all_to_all | solution.py:182
  53.3 1.0 copy-done.1
  54.3 1.2 copy-done.2
  55.5 2.6 %shard_map.94 = (bf16[256,320]{1,0:T(8,128)(2,1)S(1)}, f32[1024,256]{1,0:T(8,128)S(1)}, bf16[1024,512]{1,0:T(8,128)(2,1)S(1)}) custom-call(s32[1]{0:T(128)} %bitcast.1.double_ref, bf16[1024,512]{1,0:T(8,128)(2,1)S(1)} %bitcast.14), custom_call_target="tpu_custom_call" | custom-call | tf_op jit(solution)/shard_map/pallas_call | solution.py:24
  58.1 1.0 copy-done.4
  59.1 2.1 %collective-permute-start = (bf16[256,320]{1,0:T(8,128)(2,1)S(1)}, bf16[256,320]{1,0:T(8,128)(2,1)S(1)}, u32[]{:S(2)}, u32[]{:S(2)}) collective-permute-start(bf16[256,320]{1,0:T(8,128)(2,1)S(1)} %get-tuple-element.11.att_ref.own_ref), channel_id=1, source_target_pairs={{0,1},{1,0},{2,3},{3,2},{4,5},{5,4},{6,7},{7,6},{8,9},{9,8},{10,11... | collective-permute-start | bytes 491528 | tf_op jit(solution)/shard_map/ppermute | solution.py:189
  61.2 1.2 collective-permute-done.other_ref
  62.4 1.6 shard_map.97
  64.0 1.0 copy-done.3
  65.0 6.2 %all-to-all-start.2 = ((bf16[32,24,640]{2,1,0:T(8,128)(2,1)}), bf16[32,24,640]{2,1,0:T(8,128)(2,1)}, u32[]{:S(2)}, u32[]{:S(2)}) async-start(bf16[32,24,640]{2,1,0:T(8,128)(2,1)} %bitcast.15), calls=%async_computation.2 | async-start | bytes 1966080 | tf_op jit(solution)/shard_map/all_to_all | solution.py:193
  71.1 1.2 copy-done.5
  72.4 3.9 %shard_map.95 = bf16[1024,320]{1,0:T(8,128)(2,1)} custom-call(bf16[1024,512]{1,0:T(8,128)(2,1)S(1)} %get-tuple-element.9.sorted_ref, f32[1024,256]{1,0:T(8,128)S(1)} %copy-done.5, bf16[256,320]{1,0:T(8,128)(2,1)S(1)} %get-tuple-element.11.att_ref.own_ref), custom_call_target="tpu_custom_call" | custom-call | tf_op jit(solution)/shard_map/pallas_call | solution.py:24
  76.2 21.3 %all-to-all-done.2 = bf16[32,24,640]{2,1,0:T(8,128)(2,1)} async-done(((bf16[32,24,640]{2,1,0:T(8,128)(2,1)}), bf16[32,24,640]{2,1,0:T(8,128)(2,1)}, u32[]{:S(2)}, u32[]{:S(2)}) %all-to-all-start.2) | async-done | bytes 983072 | tf_op jit(solution)/shard_map/all_to_all | solution.py:193
  97.5 6.6 %all-to-all-start.1 = ((bf16[64,16,320]{2,1,0:T(8,128)(2,1)}), bf16[64,16,320]{2,1,0:T(8,128)(2,1)S(1)}, u32[]{:S(2)}, u32[]{:S(2)}) async-start(bf16[64,16,320]{2,1,0:T(8,128)(2,1)} %bitcast.4), calls=%async_computation.1 | async-start | bytes 1572864 | tf_op jit(solution)/shard_map/all_to_all | solution.py:198
  104.1 1.4 reduce_sum.41
  105.5 21.0 %all-to-all-done.1 = bf16[64,16,320]{2,1,0:T(8,128)(2,1)S(1)} async-done(((bf16[64,16,320]{2,1,0:T(8,128)(2,1)}), bf16[64,16,320]{2,1,0:T(8,128)(2,1)S(1)}, u32[]{:S(2)}, u32[]{:S(2)}) %all-to-all-start.1) | async-done | bytes 655392 | tf_op jit(solution)/shard_map/all_to_all | solution.py:198
  126.5 0.8 broadcast_in_dim.11
  127.3 12.2 %all-to-all-start.3 = ((bf16[16,24,640]{2,1,0:T(8,128)(2,1)}), bf16[16,24,640]{2,1,0:T(8,128)(2,1)}, u32[]{:S(2)}, u32[]{:S(2)}) async-start(bf16[16,24,640]{2,1,0:T(8,128)(2,1)} %broadcast_in_dim.11), calls=%async_computation.3 | async-start | bytes 983040 | tf_op jit(solution)/shard_map/all_to_all | solution.py:196
  139.5 1.6 shard_map.96
  141.1 1.0 reshape.133
  142.1 0.8 reshape.132
  142.9 25.1 %all-to-all-done.3 = bf16[16,24,640]{2,1,0:T(8,128)(2,1)} async-done(((bf16[16,24,640]{2,1,0:T(8,128)(2,1)}), bf16[16,24,640]{2,1,0:T(8,128)(2,1)}, u32[]{:S(2)}, u32[]{:S(2)}) %all-to-all-start.3) | async-done | bytes 491552 | tf_op jit(solution)/shard_map/all_to_all | solution.py:196
  168.0 1.1 convert_reduce_fusion
  169.1 0.6 slice_bitcast_fusion
  169.8 0.5 slice_bitcast_fusion.1
  (22 shorter events, 0.6 us)
Async XLA Ops:
  0.6 4.4 %copy-start.6 = (s32[1,768]{1,0:T(1,128)S(1)}, s32[1,768]{1,0:T(1,128)}, u32[]{:S(2)}) copy-start(s32[1,768]{1,0:T(1,128)} %constant.31.clone.pick_ref) | copy-start | bytes 9220
  0.6 4.2 %copy-start.7 = (bf16[1,64,2,1280]{3,2,1,0:T(2,128)(2,1)S(1)}, bf16[1,64,2,1280]{3,2,1,0:T(2,128)(2,1)}, u32[]{:S(2)}) copy-start(bf16[1,64,2,1280]{3,2,1,0:T(2,128)(2,1)} %param.7) | copy-start | bytes 983044
  0.7 4.4 %copy-start = (bf16[640,1280]{1,0:T(8,128)(2,1)S(1)}, bf16[640,1280]{1,0:T(8,128)(2,1)}, u32[]{:S(2)}) copy-start(bf16[640,1280]{1,0:T(8,128)(2,1)} %weight_ref.3) | copy-start | bytes 4915204
  8.1 45.2 %all-to-all-start = ((bf16[64,16,512]{2,1,0:T(8,128)(2,1)}), bf16[64,16,512]{2,1,0:T(8,128)(2,1)S(1)}, u32[]{:S(2)}, u32[]{:S(2)}) async-start(bf16[64,16,512]{2,1,0:T(8,128)(2,1)} %bitcast.2), calls=%async_computation | async-start | bytes 2097152 | tf_op jit(solution)/shard_map/all_to_all | solution.py:182
  53.3 1.0 copy-start.1
  54.3 1.2 copy-start.2
  58.1 1.0 copy-start.4
  59.1 3.3 %collective-permute-start = (bf16[256,320]{1,0:T(8,128)(2,1)S(1)}, bf16[256,320]{1,0:T(8,128)(2,1)S(1)}, u32[]{:S(2)}, u32[]{:S(2)}) collective-permute-start(bf16[256,320]{1,0:T(8,128)(2,1)S(1)} %get-tuple-element.11.att_ref.own_ref), channel_id=1, source_target_pairs={{0,1},{1,0},{2,3},{3,2},{4,5},{5,4},{6,7},{7,6},{8,9},{9,8},{10,11... | collective-permute-start | bytes 491528 | tf_op jit(solution)/shard_map/ppermute | solution.py:189
  64.0 1.0 copy-start.3
  65.0 32.6 %all-to-all-start.2 = ((bf16[32,24,640]{2,1,0:T(8,128)(2,1)}), bf16[32,24,640]{2,1,0:T(8,128)(2,1)}, u32[]{:S(2)}, u32[]{:S(2)}) async-start(bf16[32,24,640]{2,1,0:T(8,128)(2,1)} %bitcast.15), calls=%async_computation.2 | async-start | bytes 1966080 | tf_op jit(solution)/shard_map/all_to_all | solution.py:193
  71.1 1.2 copy-start.5
  97.5 28.9 %all-to-all-start.1 = ((bf16[64,16,320]{2,1,0:T(8,128)(2,1)}), bf16[64,16,320]{2,1,0:T(8,128)(2,1)S(1)}, u32[]{:S(2)}, u32[]{:S(2)}) async-start(bf16[64,16,320]{2,1,0:T(8,128)(2,1)} %bitcast.4), calls=%async_computation.1 | async-start | bytes 1572864 | tf_op jit(solution)/shard_map/all_to_all | solution.py:198
  104.1 35.3 %copy-start.8 = (bf16[1280]{0:T(1024)(128)(2,1)S(1)}, bf16[1280]{0:T(1024)(128)(2,1)}, u32[]{:S(2)}) copy-start(bf16[1280]{0:T(1024)(128)(2,1)} %param.10) | copy-start | bytes 7684
  127.3 40.7 %all-to-all-start.3 = ((bf16[16,24,640]{2,1,0:T(8,128)(2,1)}), bf16[16,24,640]{2,1,0:T(8,128)(2,1)}, u32[]{:S(2)}, u32[]{:S(2)}) async-start(bf16[16,24,640]{2,1,0:T(8,128)(2,1)} %broadcast_in_dim.11), calls=%async_computation.3 | async-start | bytes 983040 | tf_op jit(solution)/shard_map/all_to_all | solution.py:196

commit v2 on v1

--- a/solution.py
+++ b/solution.py
@@ -13,7 +13,7 @@
 
 VM = pl.BlockSpec(memory_space=pltpu.VMEM)
 SM = pl.BlockSpec(memory_space=pltpu.SMEM)
-PARAMS = pltpu.CompilerParams(vmem_limit_bytes=48 * 1024 * 1024)
+PARAMS = pltpu.CompilerParams(vmem_limit_bytes=20 * 1024 * 1024)
 
 
 def dot(a, b, ca=1, cb=0):
@@ -44,7 +44,29 @@
     return ((i >> 2) & 3) * 256 + ((i >> 1) & 1) * 128 + (i >> 4) * 2 + (i & 1)
 
 
-def send_kernel(qkv_ref, grad_ref, weight_ref, dst_ref, pick_ref, out_ref):
+def placement(image_row):
+    row = lax.broadcasted_iota(jnp.int32, (64, 64), 0)
+    col = lax.broadcasted_iota(jnp.int32, (64, 64), 1)
+    image_rows = jnp.broadcast_to(image_row, (64, 64))
+    image_col = jnp.sum(jnp.where(row == col, image_rows, 0), axis=1, keepdims=True)
+    alike = jnp.where((image_col == image_rows) & (row != col), 1.0, 0.0)
+    twin_col = jnp.sum(alike, axis=1, keepdims=True)
+    twin_row = jnp.sum(alike, axis=0, keepdims=True)
+    rank = jnp.sum(jnp.where((row < col) & (twin_col == twin_row), 1.0, 0.0), axis=0, keepdims=True)
+    twins = jnp.sum(twin_row, axis=1, keepdims=True)
+    place = rank + jnp.where(twin_row > 0, 0.0, twins)
+    lane = lax.broadcasted_iota(jnp.int32, (64, 1024), 1)
+    block = lax.broadcasted_iota(jnp.int32, (64, 1024), 0)
+    widen = jnp.where(((lane >> 1) & 63) == block, 1.0, 0.0).astype(BF)
+    wide = dot(jnp.broadcast_to(place, (8, 64)).astype(BF), widen).astype(jnp.int32)
+    lane = lax.broadcasted_iota(jnp.int32, (8, 1024), 1)
+    dst = (wide >> 1) * 32 + ((lane >> 9) & 1) * 16 + ((lane >> 7) & 3) * 4 + (wide & 1) * 2 + (lane & 1)
+    return dst, jnp.broadcast_to(twins, (8, 1024)).astype(jnp.int32)
+
+
+def send_kernel(qkv_ref, grad_ref, weight_ref, image_ref, pick_ref, out_ref, info_ref):
+    dst, twins = placement(image_ref[...])
+    info_ref[...] = jnp.concatenate([dst, twins], axis=0)
     grad = grad_ref[...]
     delta = dot(grad, weight_ref[...], 1, 1).astype(BF)
     pick = rows_at(pick_ref[...], 640)
@@ -61,7 +83,7 @@
                 kind = delta[:, t * 320:(t + 1) * 320]
             blocks.append(jnp.concatenate([kind, picked[:, g * 192:(g + 1) * 192]], axis=1))
     stack = jnp.concatenate(blocks, axis=0)
-    out_ref[...] = dot(rows_at(dst_ref[...], 1024), stack).astype(BF)
+    out_ref[...] = dot(rows_at(dst[:1], 1024), stack).astype(BF)
 
 
 def head_masks(rows):
@@ -81,7 +103,7 @@
     return total
 
 
-def attend_kernel(double_ref, got_ref, att_ref, probs_ref, sorted_ref):
+def attend_kernel(own_ref, info_ref, got_ref, att_ref, probs_ref, sorted_ref):
     sel = rows_at(slot_rows((1, 1024), 1), 1024)
     rows = dot(sel, got_ref[...]).astype(BF)
     sorted_ref[...] = rows
@@ -90,7 +112,8 @@
     scores = dot(by_head(query, masks), key, 1, 1) * (HD ** -0.5)
     row = lax.broadcasted_iota(jnp.int32, (1024, 256), 0)
     col = lax.broadcasted_iota(jnp.int32, (1024, 256), 1)
-    apart = (((row ^ col) >> 7) & 1) > double_ref[0]
+    twins = info_ref[8:9, :256]
+    apart = (((row ^ col) >> 7) & 1) > jnp.where(2 * own_ref[0] < twins, 1, 0)
     scores = jnp.where(apart, masked_score, scores)
     exp_scores = jnp.exp(scores - jnp.max(scores, axis=-1, keepdims=True))
     probs = exp_scores / jnp.sum(exp_scores, axis=-1, keepdims=True)
@@ -137,8 +160,8 @@
     out_ref[...] = jnp.where(in_chunk == 20, bias, part).astype(BF)
 
 
-def home_kernel(got_ref, dst_ref, weight_ref, bias_ref, branch_ref, grad_ref):
-    rows = dot(rows_at(dst_ref[...], 1024), got_ref[...], 0, 0).astype(BF)
+def home_kernel(got_ref, info_ref, weight_ref, bias_ref, branch_ref, grad_ref):
+    rows = dot(rows_at(info_ref[:1, :], 1024), got_ref[...], 0, 0).astype(BF)
     att = jnp.concatenate([rows[:128], rows[512:640]], axis=1)
     branch_ref[...] = (dot(att, weight_ref[...]) + bias_ref[...].astype(F32)).astype(BF)
     grad_ref[...] = jnp.concatenate(
@@ -155,36 +178,18 @@
 def body(qkv, out_grad, block_image, proj_weight, proj_bias):
     own_sp, own_tp = lax.axis_index("sp"), lax.axis_index("tp")
     dp_count = lax.axis_size("dp")
-    images = block_image[0]
-    index = jnp.arange(64, dtype=jnp.int32)
-    alike = (images[:, None] == images[None, :]) & (index[:, None] != index[None, :])
-    twin = jnp.any(alike, axis=1)
-    twin_row = jnp.any(alike, axis=0)
-    before = index[None, :] < index[:, None]
-    rank = jnp.sum((before & (twin_row[None, :] == twin[:, None])).astype(jnp.int32), axis=1)
-    twins = jnp.sum(twin.astype(jnp.int32))
-    place = jnp.where(twin, rank, twins + rank)
-    is_double = (2 * own_sp < twins).astype(jnp.int32)[None]
-    four = jnp.arange(4, dtype=jnp.int32)
-    two = jnp.arange(2, dtype=jnp.int32)
-    dst = (
-        ((place >> 1) * 32 + (place & 1) * 2)[None, None, :, None]
-        + two[:, None, None, None] * 16
-        + four[None, :, None, None] * 4
-        + two[None, None, None, :]
-    ).reshape(1, 1024)
     qkv_rows = qkv.reshape(128, 1920)
     grad_rows = out_grad.reshape(128, 1280)
-    outgoing = call(
-        send_kernel, arr((1024, 512), BF), [VM] * 5,
-        qkv_rows, grad_rows, proj_weight, dst, jnp.asarray(picked_columns()),
+    outgoing, info = call(
+        send_kernel, (arr((1024, 512), BF), arr((16, 1024), jnp.int32)), [VM] * 5,
+        qkv_rows, grad_rows, proj_weight, block_image, jnp.asarray(picked_columns()),
     )
     arrived = lax.all_to_all(
         outgoing.reshape(64, 16, 512), ("sp", "tp"), split_axis=0, concat_axis=0, tiled=True
     ).reshape(1024, 512)
     attended, probs, ordered = call(
-        attend_kernel, (arr((256, 320), BF), arr((1024, 256), F32), arr((1024, 512), BF)), [SM, VM],
-        is_double, arrived,
+        attend_kernel, (arr((256, 320), BF), arr((1024, 256), F32), arr((1024, 512), BF)), [SM, VM, VM],
+        own_sp.astype(jnp.int32)[None], info, arrived,
     )
     other = lax.ppermute(attended, "tp", [(0, 1), (1, 0)])
     returning = call(back_kernel, arr((1024, 320), BF), [VM] * 3, ordered, probs, attended)
@@ -192,15 +197,14 @@
     part = call(weight_kernel, arr((768, 640), BF), [SM, VM, VM, VM], core, ordered, attended, other)
     shares = lax.all_to_all(part.reshape(32, 24, 640), "sp", split_axis=0, concat_axis=0, tiled=True)
     share = jnp.sum(shares.astype(F32), axis=0).astype(BF)
-    spread = jnp.broadcast_to(share[None], (dp_count, 24, 640))
-    totals = lax.all_to_all(spread, "dp", split_axis=0, concat_axis=0, tiled=True)
+    totals = lax.all_gather(share, "dp")
     total = jnp.sum(totals.astype(F32), axis=0) * ((dp_count * 8192) ** -0.5)
     returned = lax.all_to_all(
         returning.reshape(64, 16, 320), ("sp", "tp"), split_axis=0, concat_axis=0, tiled=True
     ).reshape(1024, 320)
     branch, qkv_grad = call(
         home_kernel, (arr((128, 1280), BF), arr((128, 1920), BF)), [VM] * 4,
-        returned, dst, proj_weight, proj_bias.reshape(1, 1280),
+        returned, info, proj_weight, proj_bias.reshape(1, 1280),
     )
     return (
         branch.reshape(1, 64, 2, 1280),

time: 171 us -> 163 us (0.953)
  the two profiles are of different devices: /device:TPU:8 before, /device:TPU:16 now
where the time goes in v2:
time: 163 us; the launch traced here: 162 us
  waiting for transfers between devices  67.5 us (41%)
  blocking collectives  38.4 us (24%)
  starting transfers between devices  30.7 us (19%)
  Pallas kernels  13 us (8%)
  local copies, waits for them, and re-layouts  10.2 us (6%)
    all_gather x1, blocking collectives, body(): totals = lax.all_gather(share, 'dp')  38.4 us
    all_to_all x1, waiting for transfers between devices, body(): lax.all_to_all(outgoing.reshape(64, 16, 512), ('sp', 'tp'), split_axis=0,...  28.5 us
    all_to_all x1, waiting for transfers between devices, body(): lax.all_to_all(part.reshape(32, 24, 640), 'sp', split_axis=0, concat_axis...  23.1 us
    all_to_all x1, starting transfers between devices, body(): lax.all_to_all(outgoing.reshape(64, 16, 512), ('sp', 'tp'), split_axis=0,...  17.2 us
    all_to_all x1, waiting for transfers between devices, body(): lax.all_to_all(returning.reshape(64, 16, 320), ('sp', 'tp'), split_axis=0...  14.6 us
    pallas_call x5, Pallas kernels, call(): pl.pallas_call(kernel, out_shape=outs, in_specs=specs, out_specs=jax.tree...  13 us
    all_to_all x1, starting transfers between devices, body(): lax.all_to_all(returning.reshape(64, 16, 320), ('sp', 'tp'), split_axis=0...  5.93 us
    all_to_all x1, starting transfers between devices, body(): lax.all_to_all(part.reshape(32, 24, 640), 'sp', split_axis=0, concat_axis...  5.56 us
  transfers between devices with their start and end apart: 4, of which 4 were waited for; matrix products, arithmetic and copies ran while one was open for 1% of the time, Pallas kernels for 2%

profile of v2, /device:TPU:16, one launch (start us, length us, event | category | flops | bytes accessed | tf_op | source)
XLA Modules:
  0.0 162.1 jit_solution(10829302870814938177)
XLA Ops:
  0.6 0.0 copy-start.7
  0.6 0.0 copy-start.8
  0.7 1.2 reshape.38.qkv_ref
  1.9 1.1 reshape.39.grad_ref
  3.0 0.0 copy-start
  3.0 1.4 copy-done
  4.4 3.3 %shard_map.93 = (bf16[1024,512]{1,0:T(8,128)(2,1)}, s32[16,1024]{1,0:T(8,128)S(1)}) custom-call(bf16[128,1920]{1,0:T(8,128)(2,1)S(1)} %reshape.38.qkv_ref, bf16[128,1280]{1,0:T(8,128)(2,1)S(1)} %reshape.39.grad_ref, bf16[640,1280]{1,0:T(8,128)(2,1)S(1)} %copy-done, s32[1,64]{1,0:T(1,128)S(1)} %copy-done.8, s32[1,768]{1,0:T(1,128)S(1)} %copy-done.7), custom_call_target="tpu_custom_call" | custom-call | tf_op jit(solution)/shard_map/pallas_call | solution.py:24
  7.7 17.2 %all-to-all-start = ((bf16[64,16,512]{2,1,0:T(8,128)(2,1)}), bf16[64,16,512]{2,1,0:T(8,128)(2,1)S(1)}, u32[]{:S(2)}, u32[]{:S(2)}) async-start(bf16[64,16,512]{2,1,0:T(8,128)(2,1)} %bitcast.1), calls=%async_computation | async-start | bytes 2097152 | tf_op jit(solution)/shard_map/all_to_all | solution.py:187
  24.9 28.5 %all-to-all-done = bf16[64,16,512]{2,1,0:T(8,128)(2,1)S(1)} async-done(((bf16[64,16,512]{2,1,0:T(8,128)(2,1)}), bf16[64,16,512]{2,1,0:T(8,128)(2,1)S(1)}, u32[]{:S(2)}, u32[]{:S(2)}) %all-to-all-start) | async-done | bytes 1048608 | tf_op jit(solution)/shard_map/all_to_all | solution.py:187
  53.4 2.6 %shard_map.94 = (bf16[256,320]{1,0:T(8,128)(2,1)S(1)}, f32[1024,256]{1,0:T(8,128)S(1)}, bf16[1024,512]{1,0:T(8,128)(2,1)S(1)}) custom-call(s32[1]{0:T(128)} %bitcast.own_ref, s32[16,1024]{1,0:T(8,128)S(1)} %get-tuple-element.11.info_ref, bf16[1024,512]{1,0:T(8,128)(2,1)S(1)} %bitcast.13), custom_call_target="tpu_custom_call" | custom-call | tf_op jit(solution)/shard_map/pallas_call | solution.py:24
  56.0 0.0 copy-start.3
  56.0 3.9 %shard_map.95 = bf16[1024,320]{1,0:T(8,128)(2,1)} custom-call(bf16[1024,512]{1,0:T(8,128)(2,1)S(1)} %get-tuple-element.13.sorted_ref, f32[1024,256]{1,0:T(8,128)S(1)} %get-tuple-element.14.probs_ref, bf16[256,320]{1,0:T(8,128)(2,1)S(1)} %get-tuple-element.15.att_ref.own_ref), custom_call_target="tpu_custom_call" | custom-call | tf_op jit(solution)/shard_map/pallas_call | solution.py:24
  59.9 5.9 %all-to-all-start.1 = ((bf16[64,16,320]{2,1,0:T(8,128)(2,1)}), bf16[64,16,320]{2,1,0:T(8,128)(2,1)S(1)}, u32[]{:S(2)}, u32[]{:S(2)}) async-start(bf16[64,16,320]{2,1,0:T(8,128)(2,1)} %bitcast.3), calls=%async_computation.1 | async-start | bytes 1572864 | tf_op jit(solution)/shard_map/all_to_all | solution.py:202
  65.9 2.1 %collective-permute-start = (bf16[256,320]{1,0:T(8,128)(2,1)S(1)}, bf16[256,320]{1,0:T(8,128)(2,1)S(1)}, u32[]{:S(2)}, u32[]{:S(2)}) collective-permute-start(bf16[256,320]{1,0:T(8,128)(2,1)S(1)} %get-tuple-element.15.att_ref.own_ref), channel_id=1, source_target_pairs={{0,1},{1,0},{2,3},{3,2},{4,5},{5,4},{6,7},{7,6},{8,9},{9,8},{10,11... | collective-permute-start | bytes 491528 | tf_op jit(solution)/shard_map/ppermute | solution.py:194
  67.9 1.3 collective-permute-done.other_ref
  69.2 0.7 copy-done.5
  69.9 0.9 copy-done.4
  70.8 0.9 copy-done.6
  71.8 1.6 shard_map.97
  73.4 0.9 copy-done.2
  74.3 14.6 %all-to-all-done.1 = bf16[64,16,320]{2,1,0:T(8,128)(2,1)S(1)} async-done(((bf16[64,16,320]{2,1,0:T(8,128)(2,1)}), bf16[64,16,320]{2,1,0:T(8,128)(2,1)S(1)}, u32[]{:S(2)}, u32[]{:S(2)}) %all-to-all-start.1) | async-done | bytes 655392 | tf_op jit(solution)/shard_map/all_to_all | solution.py:202
  88.9 5.6 %all-to-all-start.2 = ((bf16[32,24,640]{2,1,0:T(8,128)(2,1)}), bf16[32,24,640]{2,1,0:T(8,128)(2,1)}, u32[]{:S(2)}, u32[]{:S(2)}) async-start(bf16[32,24,640]{2,1,0:T(8,128)(2,1)} %bitcast.14), calls=%async_computation.2 | async-start | bytes 1966080 | tf_op jit(solution)/shard_map/all_to_all | solution.py:198
  94.5 0.0 copy-done.9
  94.5 1.6 %shard_map.96 = (bf16[128,1280]{1,0:T(8,128)(2,1)S(1)}, bf16[128,1920]{1,0:T(8,128)(2,1)S(1)}) custom-call(bf16[1024,320]{1,0:T(8,128)(2,1)S(1)} %bitcast.15, s32[16,1024]{1,0:T(8,128)S(1)} %get-tuple-element.11.info_ref, bf16[640,1280]{1,0:T(8,128)(2,1)S(1)} %copy-done.1, bf16[1,1280]{1,0:T(2,128)(2,1)S(1)} %reshape.44.bias_ref), custom_call_target="tpu_custom_call" | custom-call | tf_op jit(solution)/shard_map/pallas_call | solution.py:24
  96.2 0.9 reshape.45
  97.0 1.0 reshape.46
  98.0 23.1 %all-to-all-done.2 = bf16[32,24,640]{2,1,0:T(8,128)(2,1)} async-done(((bf16[32,24,640]{2,1,0:T(8,128)(2,1)}), bf16[32,24,640]{2,1,0:T(8,128)(2,1)}, u32[]{:S(2)}, u32[]{:S(2)}) %all-to-all-start.2) | async-done | bytes 983072 | tf_op jit(solution)/shard_map/all_to_all | solution.py:198
  121.1 1.3 reduce_sum.21
  122.5 38.4 %all-gather = bf16[384,640]{1,0:T(8,128)(2,1)S(1)} all-gather(bf16[24,640]{1,0:T(8,128)(2,1)S(1)} %reduce_sum.21), channel_id=2, replica_groups=mesh['dp'=16,'sp'=32,'tp'=2] {'dp'}, dimensions={0}, use_global_device_ids=true | all-gather | bytes 522240 | tf_op jit(solution)/shard_map/all_gather | solution.py:200
  160.8 0.1 convert_reduce_fusion
  160.9 0.6 slice_bitcast_fusion
  161.5 0.5 slice_bitcast_fusion.1
  (12 shorter events, 0.0 us)
Async XLA Ops:
  0.6 2.4 %copy-start.7 = (s32[1,768]{1,0:T(1,128)S(1)}, s32[1,768]{1,0:T(1,128)}, u32[]{:S(2)}) copy-start(s32[1,768]{1,0:T(1,128)} %constant.16.clone.pick_ref) | copy-start | bytes 9220
  0.6 2.4 %copy-start.8 = (s32[1,64]{1,0:T(1,128)S(1)}, s32[1,64]{1,0:T(1,128)}, u32[]{:S(2)}) copy-start(s32[1,64]{1,0:T(1,128)} %image_ref.1) | copy-start | bytes 772
  3.0 1.4 copy-start
  7.7 45.7 %all-to-all-start = ((bf16[64,16,512]{2,1,0:T(8,128)(2,1)}), bf16[64,16,512]{2,1,0:T(8,128)(2,1)S(1)}, u32[]{:S(2)}, u32[]{:S(2)}) async-start(bf16[64,16,512]{2,1,0:T(8,128)(2,1)} %bitcast.1), calls=%async_computation | async-start | bytes 2097152 | tf_op jit(solution)/shard_map/all_to_all | solution.py:187
  56.0 9.9 %copy-start.3 = (bf16[256,320]{1,0:T(8,128)(2,1)}, bf16[256,320]{1,0:T(8,128)(2,1)S(1)}, u32[]{:S(2)}) copy-start(bf16[256,320]{1,0:T(8,128)(2,1)S(1)} %get-tuple-element.15.att_ref.own_ref) | copy-start | bytes 491524
  59.9 29.0 %all-to-all-start.1 = ((bf16[64,16,320]{2,1,0:T(8,128)(2,1)}), bf16[64,16,320]{2,1,0:T(8,128)(2,1)S(1)}, u32[]{:S(2)}, u32[]{:S(2)}) async-start(bf16[64,16,320]{2,1,0:T(8,128)(2,1)} %bitcast.3), calls=%async_computation.1 | async-start | bytes 1572864 | tf_op jit(solution)/shard_map/all_to_all | solution.py:202
  65.9 3.3 %collective-permute-start = (bf16[256,320]{1,0:T(8,128)(2,1)S(1)}, bf16[256,320]{1,0:T(8,128)(2,1)S(1)}, u32[]{:S(2)}, u32[]{:S(2)}) collective-permute-start(bf16[256,320]{1,0:T(8,128)(2,1)S(1)} %get-tuple-element.15.att_ref.own_ref), channel_id=1, source_target_pairs={{0,1},{1,0},{2,3},{3,2},{4,5},{5,4},{6,7},{7,6},{8,9},{9,8},{10,11... | collective-permute-start | bytes 491528 | tf_op jit(solution)/shard_map/ppermute | solution.py:194
  69.2 0.7 copy-start.5
  69.9 0.9 copy-start.4
  70.8 0.9 copy-start.6
  71.7 22.8 %copy-start.9 = (bf16[1280]{0:T(1024)(128)(2,1)S(1)}, bf16[1280]{0:T(1024)(128)(2,1)}, u32[]{:S(2)}) copy-start(bf16[1280]{0:T(1024)(128)(2,1)} %param.10) | copy-start | bytes 7684
  71.7 22.8 %copy-start.1 = (bf16[640,1280]{1,0:T(8,128)(2,1)S(1)}, bf16[640,1280]{1,0:T(8,128)(2,1)}, u32[]{:S(2)}) copy-start(bf16[640,1280]{1,0:T(8,128)(2,1)} %weight_ref.3) | copy-start | bytes 4915204
  73.4 1.0 copy-start.2
  88.9 32.2 %all-to-all-start.2 = ((bf16[32,24,640]{2,1,0:T(8,128)(2,1)}), bf16[32,24,640]{2,1,0:T(8,128)(2,1)}, u32[]{:S(2)}, u32[]{:S(2)}) async-start(bf16[32,24,640]{2,1,0:T(8,128)(2,1)} %bitcast.14), calls=%async_computation.2 | async-start | bytes 1966080 | tf_op jit(solution)/shard_map/all_to_all | solution.py:198

commit v3 on v2

--- a/solution.py
+++ b/solution.py
@@ -1,3 +1,5 @@
+import functools
+
 import jax
 import jax.numpy as jnp
 import numpy as np
@@ -39,9 +41,10 @@
     return jnp.where(lax.broadcasted_iota(jnp.int32, (count, n), 0) == row_of, 1.0, 0.0).astype(BF)
 
 
-def slot_rows(shape, dim):
+def slot_rows(shape, dim, bits):
     i = lax.broadcasted_iota(jnp.int32, shape, dim)
-    return ((i >> 2) & 3) * 256 + ((i >> 1) & 1) * 128 + (i >> 4) * 2 + (i & 1)
+    kind = (i >> 2) & ((1 << bits) - 1)
+    return kind * 256 + ((i >> 1) & 1) * 128 + (i >> (2 + bits)) * 2 + (i & 1)
 
 
 def placement(image_row):
@@ -61,12 +64,13 @@
     wide = dot(jnp.broadcast_to(place, (8, 64)).astype(BF), widen).astype(jnp.int32)
     lane = lax.broadcasted_iota(jnp.int32, (8, 1024), 1)
     dst = (wide >> 1) * 32 + ((lane >> 9) & 1) * 16 + ((lane >> 7) & 3) * 4 + (wide & 1) * 2 + (lane & 1)
-    return dst, jnp.broadcast_to(twins, (8, 1024)).astype(jnp.int32)
+    back = (wide >> 1) * 16 + ((lane >> 8) & 1) * 8 + ((lane >> 7) & 1) * 4 + (wide & 1) * 2 + (lane & 1)
+    return dst, jnp.broadcast_to(twins, (8, 1024)).astype(jnp.int32), back
 
 
 def send_kernel(qkv_ref, grad_ref, weight_ref, image_ref, pick_ref, out_ref, info_ref):
-    dst, twins = placement(image_ref[...])
-    info_ref[...] = jnp.concatenate([dst, twins], axis=0)
+    dst, twins, back = placement(image_ref[...])
+    info_ref[...] = jnp.concatenate([dst, twins, back], axis=0)
     grad = grad_ref[...]
     delta = dot(grad, weight_ref[...], 1, 1).astype(BF)
     pick = rows_at(pick_ref[...], 640)
@@ -74,7 +78,8 @@
     high = dot(grad[:, 640:], pick).astype(BF)
     blocks = []
     for t in range(2):
-        picked = jnp.concatenate([low[:, t * 384:(t + 1) * 384], high[:, t * 384:(t + 1) * 384]], axis=1)
+        parts = [half[:, t * 384 + n * 128:t * 384 + (n + 1) * 128] for n in range(3) for half in (low, high)]
+        picked = jnp.concatenate(parts, axis=1)
         for g in range(4):
             if g < 3:
                 at = g * 640 + t * 320
@@ -104,7 +109,7 @@
 
 
 def attend_kernel(own_ref, info_ref, got_ref, att_ref, probs_ref, sorted_ref):
-    sel = rows_at(slot_rows((1, 1024), 1), 1024)
+    sel = rows_at(slot_rows((1, 1024), 1, 2), 1024)
     rows = dot(sel, got_ref[...]).astype(BF)
     sorted_ref[...] = rows
     query, key, value = rows[:256, :320], rows[256:512, :320], rows[512:768, :320]
@@ -134,9 +139,15 @@
     query_grad = own_head(dot(score_grad, key), masks).astype(BF)
     key_grad = dot(score_grad, query_heads, 0, 0).astype(BF)
     value_grad = dot(probs.astype(BF), delta_heads, 0, 0).astype(BF)
-    stack = jnp.concatenate([att_ref[...], query_grad, key_grad, value_grad], axis=0)
-    lane = lax.broadcasted_iota(jnp.int32, (1024, 1024), 1)
-    back = jnp.where(lane == slot_rows((1024, 1), 0), 1.0, 0.0).astype(BF)
+    stack = jnp.concatenate(
+        [
+            jnp.concatenate([att_ref[...], query_grad], axis=1),
+            jnp.concatenate([key_grad, value_grad], axis=1),
+        ],
+        axis=0,
+    )
+    lane = lax.broadcasted_iota(jnp.int32, (512, 512), 1)
+    back = jnp.where(lane == slot_rows((512, 1), 0, 1), 1.0, 0.0).astype(BF)
     out_ref[...] = dot(back, stack).astype(BF)
 
 
@@ -147,32 +158,51 @@
     own, other = own_ref[...], other_ref[...]
     att = jnp.concatenate([jnp.where(first, own, other), jnp.where(first, other, own)], axis=1)
     part = dot(grad, att, 0, 0)
+    odd = (lax.broadcasted_iota(jnp.int32, (256, 320), 0) & 1) == 1
+    rest = jnp.where(odd, part[512:, 320:], part[512:, :320])
     sums = dot(jnp.ones((8, 256), BF), grad)[:1]
-    row = lax.broadcasted_iota(jnp.int32, (768, 768), 0)
-    col = lax.broadcasted_iota(jnp.int32, (768, 768), 1)
-    start = row - 20
-    own_sums = jnp.where((col >= start) & (col < row), sums, 0.0).astype(BF)
-    in_chunk = lax.broadcasted_iota(jnp.int32, (768, 1), 0)
-    in_chunk = in_chunk - (in_chunk * 2731 >> 16) * 24
-    lane = lax.broadcasted_iota(jnp.int32, (768, 640), 1)
-    spread = jnp.where(lane == in_chunk, 1.0, 0.0).astype(BF)
+    row = lax.broadcasted_iota(jnp.int32, (256, 768), 0)
+    col = lax.broadcasted_iota(jnp.int32, (256, 768), 1)
+    own_sums = jnp.where(((col >> 3) & 31) == (row >> 3), sums, 0.0).astype(BF)
+    k = lax.broadcasted_iota(jnp.int32, (768, 64), 0)
+    lane = lax.broadcasted_iota(jnp.int32, (768, 64), 1)
+    at = jnp.where(k < 512, (k >> 8) * 8 + (k & 7), 16 + ((k & 7) >> 1))
+    spread = jnp.where((lane == at) & ((k < 512) | ((k & 1) == 0)), 1.0, 0.0).astype(BF)
     bias = dot(own_sums, spread)
-    out_ref[...] = jnp.where(in_chunk == 20, bias, part).astype(BF)
+    out_ref[...] = jnp.concatenate([part[:256], part[256:512], rest, bias], axis=1).astype(BF)
+
+
+def total_kernel(scale, got_ref, weight_ref, bias_ref):
+    total = got_ref[0].astype(F32)
+    for n in range(1, got_ref.shape[0]):
+        total = total + got_ref[n].astype(F32)
+    total = total * scale
+    weight_ref[0:8, :] = total[:, :640]
+    weight_ref[8:16, :] = total[:, 640:1280]
+    for n in range(4):
+        weight_ref[16 + n:17 + n, 0:320] = total[2 * n:2 * n + 1, 1280:1600]
+        weight_ref[16 + n:17 + n, 320:640] = total[2 * n + 1:2 * n + 2, 1280:1600]
+    bias_ref[...] = total[:1, 1600:]
 
 
 def home_kernel(got_ref, info_ref, weight_ref, bias_ref, branch_ref, grad_ref):
-    rows = dot(rows_at(info_ref[:1, :], 1024), got_ref[...], 0, 0).astype(BF)
-    att = jnp.concatenate([rows[:128], rows[512:640]], axis=1)
+    rows = dot(rows_at(info_ref[16:17, :512], 512), got_ref[...], 0, 0).astype(BF)
+    att = jnp.concatenate([rows[:128, :320], rows[256:384, :320]], axis=1)
     branch_ref[...] = (dot(att, weight_ref[...]) + bias_ref[...].astype(F32)).astype(BF)
     grad_ref[...] = jnp.concatenate(
-        [rows[(t * 4 + g) * 128:(t * 4 + g + 1) * 128] for g in range(1, 4) for t in range(2)], axis=1
+        [
+            rows[(t * 2 + p) * 128:(t * 2 + p + 1) * 128, n * 320:(n + 1) * 320]
+            for p, n in ((0, 1), (1, 0), (1, 1))
+            for t in range(2)
+        ],
+        axis=1,
     )
 
 
 def picked_columns():
     col = np.arange(768)
-    t, sp, j = col // 384, (col % 384) // 24, col % 24
-    return np.where(j < 20, sp * 40 + t * 20 + j, -1).astype(np.int32)[None]
+    t, group, sp, r = col // 384, (col // 128) % 3, (col // 8) % 16, col % 8
+    return (sp * 40 + t * 20 + np.where(group < 2, group * 8 + r, 16 + r // 2)).astype(np.int32)[None]
 
 
 def body(qkv, out_grad, block_image, proj_weight, proj_bias):
@@ -181,7 +211,7 @@
     qkv_rows = qkv.reshape(128, 1920)
     grad_rows = out_grad.reshape(128, 1280)
     outgoing, info = call(
-        send_kernel, (arr((1024, 512), BF), arr((16, 1024), jnp.int32)), [VM] * 5,
+        send_kernel, (arr((1024, 512), BF), arr((24, 1024), jnp.int32)), [VM] * 5,
         qkv_rows, grad_rows, proj_weight, block_image, jnp.asarray(picked_columns()),
     )
     arrived = lax.all_to_all(
@@ -192,16 +222,20 @@
         own_sp.astype(jnp.int32)[None], info, arrived,
     )
     other = lax.ppermute(attended, "tp", [(0, 1), (1, 0)])
-    returning = call(back_kernel, arr((1024, 320), BF), [VM] * 3, ordered, probs, attended)
+    returning = call(back_kernel, arr((512, 640), BF), [VM] * 3, ordered, probs, attended)
     core = own_tp.astype(jnp.int32)[None]
-    part = call(weight_kernel, arr((768, 640), BF), [SM, VM, VM, VM], core, ordered, attended, other)
-    shares = lax.all_to_all(part.reshape(32, 24, 640), "sp", split_axis=0, concat_axis=0, tiled=True)
+    part = call(weight_kernel, arr((256, 1664), BF), [SM, VM, VM, VM], core, ordered, attended, other)
+    shares = lax.all_to_all(part.reshape(32, 8, 1664), "sp", split_axis=0, concat_axis=0, tiled=True)
     share = jnp.sum(shares.astype(F32), axis=0).astype(BF)
+    share, returning = lax.optimization_barrier((share, returning))
     totals = lax.all_gather(share, "dp")
-    total = jnp.sum(totals.astype(F32), axis=0) * ((dp_count * 8192) ** -0.5)
+    total, sums = call(
+        functools.partial(total_kernel, (dp_count * 8192) ** -0.5),
+        (arr((20, 640), F32), arr((1, 64), F32)), [VM], totals,
+    )
     returned = lax.all_to_all(
-        returning.reshape(64, 16, 320), ("sp", "tp"), split_axis=0, concat_axis=0, tiled=True
-    ).reshape(1024, 320)
+        returning.reshape(64, 8, 640), ("sp", "tp"), split_axis=0, concat_axis=0, tiled=True
+    ).reshape(512, 640)
     branch, qkv_grad = call(
         home_kernel, (arr((128, 1280), BF), arr((128, 1920), BF)), [VM] * 4,
         returned, info, proj_weight, proj_bias.reshape(1, 1280),
@@ -209,8 +243,8 @@
     return (
         branch.reshape(1, 64, 2, 1280),
         qkv_grad.reshape(1, 64, 2, 1920),
-        total[:20].T,
-        total[20, :20],
+        total.T,
+        sums[0, :20],
     )
 
 

time: 163 us -> 141 us (0.87)
  the two profiles are of different devices: /device:TPU:16 before, /device:TPU:2 now
where the time goes in v3:
time: 141 us; the launch traced here: 140 us
  waiting for transfers between devices  51.3 us (36%)
  blocking collectives  37.9 us (27%)
  starting transfers between devices  30.5 us (22%)
  Pallas kernels  12.6 us (9%)
  local copies, waits for them, and re-layouts  6.1 us (4%)
    all_gather x1, blocking collectives, body(): totals = lax.all_gather(share, 'dp')  37.9 us
    all_to_all x1, waiting for transfers between devices, body(): lax.all_to_all(outgoing.reshape(64, 16, 512), ('sp', 'tp'), split_axis=0,...  28.9 us
    all_to_all x1, waiting for transfers between devices, body(): lax.all_to_all(part.reshape(32, 8, 1664), 'sp', split_axis=0, concat_axis...  21 us
    all_to_all x1, starting transfers between devices, body(): lax.all_to_all(outgoing.reshape(64, 16, 512), ('sp', 'tp'), split_axis=0,...  17.3 us
    pallas_call x6, Pallas kernels, call(): pl.pallas_call(kernel, out_shape=outs, in_specs=specs, out_specs=jax.tree...  12.6 us
    all_to_all x1, starting transfers between devices, body(): lax.all_to_all(returning.reshape(64, 8, 640), ('sp', 'tp'), split_axis=0,...  5.98 us
    all_to_all x1, starting transfers between devices, body(): lax.all_to_all(part.reshape(32, 8, 1664), 'sp', split_axis=0, concat_axis...  5.31 us
  transfers between devices with their start and end apart: 4, of which 3 were waited for; matrix products, arithmetic and copies ran while one was open for 0% of the time, Pallas kernels for 3%

profile of v3, /device:TPU:2, one launch (start us, length us, event | category | flops | bytes accessed | tf_op | source)
XLA Modules:
  0.0 140.5 jit_solution(18136585433553394560)
XLA Ops:
  0.6 0.0 copy-start.2
  0.6 0.0 copy-start.3
  0.7 1.1 reshape.39.grad_ref
  1.8 1.2 reshape.38.qkv_ref
  3.0 0.0 copy-done.2
  3.0 0.0 copy-done.3
  3.0 0.0 copy-start
  3.0 1.4 %copy-done = bf16[640,1280]{1,0:T(8,128)(2,1)S(1)} copy-done((bf16[640,1280]{1,0:T(8,128)(2,1)S(1)}, bf16[640,1280]{1,0:T(8,128)(2,1)}, u32[]{:S(2)}) %copy-start) | copy-done | bytes 1638424
  4.4 3.4 %shard_map.93 = (bf16[1024,512]{1,0:T(8,128)(2,1)}, s32[24,1024]{1,0:T(8,128)S(1)}) custom-call(bf16[128,1920]{1,0:T(8,128)(2,1)S(1)} %reshape.38.qkv_ref, bf16[128,1280]{1,0:T(8,128)(2,1)S(1)} %reshape.39.grad_ref, bf16[640,1280]{1,0:T(8,128)(2,1)S(1)} %copy-done, s32[1,64]{1,0:T(1,128)S(1)} %copy-done.3, s32[1,768]{1,0:T(1,128)S(1)} %copy-done.2), custom_call_target="tpu_custom_call" | custom-call | tf_op jit(solution)/shard_map/pallas_call | solution.py:26
  7.8 17.3 %all-to-all-start = ((bf16[64,16,512]{2,1,0:T(8,128)(2,1)}), bf16[64,16,512]{2,1,0:T(8,128)(2,1)S(1)}, u32[]{:S(2)}, u32[]{:S(2)}) async-start(bf16[64,16,512]{2,1,0:T(8,128)(2,1)} %bitcast.2), calls=%async_computation | async-start | bytes 2097152 | tf_op jit(solution)/shard_map/all_to_all | solution.py:217
  25.1 28.9 %all-to-all-done = bf16[64,16,512]{2,1,0:T(8,128)(2,1)S(1)} async-done(((bf16[64,16,512]{2,1,0:T(8,128)(2,1)}), bf16[64,16,512]{2,1,0:T(8,128)(2,1)S(1)}, u32[]{:S(2)}, u32[]{:S(2)}) %all-to-all-start) | async-done | bytes 1048608 | tf_op jit(solution)/shard_map/all_to_all | solution.py:217
  54.0 2.6 %shard_map.94 = (bf16[256,320]{1,0:T(8,128)(2,1)S(1)}, f32[1024,256]{1,0:T(8,128)S(1)}, bf16[1024,512]{1,0:T(8,128)(2,1)S(1)}) custom-call(s32[1]{0:T(128)} %bitcast.1.own_ref, s32[24,1024]{1,0:T(8,128)S(1)} %get-tuple-element.15.info_ref, bf16[1024,512]{1,0:T(8,128)(2,1)S(1)} %bitcast.11), custom_call_target="tpu_custom_call" | custom-call | tf_op jit(solution)/shard_map/pallas_call | solution.py:26
  56.6 1.9 %collective-permute-start = (bf16[256,320]{1,0:T(8,128)(2,1)S(1)}, bf16[256,320]{1,0:T(8,128)(2,1)S(1)}, u32[]{:S(2)}, u32[]{:S(2)}) collective-permute-start(bf16[256,320]{1,0:T(8,128)(2,1)S(1)} %get-tuple-element.18.own_ref.att_ref), channel_id=1, source_target_pairs={{0,1},{1,0},{2,3},{3,2},{4,5},{5,4},{6,7},{7,6},{8,9},{9,8},{10,11... | collective-permute-start | bytes 491528 | tf_op jit(solution)/shard_map/ppermute | solution.py:224
  58.5 1.4 collective-permute-done.other_ref
  59.9 1.8 %shard_map.95 = bf16[256,1664]{1,0:T(8,128)(2,1)} custom-call(s32[1]{0:T(128)} %bitcast.core_ref, bf16[1024,512]{1,0:T(8,128)(2,1)S(1)} %get-tuple-element.17.sorted_ref, bf16[256,320]{1,0:T(8,128)(2,1)S(1)} %get-tuple-element.18.own_ref.att_ref, bf16[256,320]{1,0:T(8,128)(2,1)S(1)} %collective-permute-done.other_ref), custom_call_target="tpu_custom_call" | custom-call | tf_op jit(solution)/shard_map/pallas_call | solution.py:26
  61.8 5.3 %all-to-all-start.1 = ((bf16[32,8,1664]{2,1,0:T(8,128)(2,1)}), bf16[32,8,1664]{2,1,0:T(8,128)(2,1)}, u32[]{:S(2)}, u32[]{:S(2)}) async-start(bf16[32,8,1664]{2,1,0:T(8,128)(2,1)} %bitcast.4), calls=%async_computation.1 | async-start | bytes 1703936 | tf_op jit(solution)/shard_map/all_to_all | solution.py:228
  67.1 3.2 %shard_map.96 = bf16[512,640]{1,0:T(8,128)(2,1)} custom-call(bf16[1024,512]{1,0:T(8,128)(2,1)S(1)} %get-tuple-element.17.sorted_ref, f32[1024,256]{1,0:T(8,128)S(1)} %get-tuple-element.19.probs_ref, bf16[256,320]{1,0:T(8,128)(2,1)S(1)} %get-tuple-element.18.own_ref.att_ref), custom_call_target="tpu_custom_call" | custom-call | tf_op jit(solution)/shard_map/pallas_call | solution.py:26
  70.2 0.0 copy-start.4
  70.2 0.0 copy-start.1
  70.2 21.0 %all-to-all-done.1 = bf16[32,8,1664]{2,1,0:T(8,128)(2,1)} async-done(((bf16[32,8,1664]{2,1,0:T(8,128)(2,1)}), bf16[32,8,1664]{2,1,0:T(8,128)(2,1)}, u32[]{:S(2)}, u32[]{:S(2)}) %all-to-all-start.1) | async-done | bytes 852000 | tf_op jit(solution)/shard_map/all_to_all | solution.py:228
  91.3 1.3 reduce_sum.12
  92.6 6.0 %all-to-all-start.2 = ((bf16[64,8,640]{2,1,0:T(8,128)(2,1)}), bf16[64,8,640]{2,1,0:T(8,128)(2,1)S(1)}, u32[]{:S(2)}, u32[]{:S(2)}) async-start(bf16[64,8,640]{2,1,0:T(8,128)(2,1)} %bitcast.5), calls=%async_computation.2 | async-start | bytes 1310720 | tf_op jit(solution)/shard_map/all_to_all | solution.py:236
  98.6 0.0 copy-done.4
  98.6 37.9 %all-gather = bf16[128,1664]{1,0:T(8,128)(2,1)S(1)} all-gather(bf16[8,1664]{1,0:T(8,128)(2,1)S(1)} %reduce_sum.12), channel_id=2, replica_groups=mesh['dp'=16,'sp'=32,'tp'=2] {'dp'}, dimensions={0}, use_global_device_ids=true | all-gather | bytes 452608 | tf_op jit(solution)/shard_map/all_gather | solution.py:231
  136.4 0.7 shard_map.98
  137.2 0.5 slice_bitcast_fusion
  137.7 0.0 all-to-all-done.2
  137.7 0.0 copy-done.1
  137.7 0.9 shard_map.97
  138.6 0.9 reshape.46
  139.5 1.0 reshape.47
  (1 shorter events, 0.0 us)
Async XLA Ops:
  0.6 2.4 %copy-start.2 = (s32[1,768]{1,0:T(1,128)S(1)}, s32[1,768]{1,0:T(1,128)}, u32[]{:S(2)}) copy-start(s32[1,768]{1,0:T(1,128)} %constant.13.clone.pick_ref) | copy-start | bytes 9220
  0.6 2.4 %copy-start.3 = (s32[1,64]{1,0:T(1,128)S(1)}, s32[1,64]{1,0:T(1,128)}, u32[]{:S(2)}) copy-start(s32[1,64]{1,0:T(1,128)} %image_ref.1) | copy-start | bytes 772
  3.0 1.4 %copy-start = (bf16[640,1280]{1,0:T(8,128)(2,1)S(1)}, bf16[640,1280]{1,0:T(8,128)(2,1)}, u32[]{:S(2)}) copy-start(bf16[640,1280]{1,0:T(8,128)(2,1)} %weight_ref.3) | copy-start | bytes 4915204
  7.8 46.2 %all-to-all-start = ((bf16[64,16,512]{2,1,0:T(8,128)(2,1)}), bf16[64,16,512]{2,1,0:T(8,128)(2,1)S(1)}, u32[]{:S(2)}, u32[]{:S(2)}) async-start(bf16[64,16,512]{2,1,0:T(8,128)(2,1)} %bitcast.2), calls=%async_computation | async-start | bytes 2097152 | tf_op jit(solution)/shard_map/all_to_all | solution.py:217
  56.6 3.3 %collective-permute-start = (bf16[256,320]{1,0:T(8,128)(2,1)S(1)}, bf16[256,320]{1,0:T(8,128)(2,1)S(1)}, u32[]{:S(2)}, u32[]{:S(2)}) collective-permute-start(bf16[256,320]{1,0:T(8,128)(2,1)S(1)} %get-tuple-element.18.own_ref.att_ref), channel_id=1, source_target_pairs={{0,1},{1,0},{2,3},{3,2},{4,5},{5,4},{6,7},{7,6},{8,9},{9,8},{10,11... | collective-permute-start | bytes 491528 | tf_op jit(solution)/shard_map/ppermute | solution.py:224
  61.8 29.5 %all-to-all-start.1 = ((bf16[32,8,1664]{2,1,0:T(8,128)(2,1)}), bf16[32,8,1664]{2,1,0:T(8,128)(2,1)}, u32[]{:S(2)}, u32[]{:S(2)}) async-start(bf16[32,8,1664]{2,1,0:T(8,128)(2,1)} %bitcast.4), calls=%async_computation.1 | async-start | bytes 1703936 | tf_op jit(solution)/shard_map/all_to_all | solution.py:228
  70.2 28.3 %copy-start.4 = (bf16[1280]{0:T(1024)(128)(2,1)S(1)}, bf16[1280]{0:T(1024)(128)(2,1)}, u32[]{:S(2)}) copy-start(bf16[1280]{0:T(1024)(128)(2,1)} %param.10) | copy-start | bytes 7684
  70.2 67.5 %copy-start.1 = (bf16[640,1280]{1,0:T(8,128)(2,1)S(1)}, bf16[640,1280]{1,0:T(8,128)(2,1)}, u32[]{:S(2)}) copy-start(bf16[640,1280]{1,0:T(8,128)(2,1)} %weight_ref.3) | copy-start | bytes 4915204
  92.6 45.1 %all-to-all-start.2 = ((bf16[64,8,640]{2,1,0:T(8,128)(2,1)}), bf16[64,8,640]{2,1,0:T(8,128)(2,1)S(1)}, u32[]{:S(2)}, u32[]{:S(2)}) async-start(bf16[64,8,640]{2,1,0:T(8,128)(2,1)} %bitcast.5), calls=%async_computation.2 | async-start | bytes 1310720 | tf_op jit(solution)/shard_map/all_to_all | solution.py:236

commit v4 on v3

--- a/solution.py
+++ b/solution.py
@@ -2,7 +2,6 @@
 
 import jax
 import jax.numpy as jnp
-import numpy as np
 from jax import lax
 from jax.experimental import pallas as pl
 from jax.experimental.pallas import tpu as pltpu
@@ -15,7 +14,9 @@
 
 VM = pl.BlockSpec(memory_space=pltpu.VMEM)
 SM = pl.BlockSpec(memory_space=pltpu.SMEM)
+HBM = pl.BlockSpec(memory_space=pltpu.HBM)
 PARAMS = pltpu.CompilerParams(vmem_limit_bytes=20 * 1024 * 1024)
+WHOLE = pltpu.CompilerParams(vmem_limit_bytes=60 * 1024 * 1024)
 
 
 def dot(a, b, ca=1, cb=0):
@@ -44,7 +45,7 @@
 def slot_rows(shape, dim, bits):
     i = lax.broadcasted_iota(jnp.int32, shape, dim)
     kind = (i >> 2) & ((1 << bits) - 1)
-    return kind * 256 + ((i >> 1) & 1) * 128 + (i >> (2 + bits)) * 2 + (i & 1)
+    return kind * 64 + ((i >> 1) & 1) * 32 + (i >> (2 + bits)) * 2 + (i & 1)
 
 
 def placement(image_row):
@@ -58,37 +59,56 @@
     rank = jnp.sum(jnp.where((row < col) & (twin_col == twin_row), 1.0, 0.0), axis=0, keepdims=True)
     twins = jnp.sum(twin_row, axis=1, keepdims=True)
     place = rank + jnp.where(twin_row > 0, 0.0, twins)
-    lane = lax.broadcasted_iota(jnp.int32, (64, 1024), 1)
-    block = lax.broadcasted_iota(jnp.int32, (64, 1024), 0)
+    lane = lax.broadcasted_iota(jnp.int32, (64, 512), 1)
+    block = lax.broadcasted_iota(jnp.int32, (64, 512), 0)
     widen = jnp.where(((lane >> 1) & 63) == block, 1.0, 0.0).astype(BF)
     wide = dot(jnp.broadcast_to(place, (8, 64)).astype(BF), widen).astype(jnp.int32)
-    lane = lax.broadcasted_iota(jnp.int32, (8, 1024), 1)
-    dst = (wide >> 1) * 32 + ((lane >> 9) & 1) * 16 + ((lane >> 7) & 3) * 4 + (wide & 1) * 2 + (lane & 1)
-    back = (wide >> 1) * 16 + ((lane >> 8) & 1) * 8 + ((lane >> 7) & 1) * 4 + (wide & 1) * 2 + (lane & 1)
-    return dst, jnp.broadcast_to(twins, (8, 1024)).astype(jnp.int32), back
-
-
-def send_kernel(qkv_ref, grad_ref, weight_ref, image_ref, pick_ref, out_ref, info_ref):
+    lane = lax.broadcasted_iota(jnp.int32, (8, 512), 1)
+    base = (wide >> 1) * 16 + (wide & 1) * 2 + (lane & 1)
+    dst = base + ((lane >> 7) & 3) * 4
+    back = base + ((lane >> 8) & 1) * 8 + ((lane >> 7) & 1) * 4
+    return dst, jnp.broadcast_to(twins, (8, 512)).astype(jnp.int32), back
+
+
+def picked_columns():
+    k = lax.broadcasted_iota(jnp.int32, (1, 768), 1)
+    t = jnp.where(k >= 384, 1, 0)
+    k = k - 384 * t
+    return ((k >> 3) & 15) * 40 + t * 20 + jnp.where(k < 256, (k >> 7) * 8 + (k & 7), 16 + ((k & 7) >> 1))
+
+
+def send_kernel(
+    qkv_hbm, grad_hbm, weight_hbm, image_hbm, out_ref, info_ref, qkv_ref, grad_ref, weight_ref, image_ref, sems
+):
+    pairs = ((image_hbm, image_ref), (grad_hbm, grad_ref), (qkv_hbm, qkv_ref), (weight_hbm, weight_ref))
+    copies = [pltpu.make_async_copy(a, b, sems.at[n]) for n, (a, b) in enumerate(pairs)]
+    for copy in copies:
+        copy.start()
+    pick = rows_at(picked_columns(), 640)
+    copies[0].wait()
     dst, twins, back = placement(image_ref[...])
     info_ref[...] = jnp.concatenate([dst, twins, back], axis=0)
-    grad = grad_ref[...]
-    delta = dot(grad, weight_ref[...], 1, 1).astype(BF)
-    pick = rows_at(pick_ref[...], 640)
+    move = rows_at(dst[:1], 512)
+    copies[1].wait()
+    grad = grad_ref[...].reshape(128, 1280)
     low = dot(grad[:, :640], pick).astype(BF)
     high = dot(grad[:, 640:], pick).astype(BF)
-    blocks = []
+    copies[2].wait()
+    qkv = qkv_ref[...].reshape(128, 1920)
+    copies[3].wait()
+    delta = dot(grad, weight_ref[...], 1, 1).astype(BF)
     for t in range(2):
         parts = [half[:, t * 384 + n * 128:t * 384 + (n + 1) * 128] for n in range(3) for half in (low, high)]
         picked = jnp.concatenate(parts, axis=1)
+        blocks = []
         for g in range(4):
             if g < 3:
-                at = g * 640 + t * 320
-                kind = qkv_ref[:, at:at + 320]
+                kind = qkv[:, g * 640 + t * 320:g * 640 + (t + 1) * 320]
             else:
                 kind = delta[:, t * 320:(t + 1) * 320]
             blocks.append(jnp.concatenate([kind, picked[:, g * 192:(g + 1) * 192]], axis=1))
-    stack = jnp.concatenate(blocks, axis=0)
-    out_ref[...] = dot(rows_at(dst[:1], 1024), stack).astype(BF)
+        stack = jnp.concatenate(blocks, axis=0)
+        out_ref[:, t] = dot(move, stack).astype(BF).reshape(32, 16, 512)
 
 
 def head_masks(rows):
@@ -109,21 +129,26 @@
 
 
 def attend_kernel(own_ref, info_ref, got_ref, att_ref, probs_ref, sorted_ref):
-    sel = rows_at(slot_rows((1, 1024), 1, 2), 1024)
-    rows = dot(sel, got_ref[...]).astype(BF)
-    sorted_ref[...] = rows
-    query, key, value = rows[:256, :320], rows[256:512, :320], rows[512:768, :320]
+    sel = rows_at(slot_rows((1, 256), 1, 2), 256)
+    quarters = [dot(sel, got_ref[n * 256:(n + 1) * 256, :]).astype(BF) for n in range(4)]
+    kinds = [jnp.concatenate([x[g * 64:(g + 1) * 64] for x in quarters], axis=0) for g in range(4)]
+    for g in range(4):
+        sorted_ref[g * 256:(g + 1) * 256, :] = kinds[g]
+    query, key, value = kinds[0][:, :320], kinds[1][:, :320], kinds[2][:, :320]
     masks = head_masks(256)
     scores = dot(by_head(query, masks), key, 1, 1) * (HD ** -0.5)
-    row = lax.broadcasted_iota(jnp.int32, (1024, 256), 0)
-    col = lax.broadcasted_iota(jnp.int32, (1024, 256), 1)
+    row = lax.broadcasted_iota(jnp.int32, (256, 256), 0)
+    col = lax.broadcasted_iota(jnp.int32, (256, 256), 1)
     twins = info_ref[8:9, :256]
-    apart = (((row ^ col) >> 7) & 1) > jnp.where(2 * own_ref[0] < twins, 1, 0)
-    scores = jnp.where(apart, masked_score, scores)
-    exp_scores = jnp.exp(scores - jnp.max(scores, axis=-1, keepdims=True))
-    probs = exp_scores / jnp.sum(exp_scores, axis=-1, keepdims=True)
-    probs_ref[...] = probs
-    att_ref[...] = own_head(dot(probs.astype(BF), value), masks).astype(BF)
+    apart = (((row ^ col) >> 5) & 1) > jnp.where(2 * own_ref[0] < twins, 1, 0)
+    probs_bf = []
+    for h in range(4):
+        own = jnp.where(apart, masked_score, scores[h * 256:(h + 1) * 256])
+        exp_scores = jnp.exp(own - jnp.max(own, axis=-1, keepdims=True))
+        probs = exp_scores / jnp.sum(exp_scores, axis=-1, keepdims=True)
+        probs_ref[h * 256:(h + 1) * 256, :] = probs
+        probs_bf.append(probs.astype(BF))
+    att_ref[...] = own_head(dot(jnp.concatenate(probs_bf, axis=0), value), masks).astype(BF)
 
 
 def back_kernel(sorted_ref, probs_ref, att_ref, out_ref):
@@ -139,16 +164,13 @@
     query_grad = own_head(dot(score_grad, key), masks).astype(BF)
     key_grad = dot(score_grad, query_heads, 0, 0).astype(BF)
     value_grad = dot(probs.astype(BF), delta_heads, 0, 0).astype(BF)
-    stack = jnp.concatenate(
-        [
-            jnp.concatenate([att_ref[...], query_grad], axis=1),
-            jnp.concatenate([key_grad, value_grad], axis=1),
-        ],
-        axis=0,
-    )
-    lane = lax.broadcasted_iota(jnp.int32, (512, 512), 1)
-    back = jnp.where(lane == slot_rows((512, 1), 0, 1), 1.0, 0.0).astype(BF)
-    out_ref[...] = dot(back, stack).astype(BF)
+    first = jnp.concatenate([att_ref[...], query_grad], axis=1)
+    second = jnp.concatenate([key_grad, value_grad], axis=1)
+    lane = lax.broadcasted_iota(jnp.int32, (128, 128), 1)
+    back = jnp.where(lane == slot_rows((128, 1), 0, 1), 1.0, 0.0).astype(BF)
+    for n in range(4):
+        stack = jnp.concatenate([first[n * 64:(n + 1) * 64], second[n * 64:(n + 1) * 64]], axis=0)
+        out_ref[n * 128:(n + 1) * 128, :] = dot(back, stack).astype(BF)
 
 
 def weight_kernel(core_ref, sorted_ref, own_ref, other_ref, out_ref):
@@ -186,34 +208,32 @@
 
 
 def home_kernel(got_ref, info_ref, weight_ref, bias_ref, branch_ref, grad_ref):
-    rows = dot(rows_at(info_ref[16:17, :512], 512), got_ref[...], 0, 0).astype(BF)
+    rows = dot(rows_at(info_ref[16:17, :], 512), got_ref[...], 0, 0).astype(BF)
     att = jnp.concatenate([rows[:128, :320], rows[256:384, :320]], axis=1)
-    branch_ref[...] = (dot(att, weight_ref[...]) + bias_ref[...].astype(F32)).astype(BF)
-    grad_ref[...] = jnp.concatenate(
-        [
-            rows[(t * 2 + p) * 128:(t * 2 + p + 1) * 128, n * 320:(n + 1) * 320]
-            for p, n in ((0, 1), (1, 0), (1, 1))
-            for t in range(2)
-        ],
-        axis=1,
-    )
-
-
-def picked_columns():
-    col = np.arange(768)
-    t, group, sp, r = col // 384, (col // 128) % 3, (col // 8) % 16, col % 8
-    return (sp * 40 + t * 20 + np.where(group < 2, group * 8 + r, 16 + r // 2)).astype(np.int32)[None]
+    branch = dot(att, weight_ref[...]) + bias_ref[...].astype(F32)
+    branch_ref[...] = branch.astype(BF).reshape(64, 2, 1280)
+    for n, (p, m) in enumerate(((0, 1), (1, 0), (1, 1))):
+        both = [rows[(t * 2 + p) * 128:(t * 2 + p + 1) * 128, m * 320:(m + 1) * 320] for t in range(2)]
+        grad_ref[:, :, n * 640:(n + 1) * 640] = jnp.concatenate(both, axis=1).reshape(64, 2, 640)
 
 
 def body(qkv, out_grad, block_image, proj_weight, proj_bias):
     own_sp, own_tp = lax.axis_index("sp"), lax.axis_index("tp")
     dp_count = lax.axis_size("dp")
-    qkv_rows = qkv.reshape(128, 1920)
-    grad_rows = out_grad.reshape(128, 1280)
-    outgoing, info = call(
-        send_kernel, (arr((1024, 512), BF), arr((24, 1024), jnp.int32)), [VM] * 5,
-        qkv_rows, grad_rows, proj_weight, block_image, jnp.asarray(picked_columns()),
-    )
+    outgoing, info = pl.pallas_call(
+        send_kernel,
+        out_shape=(arr((32, 2, 16, 512), BF), arr((24, 512), jnp.int32)),
+        in_specs=[HBM] * 4,
+        out_specs=(VM, VM),
+        scratch_shapes=[
+            pltpu.VMEM((64, 2, 1920), BF),
+            pltpu.VMEM((64, 2, 1280), BF),
+            pltpu.VMEM((640, 1280), BF),
+            pltpu.VMEM((1, 64), jnp.int32),
+            pltpu.SemaphoreType.DMA((4,)),
+        ],
+        compiler_params=WHOLE,
+    )(qkv[0], out_grad[0], proj_weight, block_image)
     arrived = lax.all_to_all(
         outgoing.reshape(64, 16, 512), ("sp", "tp"), split_axis=0, concat_axis=0, tiled=True
     ).reshape(1024, 512)
@@ -228,7 +248,12 @@
     shares = lax.all_to_all(part.reshape(32, 8, 1664), "sp", split_axis=0, concat_axis=0, tiled=True)
     share = jnp.sum(shares.astype(F32), axis=0).astype(BF)
     share, returning = lax.optimization_barrier((share, returning))
-    totals = lax.all_gather(share, "dp")
+    count = dp_count // 4
+    near = [[4 * n + m for m in range(4)] for n in range(count)]
+    far = [[4 * n + m for n in range(count)] for m in range(4)]
+    fours = lax.all_gather(share, "dp", axis_index_groups=near)
+    fours = jnp.sum(fours.astype(F32), axis=0).astype(BF)
+    totals = lax.all_gather(fours, "dp", axis_index_groups=far)
     total, sums = call(
         functools.partial(total_kernel, (dp_count * 8192) ** -0.5),
         (arr((20, 640), F32), arr((1, 64), F32)), [VM], totals,
@@ -237,12 +262,12 @@
         returning.reshape(64, 8, 640), ("sp", "tp"), split_axis=0, concat_axis=0, tiled=True
     ).reshape(512, 640)
     branch, qkv_grad = call(
-        home_kernel, (arr((128, 1280), BF), arr((128, 1920), BF)), [VM] * 4,
+        home_kernel, (arr((64, 2, 1280), BF), arr((64, 2, 1920), BF)), [VM] * 4,
         returned, info, proj_weight, proj_bias.reshape(1, 1280),
     )
     return (
-        branch.reshape(1, 64, 2, 1280),
-        qkv_grad.reshape(1, 64, 2, 1920),
+        branch[None],
+        qkv_grad[None],
         total.T,
         sums[0, :20],
     )

time: 141 us -> 135 us (0.957)
  the two profiles are of different devices: /device:TPU:2 before, /device:TPU:4 now
where the time goes in v4:
time: 135 us; the launch traced here: 134 us
  waiting for transfers between devices  51.6 us (38%)
  blocking collectives  36.4 us (27%)
  starting transfers between devices  30.6 us (23%)
  Pallas kernels  13 us (10%)
    all_to_all x1, waiting for transfers between devices, body(): lax.all_to_all(outgoing.reshape(64, 16, 512), ('sp', 'tp'), split_axis=0,...  28.9 us
    all_gather x1, blocking collectives, body(): totals = lax.all_gather(fours, 'dp', axis_index_groups=far)  23 us
    all_to_all x1, waiting for transfers between devices, body(): lax.all_to_all(part.reshape(32, 8, 1664), 'sp', split_axis=0, concat_axis...  21.3 us
    all_to_all x1, starting transfers between devices, body(): lax.all_to_all(outgoing.reshape(64, 16, 512), ('sp', 'tp'), split_axis=0,...  17.4 us
    all_gather x1, blocking collectives, body(): fours = lax.all_gather(share, 'dp', axis_index_groups=near)  13.5 us
    pallas_call x5, Pallas kernels, call(): pl.pallas_call(kernel, out_shape=outs, in_specs=specs, out_specs=jax.tree...  9.04 us
    all_to_all x1, starting transfers between devices, body(): lax.all_to_all(returning.reshape(64, 8, 640), ('sp', 'tp'), split_axis=0,...  5.98 us
    all_to_all x1, starting transfers between devices, body(): lax.all_to_all(part.reshape(32, 8, 1664), 'sp', split_axis=0, concat_axis...  5.3 us
  transfers between devices with their start and end apart: 4, of which 3 were waited for; matrix products, arithmetic and copies ran while one was open for 0% of the time, Pallas kernels for 3%

profile of v4, /device:TPU:4, one launch (start us, length us, event | category | flops | bytes accessed | tf_op | source)
XLA Modules:
  0.0 134.2 jit_solution(16712374734949821275)
XLA Ops:
  0.6 3.9 %shard_map.84 = (bf16[32,2,16,512]{3,2,1,0:T(8,128)(2,1)}, s32[24,512]{1,0:T(8,128)}) custom-call(bf16[64,2,1920]{2,1,0:T(2,128)(2,1)} %bitcast.21, bf16[64,2,1280]{2,1,0:T(2,128)(2,1)} %bitcast.22, bf16[640,1280]{1,0:T(8,128)(2,1)} %weight_ref.1, s32[1,64]{1,0:T(1,128)} %image_hbm.1), custom_call_target="tpu_custom_call" | custom-call | tf_op jit(solution)/shard_map/pallas_call | solution.py:223
  4.6 0.0 copy-start.1
  4.6 17.4 %all-to-all-start = ((bf16[64,16,512]{2,1,0:T(8,128)(2,1)}), bf16[64,16,512]{2,1,0:T(8,128)(2,1)S(1)}, u32[]{:S(2)}, u32[]{:S(2)}) async-start(bf16[64,16,512]{2,1,0:T(8,128)(2,1)} %bitcast.20), calls=%async_computation | async-start | bytes 2097152 | tf_op jit(solution)/shard_map/all_to_all | solution.py:237
  22.0 28.9 %all-to-all-done = bf16[64,16,512]{2,1,0:T(8,128)(2,1)S(1)} async-done(((bf16[64,16,512]{2,1,0:T(8,128)(2,1)}), bf16[64,16,512]{2,1,0:T(8,128)(2,1)S(1)}, u32[]{:S(2)}, u32[]{:S(2)}) %all-to-all-start) | async-done | bytes 1048608 | tf_op jit(solution)/shard_map/all_to_all | solution.py:237
  50.9 0.0 copy-done.1
  50.9 1.8 %shard_map.85 = (bf16[256,320]{1,0:T(8,128)(2,1)S(1)}, f32[1024,256]{1,0:T(8,128)S(1)}, bf16[1024,512]{1,0:T(8,128)(2,1)S(1)}) custom-call(s32[1]{0:T(128)} %bitcast.1.own_ref, s32[24,512]{1,0:T(8,128)S(1)} %copy-done.1, bf16[1024,512]{1,0:T(8,128)(2,1)S(1)} %bitcast.17), custom_call_target="tpu_custom_call" | custom-call | tf_op jit(solution)/shard_map/pallas_call | solution.py:27
  52.7 1.9 %collective-permute-start = (bf16[256,320]{1,0:T(8,128)(2,1)S(1)}, bf16[256,320]{1,0:T(8,128)(2,1)S(1)}, u32[]{:S(2)}, u32[]{:S(2)}) collective-permute-start(bf16[256,320]{1,0:T(8,128)(2,1)S(1)} %get-tuple-element.18.own_ref.att_ref), channel_id=1, source_target_pairs={{0,1},{1,0},{2,3},{3,2},{4,5},{5,4},{6,7},{7,6},{8,9},{9,8},{10,11... | collective-permute-start | bytes 491528 | tf_op jit(solution)/shard_map/ppermute | solution.py:244
  54.6 1.4 %collective-permute-done.other_ref = bf16[256,320]{1,0:T(8,128)(2,1)S(1)} collective-permute-done((bf16[256,320]{1,0:T(8,128)(2,1)S(1)}, bf16[256,320]{1,0:T(8,128)(2,1)S(1)}, u32[]{:S(2)}, u32[]{:S(2)}) %collective-permute-start) | collective-permute-done | bytes 163872 | tf_op jit(solution)/shard_map/ppermute | solution.py:244
  56.0 1.9 %shard_map.86 = bf16[256,1664]{1,0:T(8,128)(2,1)} custom-call(s32[1]{0:T(128)} %bitcast.core_ref, bf16[1024,512]{1,0:T(8,128)(2,1)S(1)} %get-tuple-element.17.sorted_ref, bf16[256,320]{1,0:T(8,128)(2,1)S(1)} %get-tuple-element.18.own_ref.att_ref, bf16[256,320]{1,0:T(8,128)(2,1)S(1)} %collective-permute-done.other_ref), custom_call_target="tpu_custom_call" | custom-call | tf_op jit(solution)/shard_map/pallas_call | solution.py:27
  57.9 5.3 %all-to-all-start.1 = ((bf16[32,8,1664]{2,1,0:T(8,128)(2,1)}), bf16[32,8,1664]{2,1,0:T(8,128)(2,1)}, u32[]{:S(2)}, u32[]{:S(2)}) async-start(bf16[32,8,1664]{2,1,0:T(8,128)(2,1)} %bitcast.6), calls=%async_computation.1 | async-start | bytes 1703936 | tf_op jit(solution)/shard_map/all_to_all | solution.py:248
  63.2 2.9 %shard_map.87 = bf16[512,640]{1,0:T(8,128)(2,1)} custom-call(bf16[1024,512]{1,0:T(8,128)(2,1)S(1)} %get-tuple-element.17.sorted_ref, f32[1024,256]{1,0:T(8,128)S(1)} %get-tuple-element.19.probs_ref, bf16[256,320]{1,0:T(8,128)(2,1)S(1)} %get-tuple-element.18.own_ref.att_ref), custom_call_target="tpu_custom_call" | custom-call | tf_op jit(solution)/shard_map/pallas_call | solution.py:27
  66.1 0.0 copy-start.2
  66.1 0.0 copy-start
  66.1 21.3 %all-to-all-done.1 = bf16[32,8,1664]{2,1,0:T(8,128)(2,1)} async-done(((bf16[32,8,1664]{2,1,0:T(8,128)(2,1)}), bf16[32,8,1664]{2,1,0:T(8,128)(2,1)}, u32[]{:S(2)}, u32[]{:S(2)}) %all-to-all-start.1) | async-done | bytes 852000 | tf_op jit(solution)/shard_map/all_to_all | solution.py:248
  87.4 1.3 reduce_sum.24
  88.7 6.0 %all-to-all-start.2 = ((bf16[64,8,640]{2,1,0:T(8,128)(2,1)}), bf16[64,8,640]{2,1,0:T(8,128)(2,1)S(1)}, u32[]{:S(2)}, u32[]{:S(2)}) async-start(bf16[64,8,640]{2,1,0:T(8,128)(2,1)} %bitcast.7), calls=%async_computation.2 | async-start | bytes 1310720 | tf_op jit(solution)/shard_map/all_to_all | solution.py:261
  94.7 0.0 copy-done.2
  94.7 13.5 %all-gather = bf16[32,1664]{1,0:T(8,128)(2,1)S(1)} all-gather(bf16[8,1664]{1,0:T(8,128)(2,1)S(1)} %reduce_sum.24), channel_id=2, replica_groups={{0,64,128,192},{256,320,384,448},{512,576,640,704},{768,832,896,960},{1..., dimensions={0}, use_global_device_ids=true | all-gather | bytes 133120 | tf_op jit(solution)/shard_map/all_gather | solution.py:254
  108.2 23.0 %all-gather.1 = bf16[32,1664]{1,0:T(8,128)(2,1)S(1)} all-gather(bf16[8,1664]{1,0:T(8,128)(2,1)S(1)} %bitcast_reduce_fusion), channel_id=3, replica_groups={{0,256,512,768},{64,320,576,832},{128,384,640,896},{192,448,704,960},{1..., dimensions={0}, use_global_device_ids=true | all-gather | bytes 133120 | tf_op jit(solution)/shard_map/all_gather | solution.py:256
  131.2 0.7 shard_map.89
  131.9 0.5 slice_bitcast_fusion
  132.4 0.0 all-to-all-done.2
  132.4 0.0 copy-done
  132.4 1.8 %shard_map.88 = (bf16[64,2,1280]{2,1,0:T(2,128)(2,1)}, bf16[64,2,1920]{2,1,0:T(2,128)(2,1)}) custom-call(bf16[512,640]{1,0:T(8,128)(2,1)S(1)} %bitcast.18, s32[24,512]{1,0:T(8,128)S(1)} %copy-done.1, bf16[640,1280]{1,0:T(8,128)(2,1)S(1)} %copy-done, bf16[1,1280]{1,0:T(2,128)(2,1)S(1)} %reshape.31.bias_ref), custom_call_target="tpu_custom_call" | custom-call | tf_op jit(solution)/shard_map/pallas_call | solution.py:27
  (2 shorter events, 0.0 us)
Async XLA Ops:
  4.6 46.3 %copy-start.1 = (s32[24,512]{1,0:T(8,128)S(1)}, s32[24,512]{1,0:T(8,128)}, u32[]{:S(2)}) copy-start(s32[24,512]{1,0:T(8,128)} %get-tuple-element.15.info_ref) | copy-start | bytes 147460
  4.6 46.3 %all-to-all-start = ((bf16[64,16,512]{2,1,0:T(8,128)(2,1)}), bf16[64,16,512]{2,1,0:T(8,128)(2,1)S(1)}, u32[]{:S(2)}, u32[]{:S(2)}) async-start(bf16[64,16,512]{2,1,0:T(8,128)(2,1)} %bitcast.20), calls=%async_computation | async-start | bytes 2097152 | tf_op jit(solution)/shard_map/all_to_all | solution.py:237
  52.7 3.3 %collective-permute-start = (bf16[256,320]{1,0:T(8,128)(2,1)S(1)}, bf16[256,320]{1,0:T(8,128)(2,1)S(1)}, u32[]{:S(2)}, u32[]{:S(2)}) collective-permute-start(bf16[256,320]{1,0:T(8,128)(2,1)S(1)} %get-tuple-element.18.own_ref.att_ref), channel_id=1, source_target_pairs={{0,1},{1,0},{2,3},{3,2},{4,5},{5,4},{6,7},{7,6},{8,9},{9,8},{10,11... | collective-permute-start | bytes 491528 | tf_op jit(solution)/shard_map/ppermute | solution.py:244
  57.9 29.5 %all-to-all-start.1 = ((bf16[32,8,1664]{2,1,0:T(8,128)(2,1)}), bf16[32,8,1664]{2,1,0:T(8,128)(2,1)}, u32[]{:S(2)}, u32[]{:S(2)}) async-start(bf16[32,8,1664]{2,1,0:T(8,128)(2,1)} %bitcast.6), calls=%async_computation.1 | async-start | bytes 1703936 | tf_op jit(solution)/shard_map/all_to_all | solution.py:248
  66.1 28.6 %copy-start.2 = (bf16[1280]{0:T(1024)(128)(2,1)S(1)}, bf16[1280]{0:T(1024)(128)(2,1)}, u32[]{:S(2)}) copy-start(bf16[1280]{0:T(1024)(128)(2,1)} %param.9) | copy-start | bytes 7684
  66.1 66.3 %copy-start = (bf16[640,1280]{1,0:T(8,128)(2,1)S(1)}, bf16[640,1280]{1,0:T(8,128)(2,1)}, u32[]{:S(2)}) copy-start(bf16[640,1280]{1,0:T(8,128)(2,1)} %weight_ref.1) | copy-start | bytes 4915204
  88.7 43.7 %all-to-all-start.2 = ((bf16[64,8,640]{2,1,0:T(8,128)(2,1)}), bf16[64,8,640]{2,1,0:T(8,128)(2,1)S(1)}, u32[]{:S(2)}, u32[]{:S(2)}) async-start(bf16[64,8,640]{2,1,0:T(8,128)(2,1)} %bitcast.7), calls=%async_computation.2 | async-start | bytes 1310720 | tf_op jit(solution)/shard_map/all_to_all | solution.py:261

commit v5 on v4

v5 whole, which is shorter than its diff:
```python
import functools

import jax
import jax.numpy as jnp
from jax import lax
from jax.experimental import pallas as pl
from jax.experimental.pallas import tpu as pltpu
from jax.sharding import PartitionSpec as P

HD = 80
BF = jnp.bfloat16
F32 = jnp.float32
masked_score = -1e30

VM = pl.BlockSpec(memory_space=pltpu.VMEM)
SM = pl.BlockSpec(memory_space=pltpu.SMEM)
HBM = pl.BlockSpec(memory_space=pltpu.HBM)
PARAMS = pltpu.CompilerParams(vmem_limit_bytes=20 * 1024 * 1024)
WHOLE = pltpu.CompilerParams(vmem_limit_bytes=60 * 1024 * 1024)


def dot(a, b, ca=1, cb=0):
    return lax.dot_general(a, b, (((ca,), (cb,)), ((), ())), preferred_element_type=F32)


def call(kernel, outs, specs, *args):
    return pl.pallas_call(
        kernel,
        out_shape=outs,
        in_specs=specs,
        out_specs=jax.tree.map(lambda _: VM, outs),
        compiler_params=PARAMS,
    )(*args)


def arr(shape, dtype):
    return jax.ShapeDtypeStruct(shape, dtype)


def rows_at(row_of, count):
    n = row_of.shape[1]
    return jnp.where(lax.broadcasted_iota(jnp.int32, (count, n), 0) == row_of, 1.0, 0.0).astype(BF)


def slot_rows(shape, dim):
    i = lax.broadcasted_iota(jnp.int32, shape, dim)
    return ((i >> 2) & 1) * 64 + ((i >> 1) & 1) * 32 + (i >> 3) * 2 + (i & 1)


def placement(image_row):
    row = lax.broadcasted_iota(jnp.int32, (64, 64), 0)
    col = lax.broadcasted_iota(jnp.int32, (64, 64), 1)
    image_rows = jnp.broadcast_to(image_row, (64, 64))
    image_col = jnp.sum(jnp.where(row == col, image_rows, 0), axis=1, keepdims=True)
    alike = jnp.where((image_col == image_rows) & (row != col), 1.0, 0.0)
    twin_col = jnp.sum(alike, axis=1, keepdims=True)
    twin_row = jnp.sum(alike, axis=0, keepdims=True)
    rank = jnp.sum(jnp.where((row < col) & (twin_col == twin_row), 1.0, 0.0), axis=0, keepdims=True)
    twins = jnp.sum(twin_row, axis=1, keepdims=True)
    place = rank + jnp.where(twin_row > 0, 0.0, twins)
    lane = lax.broadcasted_iota(jnp.int32, (64, 512), 1)
    block = lax.broadcasted_iota(jnp.int32, (64, 512), 0)
    widen = jnp.where(((lane >> 1) & 63) == block, 1.0, 0.0).astype(BF)
    wide = dot(jnp.broadcast_to(place, (8, 64)).astype(BF), widen).astype(jnp.int32)
    lane = lax.broadcasted_iota(jnp.int32, (8, 512), 1)
    slot_r = (wide & 1) * 2 + (lane & 1) + ((lane >> 7) & 1) * 4
    dst = (wide >> 1) * 8 + slot_r
    back = (wide >> 1) * 16 + ((lane >> 8) & 1) * 8 + slot_r
    return dst, jnp.broadcast_to(twins, (8, 512)).astype(jnp.int32), back


def picked_columns():
    k = lax.broadcasted_iota(jnp.int32, (1, 640), 1)
    eights = ((k >> 3) & 15) * 40 + ((k >> 7) & 1) * 20 + (k >> 8) * 8 + (k & 7)
    fours = ((k >> 2) & 15) * 40 + ((k >> 6) & 1) * 20 + 16 + (k & 3)
    return jnp.where(k < 512, eights, fours)


def by_core(x):
    pick = rows_at(picked_columns(), 640)
    halves = [dot(x[:, :640], pick).astype(BF), dot(x[:, 640:], pick).astype(BF)]
    return [
        jnp.concatenate(
            [h[:, at + t * n:at + (t + 1) * n] for at, n in ((0, 128), (256, 128), (512, 64)) for h in halves], axis=1
        )
        for t in range(2)
    ]


def send_kernel(qkv_hbm, grad_hbm, image_hbm, out_ref, info_ref, qkv_ref, grad_ref, image_ref, sems):
    pairs = ((image_hbm, image_ref), (grad_hbm, grad_ref), (qkv_hbm, qkv_ref))
    copies = [pltpu.make_async_copy(a, b, sems.at[n]) for n, (a, b) in enumerate(pairs)]
    for copy in copies:
        copy.start()
    copies[0].wait()
    dst, twins, back = placement(image_ref[...])
    info_ref[...] = jnp.concatenate([dst, twins, back], axis=0)
    move = rows_at(dst[:1, :256], 256)
    copies[1].wait()
    grads = by_core(grad_ref[...].reshape(128, 1280))
    copies[2].wait()
    qkv = qkv_ref[...].reshape(128, 1920)
    for t in range(2):
        query, key, value = [qkv[:, g * 640 + t * 320:g * 640 + (t + 1) * 320] for g in range(3)]
        first = [grads[t][:, 512:], query, key, jnp.zeros((128, 64), BF)]
        second = [grads[t][:, :512], value]
        stack = jnp.concatenate([jnp.concatenate(first, axis=1), jnp.concatenate(second, axis=1)], axis=0)
        out_ref[:, t] = dot(move, stack).reshape(32, 8, 832).astype(BF)


def head_masks(rows):
    lane = lax.broadcasted_iota(jnp.int32, (rows, 320), 1)
    return [(lane >= h * HD) & (lane < (h + 1) * HD) for h in range(4)]


def by_head(x, masks):
    zero = jnp.zeros_like(x)
    return jnp.concatenate([jnp.where(m, x, zero) for m in masks], axis=0)


def own_head(x, masks):
    total = jnp.zeros((256, 320), F32)
    for h, m in enumerate(masks):
        total = jnp.where(m, x[h * 256:(h + 1) * 256], total)
    return total


def by_kind(got_ref):
    sel = rows_at(slot_rows((1, 128), 1), 128)
    quarters = [dot(sel, got_ref[n * 128:(n + 1) * 128, :]).astype(BF) for n in range(4)]
    first = jnp.concatenate([x[:64] for x in quarters], axis=0)
    second = jnp.concatenate([x[64:] for x in quarters], axis=0)
    grad = jnp.concatenate([second[:, :512], first[:, :128]], axis=1)
    return first[:, 128:448], first[:, 448:768], second[:, 512:], grad


def head_probs(own_ref, info_ref, query, key, masks):
    scores = dot(by_head(query, masks), key, 1, 1) * (HD ** -0.5)
    row = lax.broadcasted_iota(jnp.int32, (256, 256), 0)
    col = lax.broadcasted_iota(jnp.int32, (256, 256), 1)
    twins = info_ref[8:9, :256]
    apart = (((row ^ col) >> 5) & 1) > jnp.where(2 * own_ref[0] < twins, 1, 0)
    heads = []
    for h in range(4):
        own = jnp.where(apart, masked_score, scores[h * 256:(h + 1) * 256])
        exp_scores = jnp.exp(own - jnp.max(own, axis=-1, keepdims=True))
        heads.append(exp_scores / jnp.sum(exp_scores, axis=-1, keepdims=True))
    return jnp.concatenate(heads, axis=0)


def attend_kernel(own_ref, info_ref, got_ref, att_ref, grad_ref):
    query, key, value, grad_ref[...] = by_kind(got_ref)
    masks = head_masks(256)
    probs = head_probs(own_ref, info_ref, query, key, masks)
    att_ref[...] = own_head(dot(probs.astype(BF), value), masks).astype(BF)


def back_kernel(core_ref, own_ref, info_ref, got_ref, att_ref, other_ref, weight_ref, out_ref):
    query, key, value, grad = by_kind(got_ref)
    core = core_ref[0] == 0
    weights = by_core(jnp.where(core, weight_ref[:320, :], weight_ref[320:, :]))
    delta = dot(grad, jnp.where(core, weights[0], weights[1]), 1, 1)
    delta = (delta + dot(other_ref[...], jnp.where(core, weights[1], weights[0]), 1, 1)).astype(BF)
    masks = head_masks(256)
    query_heads, delta_heads = by_head(query, masks), by_head(delta, masks)
    probs = head_probs(own_ref, info_ref, query, key, masks)
    prob_grad = dot(delta_heads, value, 1, 1)
    centre = jnp.sum(probs * prob_grad, axis=-1, keepdims=True)
    score_grad = (probs * (prob_grad - centre) * (HD ** -0.5)).astype(BF)
    query_grad = own_head(dot(score_grad, key), masks).astype(BF)
    key_grad = dot(score_grad, query_heads, 0, 0).astype(BF)
    value_grad = dot(probs.astype(BF), delta_heads, 0, 0).astype(BF)
    first = jnp.concatenate([att_ref[...], query_grad], axis=1)
    second = jnp.concatenate([key_grad, value_grad], axis=1)
    lane = lax.broadcasted_iota(jnp.int32, (128, 128), 1)
    back = jnp.where(lane == slot_rows((128, 1), 0), 1.0, 0.0).astype(BF)
    for n in range(4):
        stack = jnp.concatenate([first[n * 64:(n + 1) * 64], second[n * 64:(n + 1) * 64]], axis=0)
        out_ref[n * 128:(n + 1) * 128, :] = dot(back, stack).astype(BF)


def weight_kernel(core_ref, grad_ref, own_ref, other_ref, out_ref):
    grad = grad_ref[...]
    first = core_ref[0] == 0
    own, other = own_ref[...], other_ref[...]
    att = jnp.concatenate([jnp.where(first, own, other), jnp.where(first, other, own)], axis=1)
    part = dot(grad, att, 0, 0)
    row = lax.broadcasted_iota(jnp.int32, (256, 128), 0)
    col = lax.broadcasted_iota(jnp.int32, (256, 128), 1)
    twice = dot(jnp.where((row >> 1) == col, 1.0, 0.0).astype(BF), part[512:].astype(BF))
    odd = (lax.broadcasted_iota(jnp.int32, (256, 320), 0) & 1) == 1
    rest = jnp.where(odd, twice[:, 320:], twice[:, :320])
    sums = dot(jnp.ones((8, 256), BF), grad)[:1]
    row = lax.broadcasted_iota(jnp.int32, (256, 640), 0)
    col = lax.broadcasted_iota(jnp.int32, (256, 640), 1)
    col_sp = jnp.where(col < 512, (col >> 3) & 31, (col >> 2) & 31)
    own_sums = jnp.where(col_sp == (row >> 3), sums, 0.0).astype(BF)
    k = lax.broadcasted_iota(jnp.int32, (640, 64), 0)
    lane = lax.broadcasted_iota(jnp.int32, (640, 64), 1)
    at = jnp.where(k < 512, (k >> 8) * 8 + (k & 7), 16 + (k & 3))
    bias = dot(own_sums, jnp.where(lane == at, 1.0, 0.0).astype(BF))
    out_ref[...] = jnp.concatenate([part[:256], part[256:512], rest, bias], axis=1).astype(BF)


def total_kernel(scale, got_ref, weight_ref, bias_ref):
    total = got_ref[0].astype(F32)
    for n in range(1, got_ref.shape[0]):
        total = total + got_ref[n].astype(F32)
    total = total * scale
    weight_ref[0:8, :] = total[:, :640]
    weight_ref[8:16, :] = total[:, 640:1280]
    for n in range(4):
        weight_ref[16 + n:17 + n, 0:320] = total[2 * n:2 * n + 1, 1280:1600]
        weight_ref[16 + n:17 + n, 320:640] = total[2 * n + 1:2 * n + 2, 1280:1600]
    bias_ref[...] = total[:1, 1600:]


def home_kernel(got_ref, info_ref, weight_ref, bias_ref, branch_ref, grad_ref):
    rows = dot(rows_at(info_ref[16:17, :], 512), got_ref[...], 0, 0).astype(BF)
    att = jnp.concatenate([rows[:128, :320], rows[256:384, :320]], axis=1)
    branch = dot(att, weight_ref[...]) + bias_ref[...].astype(F32)
    branch_ref[...] = branch.astype(BF).reshape(64, 2, 1280)
    for n, (p, m) in enumerate(((0, 1), (1, 0), (1, 1))):
        both = [rows[(t * 2 + p) * 128:(t * 2 + p + 1) * 128, m * 320:(m + 1) * 320] for t in range(2)]
        grad_ref[:, :, n * 640:(n + 1) * 640] = jnp.concatenate(both, axis=1).reshape(64, 2, 640)


def body(qkv, out_grad, block_image, proj_weight, proj_bias):
    own_sp, own_tp = lax.axis_index("sp"), lax.axis_index("tp")
    dp_count = lax.axis_size("dp")
    outgoing, info = pl.pallas_call(
        send_kernel,
        out_shape=(arr((32, 2, 8, 832), BF), arr((24, 512), jnp.int32)),
        in_specs=[HBM] * 3,
        out_specs=(VM, VM),
        scratch_shapes=[
            pltpu.VMEM((64, 2, 1920), BF),
            pltpu.VMEM((64, 2, 1280), BF),
            pltpu.VMEM((1, 64), jnp.int32),
            pltpu.SemaphoreType.DMA((3,)),
        ],
        compiler_params=WHOLE,
    )(qkv[0], out_grad[0], block_image)
    arrived = lax.all_to_all(
        outgoing.reshape(64, 8, 832), ("sp", "tp"), split_axis=0, concat_axis=0, tiled=True
    ).reshape(512, 832)
    own = own_sp.astype(jnp.int32)[None]
    attended, grads = call(
        attend_kernel,
        (arr((256, 320), BF), arr((256, 640), BF)),
        [SM, VM, VM], own, info, arrived,
    )
    other = lax.ppermute(attended, "tp", [(0, 1), (1, 0)])
    core = own_tp.astype(jnp.int32)[None]
    part = call(weight_kernel, arr((256, 1664), BF), [SM, VM, VM, VM], core, grads, attended, other)
    late_grads, part = lax.optimization_barrier((grads, part))
    other_grads = lax.ppermute(late_grads, "tp", [(0, 1), (1, 0)])
    returning = call(
        back_kernel, arr((512, 640), BF), [SM, SM] + [VM] * 5,
        core, own, info, arrived, attended, other_grads, proj_weight,
    )
    shares = lax.all_to_all(part.reshape(32, 8, 1664), "sp", split_axis=0, concat_axis=0, tiled=True)
    share = jnp.sum(shares.astype(F32), axis=0).astype(BF)
    share, returning = lax.optimization_barrier((share, returning))
    totals = lax.all_gather(share, "dp")
    total, sums = call(
        functools.partial(total_kernel, (dp_count * 8192) ** -0.5),
        (arr((20, 640), F32), arr((1, 64), F32)), [VM], totals,
    )
    returned = lax.all_to_all(
        returning.reshape(64, 8, 640), ("sp", "tp"), split_axis=0, concat_axis=0, tiled=True
    ).reshape(512, 640)
    branch, qkv_grad = call(
        home_kernel, (arr((64, 2, 1280), BF), arr((64, 2, 1920), BF)), [VM] * 4,
        returned, info, proj_weight, proj_bias.reshape(1, 1280),
    )
    return (
        branch[None],
        qkv_grad[None],
        total.T,
        sums[0, :20],
    )


def solution(mesh):
    in_specs = (
        P("dp", None, ("sp", "tp"), None),
        P("dp", None, ("sp", "tp"), None),
        P("dp", None),
        P(),
        P(),
    )
    out_specs = (
        P("dp", None, ("sp", "tp"), None),
        P("dp", None, ("sp", "tp"), None),
        P(None, ("sp", "tp")),
        P(("sp", "tp")),
    )
    return jax.shard_map(body, mesh=mesh, in_specs=in_specs, out_specs=out_specs, check_vma=False)
```

time: 135 us -> 133 us (0.985)
  the two profiles are of different devices: /device:TPU:4 before, /device:TPU:2 now
where the time goes in v5:
time: 133 us; the launch traced here: 132 us
  waiting for transfers between devices  45.3 us (34%)
  blocking collectives  37.9 us (28%)
  starting transfers between devices  32.7 us (25%)
  Pallas kernels  13.8 us (10%)
    all_gather x1, blocking collectives, body(): totals = lax.all_gather(share, 'dp')  37.9 us
    all_to_all x1, waiting for transfers between devices, body(): lax.all_to_all(outgoing.reshape(64, 8, 832), ('sp', 'tp'), split_axis=0,...  26.1 us
    all_to_all x1, starting transfers between devices, body(): lax.all_to_all(outgoing.reshape(64, 8, 832), ('sp', 'tp'), split_axis=0,...  17.4 us
    all_to_all x1, waiting for transfers between devices, body(): lax.all_to_all(part.reshape(32, 8, 1664), 'sp', split_axis=0, concat_axis...  16.2 us
    pallas_call x5, Pallas kernels, call(): pl.pallas_call(kernel, out_shape=outs, in_specs=specs, out_specs=jax.tree...  10.7 us
    all_to_all x1, starting transfers between devices, body(): lax.all_to_all(returning.reshape(64, 8, 640), ('sp', 'tp'), split_axis=0,...  5.98 us
    all_to_all x1, starting transfers between devices, body(): lax.all_to_all(part.reshape(32, 8, 1664), 'sp', split_axis=0, concat_axis...  5.42 us
    pallas_call x1, Pallas kernels, body(): pl.pallas_call(send_kernel, out_shape=(arr((32, 2, 8, 832), BF), arr((24,...  3.14 us
  transfers between devices with their start and end apart: 5, of which 4 were waited for; matrix products, arithmetic and copies ran while one was open for 0% of the time, Pallas kernels for 4%

profile of v5, /device:TPU:2, one launch (start us, length us, event | category | flops | bytes accessed | tf_op | source)
XLA Modules:
  0.0 132.2 jit_solution(10694114123341362575)
XLA Ops:
  0.6 3.1 %shard_map.84 = (bf16[32,2,8,832]{3,2,1,0:T(8,128)(2,1)}, s32[24,512]{1,0:T(8,128)}) custom-call(bf16[64,2,1920]{2,1,0:T(2,128)(2,1)} %bitcast.20, bf16[64,2,1280]{2,1,0:T(2,128)(2,1)} %bitcast.21, s32[1,64]{1,0:T(1,128)} %image_hbm.1), custom_call_target="tpu_custom_call" | custom-call | tf_op jit(solution)/shard_map/pallas_call | solution.py:231
  3.8 0.0 copy-start.1
  3.8 17.4 %all-to-all-start = ((bf16[64,8,832]{2,1,0:T(8,128)(2,1)}), bf16[64,8,832]{2,1,0:T(8,128)(2,1)S(1)}, u32[]{:S(2)}, u32[]{:S(2)}) async-start(bf16[64,8,832]{2,1,0:T(8,128)(2,1)} %bitcast.19), calls=%async_computation | async-start | bytes 1835008 | tf_op jit(solution)/shard_map/all_to_all | solution.py:244
  21.2 26.1 %all-to-all-done = bf16[64,8,832]{2,1,0:T(8,128)(2,1)S(1)} async-done(((bf16[64,8,832]{2,1,0:T(8,128)(2,1)}), bf16[64,8,832]{2,1,0:T(8,128)(2,1)S(1)}, u32[]{:S(2)}, u32[]{:S(2)}) %all-to-all-start) | async-done | bytes 852000 | tf_op jit(solution)/shard_map/all_to_all | solution.py:244
  47.3 0.0 copy-done.1
  47.3 1.8 %shard_map.85 = (bf16[256,320]{1,0:T(8,128)(2,1)S(1)}, bf16[256,640]{1,0:T(8,128)(2,1)S(1)}) custom-call(s32[1]{0:T(128)} %bitcast.own_ref, s32[24,512]{1,0:T(8,128)S(1)} %copy-done.1, bf16[512,832]{1,0:T(8,128)(2,1)S(1)} %bitcast.15), custom_call_target="tpu_custom_call" | custom-call | tf_op jit(solution)/shard_map/pallas_call | solution.py:27
  49.2 1.9 %collective-permute-start = (bf16[256,320]{1,0:T(8,128)(2,1)S(1)}, bf16[256,320]{1,0:T(8,128)(2,1)S(1)}, u32[]{:S(2)}, u32[]{:S(2)}) collective-permute-start(bf16[256,320]{1,0:T(8,128)(2,1)S(1)} %get-tuple-element.19.own_ref.att_ref), channel_id=1, source_target_pairs={{0,1},{1,0},{2,3},{3,2},{4,5},{5,4},{6,7},{7,6},{8,9},{9,8},{10,11... | collective-permute-start | bytes 491528 | tf_op jit(solution)/shard_map/ppermute | solution.py:253
  51.1 1.4 %collective-permute-done.other_ref = bf16[256,320]{1,0:T(8,128)(2,1)S(1)} collective-permute-done((bf16[256,320]{1,0:T(8,128)(2,1)S(1)}, bf16[256,320]{1,0:T(8,128)(2,1)S(1)}, u32[]{:S(2)}, u32[]{:S(2)}) %collective-permute-start) | collective-permute-done | bytes 163872 | tf_op jit(solution)/shard_map/ppermute | solution.py:253
  52.5 0.0 copy-start
  52.5 1.9 %shard_map.86 = bf16[256,1664]{1,0:T(8,128)(2,1)} custom-call(s32[1]{0:T(128)} %bitcast.5.core_ref, bf16[256,640]{1,0:T(8,128)(2,1)S(1)} %get-tuple-element.21.grad_ref, bf16[256,320]{1,0:T(8,128)(2,1)S(1)} %get-tuple-element.19.own_ref.att_ref, bf16[256,320]{1,0:T(8,128)(2,1)S(1)} %collective-permute-done.other_ref), custom_call_target="tpu_custom_call" | custom-call | tf_op jit(solution)/shard_map/pallas_call | solution.py:27
  54.4 5.4 %all-to-all-start.1 = ((bf16[32,8,1664]{2,1,0:T(8,128)(2,1)}), bf16[32,8,1664]{2,1,0:T(8,128)(2,1)}, u32[]{:S(2)}, u32[]{:S(2)}) async-start(bf16[32,8,1664]{2,1,0:T(8,128)(2,1)} %bitcast.6), calls=%async_computation.1 | async-start | bytes 1703936 | tf_op jit(solution)/shard_map/all_to_all | solution.py:262
  59.8 1.9 %collective-permute-start.1 = (bf16[256,640]{1,0:T(8,128)(2,1)S(1)}, bf16[256,640]{1,0:T(8,128)(2,1)S(1)}, u32[]{:S(2)}, u32[]{:S(2)}) collective-permute-start(bf16[256,640]{1,0:T(8,128)(2,1)S(1)} %get-tuple-element.21.grad_ref), channel_id=1, source_target_pairs={{0,1},{1,0},{2,3},{3,2},{4,5},{5,4},{6,7},{7,6},{8,9},{9,8},{10,11... | collective-permute-start | bytes 983048 | tf_op jit(solution)/shard_map/ppermute | solution.py:257
  61.8 1.6 %collective-permute-done.1.other_ref = bf16[256,640]{1,0:T(8,128)(2,1)S(1)} collective-permute-done((bf16[256,640]{1,0:T(8,128)(2,1)S(1)}, bf16[256,640]{1,0:T(8,128)(2,1)S(1)}, u32[]{:S(2)}, u32[]{:S(2)}) %collective-permute-start.1) | collective-permute-done | bytes 327712 | tf_op jit(solution)/shard_map/ppermute | solution.py:257
  63.4 0.0 copy-done
  63.4 4.4 %shard_map.87 = bf16[512,640]{1,0:T(8,128)(2,1)} custom-call(s32[1]{0:T(128)} %bitcast.5.core_ref, s32[1]{0:T(128)} %bitcast.own_ref, s32[24,512]{1,0:T(8,128)S(1)} %copy-done.1, bf16[512,832]{1,0:T(8,128)(2,1)S(1)} %bitcast.16, bf16[256,320]{1,0:T(8,128)(2,1)S(1)} %get-tuple-element.19.own_ref.att_ref, ...), custom_call_target="tpu_custom_call" | custom-call | tf_op jit(solution)/shard_map/pallas_call | solution.py:27
  67.8 0.0 copy-start.2
  67.8 16.2 %all-to-all-done.1 = bf16[32,8,1664]{2,1,0:T(8,128)(2,1)} async-done(((bf16[32,8,1664]{2,1,0:T(8,128)(2,1)}), bf16[32,8,1664]{2,1,0:T(8,128)(2,1)}, u32[]{:S(2)}, u32[]{:S(2)}) %all-to-all-start.1) | async-done | bytes 852000 | tf_op jit(solution)/shard_map/all_to_all | solution.py:262
  84.1 1.3 reduce_sum.12
  85.3 6.0 %all-to-all-start.2 = ((bf16[64,8,640]{2,1,0:T(8,128)(2,1)}), bf16[64,8,640]{2,1,0:T(8,128)(2,1)S(1)}, u32[]{:S(2)}, u32[]{:S(2)}) async-start(bf16[64,8,640]{2,1,0:T(8,128)(2,1)} %bitcast.7), calls=%async_computation.2 | async-start | bytes 1310720 | tf_op jit(solution)/shard_map/all_to_all | solution.py:270
  91.3 0.0 copy-done.2
  91.4 37.9 %all-gather = bf16[128,1664]{1,0:T(8,128)(2,1)S(1)} all-gather(bf16[8,1664]{1,0:T(8,128)(2,1)S(1)} %reduce_sum.12), channel_id=2, replica_groups=mesh['dp'=16,'sp'=32,'tp'=2] {'dp'}, dimensions={0}, use_global_device_ids=true | all-gather | bytes 452608 | tf_op jit(solution)/shard_map/all_gather | solution.py:265
  129.2 0.7 shard_map.89
  129.9 0.5 slice_bitcast_fusion
  130.5 0.0 all-to-all-done.2
  130.5 1.8 %shard_map.88 = (bf16[64,2,1280]{2,1,0:T(2,128)(2,1)}, bf16[64,2,1920]{2,1,0:T(2,128)(2,1)}) custom-call(bf16[512,640]{1,0:T(8,128)(2,1)S(1)} %bitcast.17, s32[24,512]{1,0:T(8,128)S(1)} %copy-done.1, bf16[640,1280]{1,0:T(8,128)(2,1)S(1)} %copy-done, bf16[1,1280]{1,0:T(2,128)(2,1)S(1)} %reshape.31.bias_ref), custom_call_target="tpu_custom_call" | custom-call | tf_op jit(solution)/shard_map/pallas_call | solution.py:27
  (1 shorter events, 0.0 us)
Async XLA Ops:
  3.8 43.5 %copy-start.1 = (s32[24,512]{1,0:T(8,128)S(1)}, s32[24,512]{1,0:T(8,128)}, u32[]{:S(2)}) copy-start(s32[24,512]{1,0:T(8,128)} %get-tuple-element.16.info_ref) | copy-start | bytes 147460
  3.8 43.5 %all-to-all-start = ((bf16[64,8,832]{2,1,0:T(8,128)(2,1)}), bf16[64,8,832]{2,1,0:T(8,128)(2,1)S(1)}, u32[]{:S(2)}, u32[]{:S(2)}) async-start(bf16[64,8,832]{2,1,0:T(8,128)(2,1)} %bitcast.19), calls=%async_computation | async-start | bytes 1835008 | tf_op jit(solution)/shard_map/all_to_all | solution.py:244
  49.2 3.3 %collective-permute-start = (bf16[256,320]{1,0:T(8,128)(2,1)S(1)}, bf16[256,320]{1,0:T(8,128)(2,1)S(1)}, u32[]{:S(2)}, u32[]{:S(2)}) collective-permute-start(bf16[256,320]{1,0:T(8,128)(2,1)S(1)} %get-tuple-element.19.own_ref.att_ref), channel_id=1, source_target_pairs={{0,1},{1,0},{2,3},{3,2},{4,5},{5,4},{6,7},{7,6},{8,9},{9,8},{10,11... | collective-permute-start | bytes 491528 | tf_op jit(solution)/shard_map/ppermute | solution.py:253
  52.5 10.9 %copy-start = (bf16[640,1280]{1,0:T(8,128)(2,1)S(1)}, bf16[640,1280]{1,0:T(8,128)(2,1)}, u32[]{:S(2)}) copy-start(bf16[640,1280]{1,0:T(8,128)(2,1)} %weight_ref.3) | copy-start | bytes 4915204
  54.4 29.6 %all-to-all-start.1 = ((bf16[32,8,1664]{2,1,0:T(8,128)(2,1)}), bf16[32,8,1664]{2,1,0:T(8,128)(2,1)}, u32[]{:S(2)}, u32[]{:S(2)}) async-start(bf16[32,8,1664]{2,1,0:T(8,128)(2,1)} %bitcast.6), calls=%async_computation.1 | async-start | bytes 1703936 | tf_op jit(solution)/shard_map/all_to_all | solution.py:262
  59.8 3.5 %collective-permute-start.1 = (bf16[256,640]{1,0:T(8,128)(2,1)S(1)}, bf16[256,640]{1,0:T(8,128)(2,1)S(1)}, u32[]{:S(2)}, u32[]{:S(2)}) collective-permute-start(bf16[256,640]{1,0:T(8,128)(2,1)S(1)} %get-tuple-element.21.grad_ref), channel_id=1, source_target_pairs={{0,1},{1,0},{2,3},{3,2},{4,5},{5,4},{6,7},{7,6},{8,9},{9,8},{10,11... | collective-permute-start | bytes 983048 | tf_op jit(solution)/shard_map/ppermute | solution.py:257
  67.8 23.5 %copy-start.2 = (bf16[1280]{0:T(1024)(128)(2,1)S(1)}, bf16[1280]{0:T(1024)(128)(2,1)}, u32[]{:S(2)}) copy-start(bf16[1280]{0:T(1024)(128)(2,1)} %param.9) | copy-start | bytes 7684
  85.3 45.1 %all-to-all-start.2 = ((bf16[64,8,640]{2,1,0:T(8,128)(2,1)}), bf16[64,8,640]{2,1,0:T(8,128)(2,1)S(1)}, u32[]{:S(2)}, u32[]{:S(2)}) async-start(bf16[64,8,640]{2,1,0:T(8,128)(2,1)} %bitcast.7), calls=%async_computation.2 | async-start | bytes 1310720 | tf_op jit(solution)/shard_map/all_to_all | solution.py:270

commit v6 on v5

--- a/solution.py
+++ b/solution.py
@@ -144,7 +144,7 @@
     for h in range(4):
         own = jnp.where(apart, masked_score, scores[h * 256:(h + 1) * 256])
         exp_scores = jnp.exp(own - jnp.max(own, axis=-1, keepdims=True))
-        heads.append(exp_scores / jnp.sum(exp_scores, axis=-1, keepdims=True))
+        heads.append(exp_scores * (1.0 / jnp.sum(exp_scores, axis=-1, keepdims=True)))
     return jnp.concatenate(heads, axis=0)
 
 
@@ -179,17 +179,22 @@
         out_ref[n * 128:(n + 1) * 128, :] = dot(back, stack).astype(BF)
 
 
-def weight_kernel(core_ref, grad_ref, own_ref, other_ref, out_ref):
-    grad = grad_ref[...]
+def weight_kernel(core_ref, turned_ref, own_ref, bias_ref, other_ref, out_ref):
     first = core_ref[0] == 0
     own, other = own_ref[...], other_ref[...]
     att = jnp.concatenate([jnp.where(first, own, other), jnp.where(first, other, own)], axis=1)
-    part = dot(grad, att, 0, 0)
-    row = lax.broadcasted_iota(jnp.int32, (256, 128), 0)
-    col = lax.broadcasted_iota(jnp.int32, (256, 128), 1)
-    twice = dot(jnp.where((row >> 1) == col, 1.0, 0.0).astype(BF), part[512:].astype(BF))
+    part = dot(turned_ref[...], att)
     odd = (lax.broadcasted_iota(jnp.int32, (256, 320), 0) & 1) == 1
-    rest = jnp.where(odd, twice[:, 320:], twice[:, :320])
+    rest = jnp.where(odd, part[512:, 320:], part[512:, :320])
+    out_ref[...] = jnp.concatenate([part[:256], part[256:512], rest, bias_ref[...]], axis=1).astype(BF)
+
+
+def turn_kernel(grad_ref, turned_ref, bias_ref):
+    grad = grad_ref[...]
+    row = lax.broadcasted_iota(jnp.int32, (768, 1), 0)
+    row = jnp.where(row < 512, row, 256 + (row >> 1))
+    col = lax.broadcasted_iota(jnp.int32, (768, 640), 1)
+    turned_ref[...] = dot(jnp.where(row == col, 1.0, 0.0).astype(BF), grad, 1, 1).astype(BF)
     sums = dot(jnp.ones((8, 256), BF), grad)[:1]
     row = lax.broadcasted_iota(jnp.int32, (256, 640), 0)
     col = lax.broadcasted_iota(jnp.int32, (256, 640), 1)
@@ -198,8 +203,14 @@
     k = lax.broadcasted_iota(jnp.int32, (640, 64), 0)
     lane = lax.broadcasted_iota(jnp.int32, (640, 64), 1)
     at = jnp.where(k < 512, (k >> 8) * 8 + (k & 7), 16 + (k & 3))
-    bias = dot(own_sums, jnp.where(lane == at, 1.0, 0.0).astype(BF))
-    out_ref[...] = jnp.concatenate([part[:256], part[256:512], rest, bias], axis=1).astype(BF)
+    bias_ref[...] = dot(own_sums, jnp.where(lane == at, 1.0, 0.0).astype(BF))
+
+
+def share_kernel(got_ref, out_ref):
+    total = got_ref[0].astype(F32)
+    for n in range(1, got_ref.shape[0]):
+        total = total + got_ref[n].astype(F32)
+    out_ref[...] = total.astype(BF)
 
 
 def total_kernel(scale, got_ref, weight_ref, bias_ref):
@@ -212,7 +223,7 @@
     for n in range(4):
         weight_ref[16 + n:17 + n, 0:320] = total[2 * n:2 * n + 1, 1280:1600]
         weight_ref[16 + n:17 + n, 320:640] = total[2 * n + 1:2 * n + 2, 1280:1600]
-    bias_ref[...] = total[:1, 1600:]
+    bias_ref[...] = total[:1, 1600:1620]
 
 
 def home_kernel(got_ref, info_ref, weight_ref, bias_ref, branch_ref, grad_ref):
@@ -252,7 +263,8 @@
     )
     other = lax.ppermute(attended, "tp", [(0, 1), (1, 0)])
     core = own_tp.astype(jnp.int32)[None]
-    part = call(weight_kernel, arr((256, 1664), BF), [SM, VM, VM, VM], core, grads, attended, other)
+    turned, sums = call(turn_kernel, (arr((768, 256), BF), arr((256, 64), F32)), [VM], grads)
+    part = call(weight_kernel, arr((256, 1664), BF), [SM] + [VM] * 4, core, turned, attended, sums, other)
     late_grads, part = lax.optimization_barrier((grads, part))
     other_grads = lax.ppermute(late_grads, "tp", [(0, 1), (1, 0)])
     returning = call(
@@ -265,7 +277,7 @@
     totals = lax.all_gather(share, "dp")
     total, sums = call(
         functools.partial(total_kernel, (dp_count * 8192) ** -0.5),
-        (arr((20, 640), F32), arr((1, 64), F32)), [VM], totals,
+        (arr((20, 640), F32), arr((1, 20), F32)), [VM], totals,
     )
     returned = lax.all_to_all(
         returning.reshape(64, 8, 640), ("sp", "tp"), split_axis=0, concat_axis=0, tiled=True
@@ -278,7 +290,7 @@
         branch[None],
         qkv_grad[None],
         total.T,
-        sums[0, :20],
+        sums.reshape(20),
     )
 
 

time: 133 us -> 132 us (level)
    pallas_call x5 -> x6, Pallas kernels: 10.7 us -> 11 us  [call(): pl.pallas_call(kernel, out_shape=outs, in_specs=specs, out_specs=jax.tree...]
where the time goes in v6:
time: 132 us; the launch traced here: 131 us
  waiting for transfers between devices  44.6 us (34%)
  blocking collectives  37.9 us (29%)
  starting transfers between devices  32.6 us (25%)
  Pallas kernels  14.1 us (11%)
    all_gather x1, blocking collectives, body(): totals = lax.all_gather(share, 'dp')  37.9 us
    all_to_all x1, waiting for transfers between devices, body(): lax.all_to_all(outgoing.reshape(64, 8, 832), ('sp', 'tp'), split_axis=0,...  26.1 us
    all_to_all x1, starting transfers between devices, body(): lax.all_to_all(outgoing.reshape(64, 8, 832), ('sp', 'tp'), split_axis=0,...  17.4 us
    all_to_all x1, waiting for transfers between devices, body(): lax.all_to_all(part.reshape(32, 8, 1664), 'sp', split_axis=0, concat_axis...  16.2 us
    pallas_call x6, Pallas kernels, call(): pl.pallas_call(kernel, out_shape=outs, in_specs=specs, out_specs=jax.tree...  11 us
    all_to_all x1, starting transfers between devices, body(): lax.all_to_all(returning.reshape(64, 8, 640), ('sp', 'tp'), split_axis=0,...  5.98 us
    all_to_all x1, starting transfers between devices, body(): lax.all_to_all(part.reshape(32, 8, 1664), 'sp', split_axis=0, concat_axis...  5.41 us
    pallas_call x1, Pallas kernels, body(): pl.pallas_call(send_kernel, out_shape=(arr((32, 2, 8, 832), BF), arr((24,...  3.14 us
  transfers between devices with their start and end apart: 5, of which 4 were waited for; matrix products, arithmetic and copies ran while one was open for 0% of the time, Pallas kernels for 4%

profile of v6, /device:TPU:2, one launch (start us, length us, event | category | flops | bytes accessed | tf_op | source)
XLA Modules:
  0.0 131.4 jit_solution(11495446255658845707)
XLA Ops:
  0.6 3.1 %shard_map.84 = (bf16[32,2,8,832]{3,2,1,0:T(8,128)(2,1)}, s32[24,512]{1,0:T(8,128)}) custom-call(bf16[64,2,1920]{2,1,0:T(2,128)(2,1)} %bitcast.19, bf16[64,2,1280]{2,1,0:T(2,128)(2,1)} %bitcast.20, s32[1,64]{1,0:T(1,128)} %image_hbm.1), custom_call_target="tpu_custom_call" | custom-call | tf_op jit(solution)/shard_map/pallas_call | solution.py:242
  3.8 0.0 copy-start.1
  3.8 17.4 %all-to-all-start = ((bf16[64,8,832]{2,1,0:T(8,128)(2,1)}), bf16[64,8,832]{2,1,0:T(8,128)(2,1)S(1)}, u32[]{:S(2)}, u32[]{:S(2)}) async-start(bf16[64,8,832]{2,1,0:T(8,128)(2,1)} %bitcast.18), calls=%async_computation | async-start | bytes 1835008 | tf_op jit(solution)/shard_map/all_to_all | solution.py:255
  21.2 26.1 %all-to-all-done = bf16[64,8,832]{2,1,0:T(8,128)(2,1)S(1)} async-done(((bf16[64,8,832]{2,1,0:T(8,128)(2,1)}), bf16[64,8,832]{2,1,0:T(8,128)(2,1)S(1)}, u32[]{:S(2)}, u32[]{:S(2)}) %all-to-all-start) | async-done | bytes 852000 | tf_op jit(solution)/shard_map/all_to_all | solution.py:255
  47.3 0.0 copy-done.1
  47.3 1.8 %shard_map.85 = (bf16[256,320]{1,0:T(8,128)(2,1)S(1)}, bf16[256,640]{1,0:T(8,128)(2,1)S(1)}) custom-call(s32[1]{0:T(128)} %bitcast.own_ref, s32[24,512]{1,0:T(8,128)S(1)} %copy-done.1, bf16[512,832]{1,0:T(8,128)(2,1)S(1)} %bitcast.14), custom_call_target="tpu_custom_call" | custom-call | tf_op jit(solution)/shard_map/pallas_call | solution.py:27
  49.2 1.9 %collective-permute-start = (bf16[256,320]{1,0:T(8,128)(2,1)S(1)}, bf16[256,320]{1,0:T(8,128)(2,1)S(1)}, u32[]{:S(2)}, u32[]{:S(2)}) collective-permute-start(bf16[256,320]{1,0:T(8,128)(2,1)S(1)} %get-tuple-element.22.own_ref.att_ref), channel_id=1, source_target_pairs={{0,1},{1,0},{2,3},{3,2},{4,5},{5,4},{6,7},{7,6},{8,9},{9,8},{10,11... | collective-permute-start | bytes 491528 | tf_op jit(solution)/shard_map/ppermute | solution.py:264
  51.1 0.7 shard_map.86
  51.7 0.8 collective-permute-done.other_ref
  52.5 0.0 copy-start
  52.5 1.6 %shard_map.87 = bf16[256,1664]{1,0:T(8,128)(2,1)} custom-call(s32[1]{0:T(128)} %bitcast.5.core_ref, bf16[768,256]{1,0:T(8,128)(2,1)S(1)} %get-tuple-element.21.turned_ref, bf16[256,320]{1,0:T(8,128)(2,1)S(1)} %get-tuple-element.22.own_ref.att_ref, f32[256,64]{1,0:T(8,128)S(1)} %get-tuple-element.23.bias_ref, bf16[256,320]{1,0:T(8,128)(2,1)S(1)} %collective-permute-done.other_ref), custom_call_target="tpu_custom_call" | custom-call | tf_op jit(solution)/shard_map/pallas_call | solution.py:27
  54.1 5.4 %all-to-all-start.1 = ((bf16[32,8,1664]{2,1,0:T(8,128)(2,1)}), bf16[32,8,1664]{2,1,0:T(8,128)(2,1)}, u32[]{:S(2)}, u32[]{:S(2)}) async-start(bf16[32,8,1664]{2,1,0:T(8,128)(2,1)} %bitcast.6), calls=%async_computation.1 | async-start | bytes 1703936 | tf_op jit(solution)/shard_map/all_to_all | solution.py:274
  59.5 1.9 %collective-permute-start.1 = (bf16[256,640]{1,0:T(8,128)(2,1)S(1)}, bf16[256,640]{1,0:T(8,128)(2,1)S(1)}, u32[]{:S(2)}, u32[]{:S(2)}) collective-permute-start(bf16[256,640]{1,0:T(8,128)(2,1)S(1)} %get-tuple-element.25.grad_ref), channel_id=1, source_target_pairs={{0,1},{1,0},{2,3},{3,2},{4,5},{5,4},{6,7},{7,6},{8,9},{9,8},{10,11... | collective-permute-start | bytes 983048 | tf_op jit(solution)/shard_map/ppermute | solution.py:269
  61.4 1.6 %collective-permute-done.1.other_ref = bf16[256,640]{1,0:T(8,128)(2,1)S(1)} collective-permute-done((bf16[256,640]{1,0:T(8,128)(2,1)S(1)}, bf16[256,640]{1,0:T(8,128)(2,1)S(1)}, u32[]{:S(2)}, u32[]{:S(2)}) %collective-permute-start.1) | collective-permute-done | bytes 327712 | tf_op jit(solution)/shard_map/ppermute | solution.py:269
  63.0 0.0 copy-done
  63.0 4.5 %shard_map.88 = bf16[512,640]{1,0:T(8,128)(2,1)} custom-call(s32[1]{0:T(128)} %bitcast.5.core_ref, s32[1]{0:T(128)} %bitcast.own_ref, s32[24,512]{1,0:T(8,128)S(1)} %copy-done.1, bf16[512,832]{1,0:T(8,128)(2,1)S(1)} %bitcast.15, bf16[256,320]{1,0:T(8,128)(2,1)S(1)} %get-tuple-element.22.own_ref.att_ref, ...), custom_call_target="tpu_custom_call" | custom-call | tf_op jit(solution)/shard_map/pallas_call | solution.py:27
  67.5 0.0 copy-start.2
  67.5 16.2 %all-to-all-done.1 = bf16[32,8,1664]{2,1,0:T(8,128)(2,1)} async-done(((bf16[32,8,1664]{2,1,0:T(8,128)(2,1)}), bf16[32,8,1664]{2,1,0:T(8,128)(2,1)}, u32[]{:S(2)}, u32[]{:S(2)}) %all-to-all-start.1) | async-done | bytes 852000 | tf_op jit(solution)/shard_map/all_to_all | solution.py:274
  83.7 1.3 reduce_sum.12
  85.0 6.0 %all-to-all-start.2 = ((bf16[64,8,640]{2,1,0:T(8,128)(2,1)}), bf16[64,8,640]{2,1,0:T(8,128)(2,1)S(1)}, u32[]{:S(2)}, u32[]{:S(2)}) async-start(bf16[64,8,640]{2,1,0:T(8,128)(2,1)} %bitcast.7), calls=%async_computation.2 | async-start | bytes 1310720 | tf_op jit(solution)/shard_map/all_to_all | solution.py:282
  91.0 0.0 copy-done.2
  91.0 37.9 %all-gather = bf16[128,1664]{1,0:T(8,128)(2,1)S(1)} all-gather(bf16[8,1664]{1,0:T(8,128)(2,1)S(1)} %reduce_sum.12), channel_id=2, replica_groups=mesh['dp'=16,'sp'=32,'tp'=2] {'dp'}, dimensions={0}, use_global_device_ids=true | all-gather | bytes 452608 | tf_op jit(solution)/shard_map/all_gather | solution.py:277
  128.9 0.7 shard_map.90
  129.6 0.0 all-to-all-done.2
  129.6 1.8 %shard_map.89 = (bf16[64,2,1280]{2,1,0:T(2,128)(2,1)}, bf16[64,2,1920]{2,1,0:T(2,128)(2,1)}) custom-call(bf16[512,640]{1,0:T(8,128)(2,1)S(1)} %bitcast.16, s32[24,512]{1,0:T(8,128)S(1)} %copy-done.1, bf16[640,1280]{1,0:T(8,128)(2,1)S(1)} %copy-done, bf16[1,1280]{1,0:T(2,128)(2,1)S(1)} %reshape.34.bias_ref), custom_call_target="tpu_custom_call" | custom-call | tf_op jit(solution)/shard_map/pallas_call | solution.py:27
  (1 shorter events, 0.0 us)
Async XLA Ops:
  3.8 43.5 %copy-start.1 = (s32[24,512]{1,0:T(8,128)S(1)}, s32[24,512]{1,0:T(8,128)}, u32[]{:S(2)}) copy-start(s32[24,512]{1,0:T(8,128)} %get-tuple-element.18.info_ref) | copy-start | bytes 147460
  3.8 43.5 %all-to-all-start = ((bf16[64,8,832]{2,1,0:T(8,128)(2,1)}), bf16[64,8,832]{2,1,0:T(8,128)(2,1)S(1)}, u32[]{:S(2)}, u32[]{:S(2)}) async-start(bf16[64,8,832]{2,1,0:T(8,128)(2,1)} %bitcast.18), calls=%async_computation | async-start | bytes 1835008 | tf_op jit(solution)/shard_map/all_to_all | solution.py:255
  49.2 3.3 %collective-permute-start = (bf16[256,320]{1,0:T(8,128)(2,1)S(1)}, bf16[256,320]{1,0:T(8,128)(2,1)S(1)}, u32[]{:S(2)}, u32[]{:S(2)}) collective-permute-start(bf16[256,320]{1,0:T(8,128)(2,1)S(1)} %get-tuple-element.22.own_ref.att_ref), channel_id=1, source_target_pairs={{0,1},{1,0},{2,3},{3,2},{4,5},{5,4},{6,7},{7,6},{8,9},{9,8},{10,11... | collective-permute-start | bytes 491528 | tf_op jit(solution)/shard_map/ppermute | solution.py:264
  52.5 10.5 %copy-start = (bf16[640,1280]{1,0:T(8,128)(2,1)S(1)}, bf16[640,1280]{1,0:T(8,128)(2,1)}, u32[]{:S(2)}) copy-start(bf16[640,1280]{1,0:T(8,128)(2,1)} %weight_ref.3) | copy-start | bytes 4915204
  54.1 29.6 %all-to-all-start.1 = ((bf16[32,8,1664]{2,1,0:T(8,128)(2,1)}), bf16[32,8,1664]{2,1,0:T(8,128)(2,1)}, u32[]{:S(2)}, u32[]{:S(2)}) async-start(bf16[32,8,1664]{2,1,0:T(8,128)(2,1)} %bitcast.6), calls=%async_computation.1 | async-start | bytes 1703936 | tf_op jit(solution)/shard_map/all_to_all | solution.py:274
  59.5 3.5 %collective-permute-start.1 = (bf16[256,640]{1,0:T(8,128)(2,1)S(1)}, bf16[256,640]{1,0:T(8,128)(2,1)S(1)}, u32[]{:S(2)}, u32[]{:S(2)}) collective-permute-start(bf16[256,640]{1,0:T(8,128)(2,1)S(1)} %get-tuple-element.25.grad_ref), channel_id=1, source_target_pairs={{0,1},{1,0},{2,3},{3,2},{4,5},{5,4},{6,7},{7,6},{8,9},{9,8},{10,11... | collective-permute-start | bytes 983048 | tf_op jit(solution)/shard_map/ppermute | solution.py:269
  67.5 23.5 %copy-start.2 = (bf16[1280]{0:T(1024)(128)(2,1)S(1)}, bf16[1280]{0:T(1024)(128)(2,1)}, u32[]{:S(2)}) copy-start(bf16[1280]{0:T(1024)(128)(2,1)} %param.9) | copy-start | bytes 7684
  85.0 44.6 %all-to-all-start.2 = ((bf16[64,8,640]{2,1,0:T(8,128)(2,1)}), bf16[64,8,640]{2,1,0:T(8,128)(2,1)S(1)}, u32[]{:S(2)}, u32[]{:S(2)}) async-start(bf16[64,8,640]{2,1,0:T(8,128)(2,1)} %bitcast.7), calls=%async_computation.2 | async-start | bytes 1310720 | tf_op jit(solution)/shard_map/all_to_all | solution.py:282

commit v7 on v6

--- a/solution.py
+++ b/solution.py
@@ -213,20 +213,17 @@
     out_ref[...] = total.astype(BF)
 
 
-def total_kernel(scale, got_ref, weight_ref, bias_ref):
-    total = got_ref[0].astype(F32)
-    for n in range(1, got_ref.shape[0]):
-        total = total + got_ref[n].astype(F32)
+def home_kernel(scale, share_ref, got_ref, info_ref, weight_ref, bias_ref, branch_ref, grad_ref, total_ref, sums_ref):
+    total = share_ref[0].astype(F32)
+    for n in range(1, share_ref.shape[0]):
+        total = total + share_ref[n].astype(F32)
     total = total * scale
-    weight_ref[0:8, :] = total[:, :640]
-    weight_ref[8:16, :] = total[:, 640:1280]
+    total_ref[0:8, :] = total[:, :640]
+    total_ref[8:16, :] = total[:, 640:1280]
     for n in range(4):
-        weight_ref[16 + n:17 + n, 0:320] = total[2 * n:2 * n + 1, 1280:1600]
-        weight_ref[16 + n:17 + n, 320:640] = total[2 * n + 1:2 * n + 2, 1280:1600]
-    bias_ref[...] = total[:1, 1600:1620]
-
-
-def home_kernel(got_ref, info_ref, weight_ref, bias_ref, branch_ref, grad_ref):
+        total_ref[16 + n:17 + n, 0:320] = total[2 * n:2 * n + 1, 1280:1600]
+        total_ref[16 + n:17 + n, 320:640] = total[2 * n + 1:2 * n + 2, 1280:1600]
+    sums_ref[...] = total[:1, 1600:1620]
     rows = dot(rows_at(info_ref[16:17, :], 512), got_ref[...], 0, 0).astype(BF)
     att = jnp.concatenate([rows[:128, :320], rows[256:384, :320]], axis=1)
     branch = dot(att, weight_ref[...]) + bias_ref[...].astype(F32)
@@ -275,16 +272,13 @@
     share = jnp.sum(shares.astype(F32), axis=0).astype(BF)
     share, returning = lax.optimization_barrier((share, returning))
     totals = lax.all_gather(share, "dp")
-    total, sums = call(
-        functools.partial(total_kernel, (dp_count * 8192) ** -0.5),
-        (arr((20, 640), F32), arr((1, 20), F32)), [VM], totals,
-    )
     returned = lax.all_to_all(
         returning.reshape(64, 8, 640), ("sp", "tp"), split_axis=0, concat_axis=0, tiled=True
     ).reshape(512, 640)
-    branch, qkv_grad = call(
-        home_kernel, (arr((64, 2, 1280), BF), arr((64, 2, 1920), BF)), [VM] * 4,
-        returned, info, proj_weight, proj_bias.reshape(1, 1280),
+    branch, qkv_grad, total, sums = call(
+        functools.partial(home_kernel, (dp_count * 8192) ** -0.5),
+        (arr((64, 2, 1280), BF), arr((64, 2, 1920), BF), arr((20, 640), F32), arr((1, 20), F32)), [VM] * 5,
+        totals, returned, info, proj_weight, proj_bias.reshape(1, 1280),
     )
     return (
         branch[None],

time: 132 us -> 131 us (level)
    pallas_call x6 -> x5, Pallas kernels: 11 us -> 10.3 us  [call(): pl.pallas_call(kernel, out_shape=outs, in_specs=specs, out_specs=jax.tree...]
where the time goes in v7:
time: 131 us
  waiting for transfers between devices  44.7 us (34%)
  blocking collectives  37.9 us (29%)
  starting transfers between devices  32.7 us (25%)
  Pallas kernels  13.4 us (10%)
    all_gather x1, blocking collectives, body(): totals = lax.all_gather(share, 'dp')  37.9 us
    all_to_all x1, waiting for transfers between devices, body(): lax.all_to_all(outgoing.reshape(64, 8, 832), ('sp', 'tp'), split_axis=0,...  26.1 us
    all_to_all x1, starting transfers between devices, body(): lax.all_to_all(outgoing.reshape(64, 8, 832), ('sp', 'tp'), split_axis=0,...  17.4 us
    all_to_all x1, waiting for transfers between devices, body(): lax.all_to_all(part.reshape(32, 8, 1664), 'sp', split_axis=0, concat_axis...  16.2 us
    pallas_call x5, Pallas kernels, call(): pl.pallas_call(kernel, out_shape=outs, in_specs=specs, out_specs=jax.tree...  10.3 us
    all_to_all x1, starting transfers between devices, body(): lax.all_to_all(returning.reshape(64, 8, 640), ('sp', 'tp'), split_axis=0,...  5.98 us
    all_to_all x1, starting transfers between devices, body(): lax.all_to_all(part.reshape(32, 8, 1664), 'sp', split_axis=0, concat_axis...  5.42 us
    pallas_call x1, Pallas kernels, body(): pl.pallas_call(send_kernel, out_shape=(arr((32, 2, 8, 832), BF), arr((24,...  3.14 us
  transfers between devices with their start and end apart: 5, of which 4 were waited for; matrix products, arithmetic and copies ran while one was open for 0% of the time, Pallas kernels for 4%

profile of v7, /device:TPU:2, one launch (start us, length us, event | category | flops | bytes accessed | tf_op | source)
XLA Modules:
  0.0 130.7 jit_solution(14565368572931174751)
XLA Ops:
  0.6 3.1 %shard_map.84 = (bf16[32,2,8,832]{3,2,1,0:T(8,128)(2,1)}, s32[24,512]{1,0:T(8,128)}) custom-call(bf16[64,2,1920]{2,1,0:T(2,128)(2,1)} %bitcast.19, bf16[64,2,1280]{2,1,0:T(2,128)(2,1)} %bitcast.20, s32[1,64]{1,0:T(1,128)} %image_hbm.1), custom_call_target="tpu_custom_call" | custom-call | tf_op jit(solution)/shard_map/pallas_call | solution.py:239
  3.8 0.0 copy-start.1
  3.8 17.4 %all-to-all-start = ((bf16[64,8,832]{2,1,0:T(8,128)(2,1)}), bf16[64,8,832]{2,1,0:T(8,128)(2,1)S(1)}, u32[]{:S(2)}, u32[]{:S(2)}) async-start(bf16[64,8,832]{2,1,0:T(8,128)(2,1)} %bitcast.18), calls=%async_computation | async-start | bytes 1835008 | tf_op jit(solution)/shard_map/all_to_all | solution.py:252
  21.2 26.1 %all-to-all-done = bf16[64,8,832]{2,1,0:T(8,128)(2,1)S(1)} async-done(((bf16[64,8,832]{2,1,0:T(8,128)(2,1)}), bf16[64,8,832]{2,1,0:T(8,128)(2,1)S(1)}, u32[]{:S(2)}, u32[]{:S(2)}) %all-to-all-start) | async-done | bytes 852000 | tf_op jit(solution)/shard_map/all_to_all | solution.py:252
  47.3 0.0 copy-done.1
  47.3 1.8 %shard_map.85 = (bf16[256,320]{1,0:T(8,128)(2,1)S(1)}, bf16[256,640]{1,0:T(8,128)(2,1)S(1)}) custom-call(s32[1]{0:T(128)} %bitcast.own_ref, s32[24,512]{1,0:T(8,128)S(1)} %copy-done.1, bf16[512,832]{1,0:T(8,128)(2,1)S(1)} %bitcast.14), custom_call_target="tpu_custom_call" | custom-call | tf_op jit(solution)/shard_map/pallas_call | solution.py:27
  49.2 1.9 %collective-permute-start = (bf16[256,320]{1,0:T(8,128)(2,1)S(1)}, bf16[256,320]{1,0:T(8,128)(2,1)S(1)}, u32[]{:S(2)}, u32[]{:S(2)}) collective-permute-start(bf16[256,320]{1,0:T(8,128)(2,1)S(1)} %get-tuple-element.22.own_ref.att_ref), channel_id=1, source_target_pairs={{0,1},{1,0},{2,3},{3,2},{4,5},{5,4},{6,7},{7,6},{8,9},{9,8},{10,11... | collective-permute-start | bytes 491528 | tf_op jit(solution)/shard_map/ppermute | solution.py:261
  51.1 0.6 shard_map.86
  51.8 0.8 collective-permute-done.other_ref
  52.5 0.0 copy-start
  52.5 1.6 %shard_map.87 = bf16[256,1664]{1,0:T(8,128)(2,1)} custom-call(s32[1]{0:T(128)} %bitcast.5.core_ref, bf16[768,256]{1,0:T(8,128)(2,1)S(1)} %get-tuple-element.21.turned_ref, bf16[256,320]{1,0:T(8,128)(2,1)S(1)} %get-tuple-element.22.own_ref.att_ref, f32[256,64]{1,0:T(8,128)S(1)} %get-tuple-element.23.bias_ref, bf16[256,320]{1,0:T(8,128)(2,1)S(1)} %collective-permute-done.other_ref), custom_call_target="tpu_custom_call" | custom-call | tf_op jit(solution)/shard_map/pallas_call | solution.py:27
  54.1 5.4 %all-to-all-start.1 = ((bf16[32,8,1664]{2,1,0:T(8,128)(2,1)}), bf16[32,8,1664]{2,1,0:T(8,128)(2,1)}, u32[]{:S(2)}, u32[]{:S(2)}) async-start(bf16[32,8,1664]{2,1,0:T(8,128)(2,1)} %bitcast.6), calls=%async_computation.1 | async-start | bytes 1703936 | tf_op jit(solution)/shard_map/all_to_all | solution.py:271
  59.5 1.9 %collective-permute-start.1 = (bf16[256,640]{1,0:T(8,128)(2,1)S(1)}, bf16[256,640]{1,0:T(8,128)(2,1)S(1)}, u32[]{:S(2)}, u32[]{:S(2)}) collective-permute-start(bf16[256,640]{1,0:T(8,128)(2,1)S(1)} %get-tuple-element.25.grad_ref), channel_id=1, source_target_pairs={{0,1},{1,0},{2,3},{3,2},{4,5},{5,4},{6,7},{7,6},{8,9},{9,8},{10,11... | collective-permute-start | bytes 983048 | tf_op jit(solution)/shard_map/ppermute | solution.py:266
  61.4 1.6 %collective-permute-done.1.other_ref = bf16[256,640]{1,0:T(8,128)(2,1)S(1)} collective-permute-done((bf16[256,640]{1,0:T(8,128)(2,1)S(1)}, bf16[256,640]{1,0:T(8,128)(2,1)S(1)}, u32[]{:S(2)}, u32[]{:S(2)}) %collective-permute-start.1) | collective-permute-done | bytes 327712 | tf_op jit(solution)/shard_map/ppermute | solution.py:266
  63.0 0.0 copy-done
  63.0 4.4 %shard_map.88 = bf16[512,640]{1,0:T(8,128)(2,1)} custom-call(s32[1]{0:T(128)} %bitcast.5.core_ref, s32[1]{0:T(128)} %bitcast.own_ref, s32[24,512]{1,0:T(8,128)S(1)} %copy-done.1, bf16[512,832]{1,0:T(8,128)(2,1)S(1)} %bitcast.15, bf16[256,320]{1,0:T(8,128)(2,1)S(1)} %get-tuple-element.22.own_ref.att_ref, ...), custom_call_target="tpu_custom_call" | custom-call | tf_op jit(solution)/shard_map/pallas_call | solution.py:27
  67.5 0.0 copy-start.2
  67.5 16.2 %all-to-all-done.1 = bf16[32,8,1664]{2,1,0:T(8,128)(2,1)} async-done(((bf16[32,8,1664]{2,1,0:T(8,128)(2,1)}), bf16[32,8,1664]{2,1,0:T(8,128)(2,1)}, u32[]{:S(2)}, u32[]{:S(2)}) %all-to-all-start.1) | async-done | bytes 852000 | tf_op jit(solution)/shard_map/all_to_all | solution.py:271
  83.7 1.3 reduce_sum.12
  85.0 6.0 %all-to-all-start.2 = ((bf16[64,8,640]{2,1,0:T(8,128)(2,1)}), bf16[64,8,640]{2,1,0:T(8,128)(2,1)S(1)}, u32[]{:S(2)}, u32[]{:S(2)}) async-start(bf16[64,8,640]{2,1,0:T(8,128)(2,1)} %bitcast.8), calls=%async_computation.2 | async-start | bytes 1310720 | tf_op jit(solution)/shard_map/all_to_all | solution.py:275
  91.0 0.0 copy-done.2
  91.0 37.9 %all-gather = bf16[128,1664]{1,0:T(8,128)(2,1)S(1)} all-gather(bf16[8,1664]{1,0:T(8,128)(2,1)S(1)} %reduce_sum.12), channel_id=2, replica_groups=mesh['dp'=16,'sp'=32,'tp'=2] {'dp'}, dimensions={0}, use_global_device_ids=true | all-gather | bytes 452608 | tf_op jit(solution)/shard_map/all_gather | solution.py:274
  128.9 0.0 all-to-all-done.2
  128.9 1.8 %shard_map.89 = (bf16[64,2,1280]{2,1,0:T(2,128)(2,1)}, bf16[64,2,1920]{2,1,0:T(2,128)(2,1)}, f32[20,640]{1,0:T(8,128)}, f32[1,20]{1,0:T(1,128)}) custom-call(bf16[16,8,1664]{2,1,0:T(8,128)(2,1)S(1)} %bitcast.17, bf16[512,640]{1,0:T(8,128)(2,1)S(1)} %bitcast.16, s32[24,512]{1,0:T(8,128)S(1)} %copy-done.1, bf16[640,1280]{1,0:T(8,128)(2,1)S(1)} %copy-done, ...), custom_call_target="tpu_custom_call" | custom-call | tf_op jit(solution)/shard_map/pallas_call | solution.py:27
  (1 shorter events, 0.0 us)
Async XLA Ops:
  3.8 43.5 %copy-start.1 = (s32[24,512]{1,0:T(8,128)S(1)}, s32[24,512]{1,0:T(8,128)}, u32[]{:S(2)}) copy-start(s32[24,512]{1,0:T(8,128)} %get-tuple-element.18.info_ref) | copy-start | bytes 147460
  3.8 43.5 %all-to-all-start = ((bf16[64,8,832]{2,1,0:T(8,128)(2,1)}), bf16[64,8,832]{2,1,0:T(8,128)(2,1)S(1)}, u32[]{:S(2)}, u32[]{:S(2)}) async-start(bf16[64,8,832]{2,1,0:T(8,128)(2,1)} %bitcast.18), calls=%async_computation | async-start | bytes 1835008 | tf_op jit(solution)/shard_map/all_to_all | solution.py:252
  49.2 3.3 %collective-permute-start = (bf16[256,320]{1,0:T(8,128)(2,1)S(1)}, bf16[256,320]{1,0:T(8,128)(2,1)S(1)}, u32[]{:S(2)}, u32[]{:S(2)}) collective-permute-start(bf16[256,320]{1,0:T(8,128)(2,1)S(1)} %get-tuple-element.22.own_ref.att_ref), channel_id=1, source_target_pairs={{0,1},{1,0},{2,3},{3,2},{4,5},{5,4},{6,7},{7,6},{8,9},{9,8},{10,11... | collective-permute-start | bytes 491528 | tf_op jit(solution)/shard_map/ppermute | solution.py:261
  52.5 10.5 %copy-start = (bf16[640,1280]{1,0:T(8,128)(2,1)S(1)}, bf16[640,1280]{1,0:T(8,128)(2,1)}, u32[]{:S(2)}) copy-start(bf16[640,1280]{1,0:T(8,128)(2,1)} %weight_ref.3) | copy-start | bytes 4915204
  54.1 29.6 %all-to-all-start.1 = ((bf16[32,8,1664]{2,1,0:T(8,128)(2,1)}), bf16[32,8,1664]{2,1,0:T(8,128)(2,1)}, u32[]{:S(2)}, u32[]{:S(2)}) async-start(bf16[32,8,1664]{2,1,0:T(8,128)(2,1)} %bitcast.6), calls=%async_computation.1 | async-start | bytes 1703936 | tf_op jit(solution)/shard_map/all_to_all | solution.py:271
  59.5 3.5 %collective-permute-start.1 = (bf16[256,640]{1,0:T(8,128)(2,1)S(1)}, bf16[256,640]{1,0:T(8,128)(2,1)S(1)}, u32[]{:S(2)}, u32[]{:S(2)}) collective-permute-start(bf16[256,640]{1,0:T(8,128)(2,1)S(1)} %get-tuple-element.25.grad_ref), channel_id=1, source_target_pairs={{0,1},{1,0},{2,3},{3,2},{4,5},{5,4},{6,7},{7,6},{8,9},{9,8},{10,11... | collective-permute-start | bytes 983048 | tf_op jit(solution)/shard_map/ppermute | solution.py:266
  67.5 23.5 %copy-start.2 = (bf16[1280]{0:T(1024)(128)(2,1)S(1)}, bf16[1280]{0:T(1024)(128)(2,1)}, u32[]{:S(2)}) copy-start(bf16[1280]{0:T(1024)(128)(2,1)} %param.9) | copy-start | bytes 7684
  85.0 43.9 %all-to-all-start.2 = ((bf16[64,8,640]{2,1,0:T(8,128)(2,1)}), bf16[64,8,640]{2,1,0:T(8,128)(2,1)S(1)}, u32[]{:S(2)}, u32[]{:S(2)}) async-start(bf16[64,8,640]{2,1,0:T(8,128)(2,1)} %bitcast.8), calls=%async_computation.2 | async-start | bytes 1310720 | tf_op jit(solution)/shard_map/all_to_all | solution.py:275

commit v8 on v7

--- a/solution.py
+++ b/solution.py
@@ -76,8 +76,7 @@
     return jnp.where(k < 512, eights, fours)
 
 
-def by_core(x):
-    pick = rows_at(picked_columns(), 640)
+def by_core(x, pick):
     halves = [dot(x[:, :640], pick).astype(BF), dot(x[:, 640:], pick).astype(BF)]
     return [
         jnp.concatenate(
@@ -92,12 +91,13 @@
     copies = [pltpu.make_async_copy(a, b, sems.at[n]) for n, (a, b) in enumerate(pairs)]
     for copy in copies:
         copy.start()
+    pick = rows_at(picked_columns(), 640)
     copies[0].wait()
     dst, twins, back = placement(image_ref[...])
     info_ref[...] = jnp.concatenate([dst, twins, back], axis=0)
     move = rows_at(dst[:1, :256], 256)
     copies[1].wait()
-    grads = by_core(grad_ref[...].reshape(128, 1280))
+    grads = by_core(grad_ref[...].reshape(128, 1280), pick)
     copies[2].wait()
     qkv = qkv_ref[...].reshape(128, 1920)
     for t in range(2):
@@ -134,7 +134,7 @@
     return first[:, 128:448], first[:, 448:768], second[:, 512:], grad
 
 
-def head_probs(own_ref, info_ref, query, key, masks):
+def head_exps(own_ref, info_ref, query, key, masks):
     scores = dot(by_head(query, masks), key, 1, 1) * (HD ** -0.5)
     row = lax.broadcasted_iota(jnp.int32, (256, 256), 0)
     col = lax.broadcasted_iota(jnp.int32, (256, 256), 1)
@@ -143,27 +143,32 @@
     heads = []
     for h in range(4):
         own = jnp.where(apart, masked_score, scores[h * 256:(h + 1) * 256])
-        exp_scores = jnp.exp(own - jnp.max(own, axis=-1, keepdims=True))
-        heads.append(exp_scores * (1.0 / jnp.sum(exp_scores, axis=-1, keepdims=True)))
-    return jnp.concatenate(heads, axis=0)
+        heads.append(jnp.exp(own - jnp.max(own, axis=-1, keepdims=True)))
+    return heads
 
 
 def attend_kernel(own_ref, info_ref, got_ref, att_ref, grad_ref):
     query, key, value, grad_ref[...] = by_kind(got_ref)
     masks = head_masks(256)
-    probs = head_probs(own_ref, info_ref, query, key, masks)
-    att_ref[...] = own_head(dot(probs.astype(BF), value), masks).astype(BF)
+    heads = head_exps(own_ref, info_ref, query, key, masks)
+    summed = jnp.concatenate([value, jnp.ones((256, 64), BF)], axis=1)
+    total = jnp.zeros((256, 320), F32)
+    for exp_scores, mask in zip(heads, masks):
+        both = dot(exp_scores.astype(BF), summed)
+        total = jnp.where(mask, both[:, :320] * (1.0 / both[:, 320:321]), total)
+    att_ref[...] = total.astype(BF)
 
 
 def back_kernel(core_ref, own_ref, info_ref, got_ref, att_ref, other_ref, weight_ref, out_ref):
     query, key, value, grad = by_kind(got_ref)
     core = core_ref[0] == 0
-    weights = by_core(jnp.where(core, weight_ref[:320, :], weight_ref[320:, :]))
+    weights = by_core(jnp.where(core, weight_ref[:320, :], weight_ref[320:, :]), rows_at(picked_columns(), 640))
     delta = dot(grad, jnp.where(core, weights[0], weights[1]), 1, 1)
     delta = (delta + dot(other_ref[...], jnp.where(core, weights[1], weights[0]), 1, 1)).astype(BF)
     masks = head_masks(256)
     query_heads, delta_heads = by_head(query, masks), by_head(delta, masks)
-    probs = head_probs(own_ref, info_ref, query, key, masks)
+    heads = head_exps(own_ref, info_ref, query, key, masks)
+    probs = jnp.concatenate([x * (1.0 / jnp.sum(x, axis=-1, keepdims=True)) for x in heads], axis=0)
     prob_grad = dot(delta_heads, value, 1, 1)
     centre = jnp.sum(probs * prob_grad, axis=-1, keepdims=True)
     score_grad = (probs * (prob_grad - centre) * (HD ** -0.5)).astype(BF)

time: 131 us -> 131 us (level)
  no operation moved by 1% of the time
where the time goes in v8:
time: 131 us; the launch traced here: 130 us
  waiting for transfers between devices  44.7 us (34%)
  blocking collectives  37.9 us (29%)
  starting transfers between devices  32.7 us (25%)
  Pallas kernels  13.2 us (10%)
    all_gather x1, blocking collectives, body(): totals = lax.all_gather(share, 'dp')  37.9 us
    all_to_all x1, waiting for transfers between devices, body(): lax.all_to_all(outgoing.reshape(64, 8, 832), ('sp', 'tp'), split_axis=0,...  26.1 us
    all_to_all x1, starting transfers between devices, body(): lax.all_to_all(outgoing.reshape(64, 8, 832), ('sp', 'tp'), split_axis=0,...  17.4 us
    all_to_all x1, waiting for transfers between devices, body(): lax.all_to_all(part.reshape(32, 8, 1664), 'sp', split_axis=0, concat_axis...  16.2 us
    pallas_call x5, Pallas kernels, call(): pl.pallas_call(kernel, out_shape=outs, in_specs=specs, out_specs=jax.tree...  10.1 us
    all_to_all x1, starting transfers between devices, body(): lax.all_to_all(returning.reshape(64, 8, 640), ('sp', 'tp'), split_axis=0,...  5.98 us
    all_to_all x1, starting transfers between devices, body(): lax.all_to_all(part.reshape(32, 8, 1664), 'sp', split_axis=0, concat_axis...  5.42 us
    pallas_call x1, Pallas kernels, body(): pl.pallas_call(send_kernel, out_shape=(arr((32, 2, 8, 832), BF), arr((24,...  3.04 us
  transfers between devices with their start and end apart: 5, of which 4 were waited for; matrix products, arithmetic and copies ran while one was open for 0% of the time, Pallas kernels for 4%

profile of v8, /device:TPU:2, one launch (start us, length us, event | category | flops | bytes accessed | tf_op | source)
XLA Modules:
  0.0 130.4 jit_solution(16372183799737580878)
XLA Ops:
  0.6 3.0 %shard_map.84 = (bf16[32,2,8,832]{3,2,1,0:T(8,128)(2,1)}, s32[24,512]{1,0:T(8,128)}) custom-call(bf16[64,2,1920]{2,1,0:T(2,128)(2,1)} %bitcast.19, bf16[64,2,1280]{2,1,0:T(2,128)(2,1)} %bitcast.20, s32[1,64]{1,0:T(1,128)} %image_hbm.1), custom_call_target="tpu_custom_call" | custom-call | tf_op jit(solution)/shard_map/pallas_call | solution.py:244
  3.7 0.0 copy-start.1
  3.7 17.4 %all-to-all-start = ((bf16[64,8,832]{2,1,0:T(8,128)(2,1)}), bf16[64,8,832]{2,1,0:T(8,128)(2,1)S(1)}, u32[]{:S(2)}, u32[]{:S(2)}) async-start(bf16[64,8,832]{2,1,0:T(8,128)(2,1)} %bitcast.18), calls=%async_computation | async-start | bytes 1835008 | tf_op jit(solution)/shard_map/all_to_all | solution.py:257
  21.1 26.1 %all-to-all-done = bf16[64,8,832]{2,1,0:T(8,128)(2,1)S(1)} async-done(((bf16[64,8,832]{2,1,0:T(8,128)(2,1)}), bf16[64,8,832]{2,1,0:T(8,128)(2,1)S(1)}, u32[]{:S(2)}, u32[]{:S(2)}) %all-to-all-start) | async-done | bytes 852000 | tf_op jit(solution)/shard_map/all_to_all | solution.py:257
  47.2 0.0 copy-done.1
  47.2 1.7 %shard_map.85 = (bf16[256,320]{1,0:T(8,128)(2,1)S(1)}, bf16[256,640]{1,0:T(8,128)(2,1)S(1)}) custom-call(s32[1]{0:T(128)} %bitcast.own_ref, s32[24,512]{1,0:T(8,128)S(1)} %copy-done.1, bf16[512,832]{1,0:T(8,128)(2,1)S(1)} %bitcast.14), custom_call_target="tpu_custom_call" | custom-call | tf_op jit(solution)/shard_map/pallas_call | solution.py:27
  48.9 1.9 %collective-permute-start = (bf16[256,320]{1,0:T(8,128)(2,1)S(1)}, bf16[256,320]{1,0:T(8,128)(2,1)S(1)}, u32[]{:S(2)}, u32[]{:S(2)}) collective-permute-start(bf16[256,320]{1,0:T(8,128)(2,1)S(1)} %get-tuple-element.22.own_ref.att_ref), channel_id=1, source_target_pairs={{0,1},{1,0},{2,3},{3,2},{4,5},{5,4},{6,7},{7,6},{8,9},{9,8},{10,11... | collective-permute-start | bytes 491528 | tf_op jit(solution)/shard_map/ppermute | solution.py:266
  50.8 0.7 shard_map.86
  51.5 0.8 collective-permute-done.other_ref
  52.3 0.0 copy-start
  52.3 1.6 %shard_map.87 = bf16[256,1664]{1,0:T(8,128)(2,1)} custom-call(s32[1]{0:T(128)} %bitcast.5.core_ref, bf16[768,256]{1,0:T(8,128)(2,1)S(1)} %get-tuple-element.21.turned_ref, bf16[256,320]{1,0:T(8,128)(2,1)S(1)} %get-tuple-element.22.own_ref.att_ref, f32[256,64]{1,0:T(8,128)S(1)} %get-tuple-element.23.bias_ref, bf16[256,320]{1,0:T(8,128)(2,1)S(1)} %collective-permute-done.other_ref), custom_call_target="tpu_custom_call" | custom-call | tf_op jit(solution)/shard_map/pallas_call | solution.py:27
  53.8 5.4 %all-to-all-start.1 = ((bf16[32,8,1664]{2,1,0:T(8,128)(2,1)}), bf16[32,8,1664]{2,1,0:T(8,128)(2,1)}, u32[]{:S(2)}, u32[]{:S(2)}) async-start(bf16[32,8,1664]{2,1,0:T(8,128)(2,1)} %bitcast.6), calls=%async_computation.1 | async-start | bytes 1703936 | tf_op jit(solution)/shard_map/all_to_all | solution.py:276
  59.2 1.9 %collective-permute-start.1 = (bf16[256,640]{1,0:T(8,128)(2,1)S(1)}, bf16[256,640]{1,0:T(8,128)(2,1)S(1)}, u32[]{:S(2)}, u32[]{:S(2)}) collective-permute-start(bf16[256,640]{1,0:T(8,128)(2,1)S(1)} %get-tuple-element.25.grad_ref), channel_id=1, source_target_pairs={{0,1},{1,0},{2,3},{3,2},{4,5},{5,4},{6,7},{7,6},{8,9},{9,8},{10,11... | collective-permute-start | bytes 983048 | tf_op jit(solution)/shard_map/ppermute | solution.py:271
  61.2 1.6 %collective-permute-done.1.other_ref = bf16[256,640]{1,0:T(8,128)(2,1)S(1)} collective-permute-done((bf16[256,640]{1,0:T(8,128)(2,1)S(1)}, bf16[256,640]{1,0:T(8,128)(2,1)S(1)}, u32[]{:S(2)}, u32[]{:S(2)}) %collective-permute-start.1) | collective-permute-done | bytes 327712 | tf_op jit(solution)/shard_map/ppermute | solution.py:271
  62.8 0.0 copy-done
  62.8 4.4 %shard_map.88 = bf16[512,640]{1,0:T(8,128)(2,1)} custom-call(s32[1]{0:T(128)} %bitcast.5.core_ref, s32[1]{0:T(128)} %bitcast.own_ref, s32[24,512]{1,0:T(8,128)S(1)} %copy-done.1, bf16[512,832]{1,0:T(8,128)(2,1)S(1)} %bitcast.15, bf16[256,320]{1,0:T(8,128)(2,1)S(1)} %get-tuple-element.22.own_ref.att_ref, ...), custom_call_target="tpu_custom_call" | custom-call | tf_op jit(solution)/shard_map/pallas_call | solution.py:27
  67.2 0.0 copy-start.2
  67.2 16.2 %all-to-all-done.1 = bf16[32,8,1664]{2,1,0:T(8,128)(2,1)} async-done(((bf16[32,8,1664]{2,1,0:T(8,128)(2,1)}), bf16[32,8,1664]{2,1,0:T(8,128)(2,1)}, u32[]{:S(2)}, u32[]{:S(2)}) %all-to-all-start.1) | async-done | bytes 852000 | tf_op jit(solution)/shard_map/all_to_all | solution.py:276
  83.5 1.3 reduce_sum.12
  84.8 6.0 %all-to-all-start.2 = ((bf16[64,8,640]{2,1,0:T(8,128)(2,1)}), bf16[64,8,640]{2,1,0:T(8,128)(2,1)S(1)}, u32[]{:S(2)}, u32[]{:S(2)}) async-start(bf16[64,8,640]{2,1,0:T(8,128)(2,1)} %bitcast.8), calls=%async_computation.2 | async-start | bytes 1310720 | tf_op jit(solution)/shard_map/all_to_all | solution.py:280
  90.7 0.0 copy-done.2
  90.8 37.9 %all-gather = bf16[128,1664]{1,0:T(8,128)(2,1)S(1)} all-gather(bf16[8,1664]{1,0:T(8,128)(2,1)S(1)} %reduce_sum.12), channel_id=2, replica_groups=mesh['dp'=16,'sp'=32,'tp'=2] {'dp'}, dimensions={0}, use_global_device_ids=true | all-gather | bytes 452608 | tf_op jit(solution)/shard_map/all_gather | solution.py:279
  128.6 0.0 all-to-all-done.2
  128.6 1.8 %shard_map.89 = (bf16[64,2,1280]{2,1,0:T(2,128)(2,1)}, bf16[64,2,1920]{2,1,0:T(2,128)(2,1)}, f32[20,640]{1,0:T(8,128)}, f32[1,20]{1,0:T(1,128)}) custom-call(bf16[16,8,1664]{2,1,0:T(8,128)(2,1)S(1)} %bitcast.17, bf16[512,640]{1,0:T(8,128)(2,1)S(1)} %bitcast.16, s32[24,512]{1,0:T(8,128)S(1)} %copy-done.1, bf16[640,1280]{1,0:T(8,128)(2,1)S(1)} %copy-done, ...), custom_call_target="tpu_custom_call" | custom-call | tf_op jit(solution)/shard_map/pallas_call | solution.py:27
  (1 shorter events, 0.0 us)
Async XLA Ops:
  3.7 43.5 %copy-start.1 = (s32[24,512]{1,0:T(8,128)S(1)}, s32[24,512]{1,0:T(8,128)}, u32[]{:S(2)}) copy-start(s32[24,512]{1,0:T(8,128)} %get-tuple-element.18.info_ref) | copy-start | bytes 147460
  3.7 43.5 %all-to-all-start = ((bf16[64,8,832]{2,1,0:T(8,128)(2,1)}), bf16[64,8,832]{2,1,0:T(8,128)(2,1)S(1)}, u32[]{:S(2)}, u32[]{:S(2)}) async-start(bf16[64,8,832]{2,1,0:T(8,128)(2,1)} %bitcast.18), calls=%async_computation | async-start | bytes 1835008 | tf_op jit(solution)/shard_map/all_to_all | solution.py:257
  48.9 3.3 %collective-permute-start = (bf16[256,320]{1,0:T(8,128)(2,1)S(1)}, bf16[256,320]{1,0:T(8,128)(2,1)S(1)}, u32[]{:S(2)}, u32[]{:S(2)}) collective-permute-start(bf16[256,320]{1,0:T(8,128)(2,1)S(1)} %get-tuple-element.22.own_ref.att_ref), channel_id=1, source_target_pairs={{0,1},{1,0},{2,3},{3,2},{4,5},{5,4},{6,7},{7,6},{8,9},{9,8},{10,11... | collective-permute-start | bytes 491528 | tf_op jit(solution)/shard_map/ppermute | solution.py:266
  52.3 10.5 %copy-start = (bf16[640,1280]{1,0:T(8,128)(2,1)S(1)}, bf16[640,1280]{1,0:T(8,128)(2,1)}, u32[]{:S(2)}) copy-start(bf16[640,1280]{1,0:T(8,128)(2,1)} %weight_ref.3) | copy-start | bytes 4915204
  53.8 29.6 %all-to-all-start.1 = ((bf16[32,8,1664]{2,1,0:T(8,128)(2,1)}), bf16[32,8,1664]{2,1,0:T(8,128)(2,1)}, u32[]{:S(2)}, u32[]{:S(2)}) async-start(bf16[32,8,1664]{2,1,0:T(8,128)(2,1)} %bitcast.6), calls=%async_computation.1 | async-start | bytes 1703936 | tf_op jit(solution)/shard_map/all_to_all | solution.py:276
  59.2 3.5 %collective-permute-start.1 = (bf16[256,640]{1,0:T(8,128)(2,1)S(1)}, bf16[256,640]{1,0:T(8,128)(2,1)S(1)}, u32[]{:S(2)}, u32[]{:S(2)}) collective-permute-start(bf16[256,640]{1,0:T(8,128)(2,1)S(1)} %get-tuple-element.25.grad_ref), channel_id=1, source_target_pairs={{0,1},{1,0},{2,3},{3,2},{4,5},{5,4},{6,7},{7,6},{8,9},{9,8},{10,11... | collective-permute-start | bytes 983048 | tf_op jit(solution)/shard_map/ppermute | solution.py:271
  67.2 23.5 %copy-start.2 = (bf16[1280]{0:T(1024)(128)(2,1)S(1)}, bf16[1280]{0:T(1024)(128)(2,1)}, u32[]{:S(2)}) copy-start(bf16[1280]{0:T(1024)(128)(2,1)} %param.9) | copy-start | bytes 7684
  84.8 43.9 %all-to-all-start.2 = ((bf16[64,8,640]{2,1,0:T(8,128)(2,1)}), bf16[64,8,640]{2,1,0:T(8,128)(2,1)S(1)}, u32[]{:S(2)}, u32[]{:S(2)}) async-start(bf16[64,8,640]{2,1,0:T(8,128)(2,1)} %bitcast.8), calls=%async_computation.2 | async-start | bytes 1310720 | tf_op jit(solution)/shard_map/all_to_all | solution.py:280
